TPU v7x, 256 devices: a whole 4x4x8 slice. The times are simulated.
256 devices in a mesh: db: 32 (over y, z), tp: 8 (over x, core).
Axes of the slice: x: 4, y: 4, z: 8, core: 2. Of those that a mesh axis runs over, the one named last changes fastest.
Arguments:
- queries: bfloat16 [16384, 2048], P('db', 'tp'), may hold values from -400 to 400
- nbr_shard: int32 [256, 2], P('db'), may hold values from 0 to 31, all different within a row; in each aligned block of 8 rows (0 to 7, 8 to 15, ...) at most 2 rows name the same one
- nbr_row: int32 [256, 2], P('db'), may hold values from 0 to 3
- database: bfloat16 [128, 128, 4096], P('db', None, 'tp'), may hold values from -6 to 6
- key_weight: bfloat16 [4096, 2048], P(None, 'tp'), may hold values from -0.09375 to 0.09375
- value_weight: bfloat16 [4096, 2048], P(None, 'tp'), may hold values from -0.09375 to 0.09375
- lambda_head: float32 [8], P('tp'), may hold values from 0.1 to 0.9
- out_weight: bfloat16 [2048, 4096], P('tp'), may hold values from -0.125 to 0.125
Outputs:
- mixed_rows: bfloat16 [16384, 4096], P(('db', 'tp'))
Inputs may be any that keep to these rules, and one draw needn't show every extreme that they name: `nbr_shard`: within the 8 rows of one device no shard is named more than 2 times, and in some device's rows one shard is named exactly 2 times; the 2 shards of a row differ.
All inputs are finite; a program needn't handle non-finite values.
Results may differ from a plain program's by a relative error of at most 0.019.
Values may be sent and summed in bfloat16 or wider, within the bound.
No kernel may reach another device: no remote copies, remote signals or barrier semaphores. Data moves between devices by JAX's collectives and lax.ppermute only.
A program may use at most 128 MiB of HBM per device.

v0:
```python
import functools
import jax
import jax.numpy as jnp
from jax import lax
from jax.experimental import pallas as pl
from jax.experimental.pallas import tpu as pltpu
from jax.sharding import Mesh, PartitionSpec as P

HD = 128
SPAN = 64
NLEN = 128
EPSILON = 1e-05
FAR = -1e30
NY, NZ, NX, NC = 4, 8, 4, 2
SPANS_DEV = 8
ENTRIES = 4
PAIRS = ENTRIES // 2
BLOCK = 4 * NLEN
QROWS = SPANS_DEV * SPAN
WIDE = 2 * HD
OROWS = SPANS_DEV * WIDE
VMEM_LIMIT = 48 * 1024 * 1024


def shift(a, axis, k):
    n = lax.axis_size(axis)
    return lax.ppermute(a, axis, [(i, (i + k) % n) for i in range(n)])


def ring_pieces(a, axis):
    n = lax.axis_size(axis)
    half = a.shape[0] // 2
    out = [(0, 0, a)]
    up = down = a
    for k in range(1, (n - 1) // 2 + 1):
        up, down = shift(up, axis, 1), shift(down, axis, -1)
        out += [(k, 0, up), (n - k, 0, down)]
    out += [(n // 2, 0, shift(up[:half], axis, 1)), (n // 2, half, shift(down[half:], axis, -1))]
    return out


def project_kernel(layout, feature_ref, *refs):
    pieces, (key_ref, value_ref) = refs[: -2 - PAIRS], refs[-2 - PAIRS : -PAIRS]
    out_refs = refs[-PAIRS:]
    key_sum = value_sum = squares = None
    for block, members in enumerate(layout):
        rows = [pieces[i][...] for i in members]
        tokens = rows[0] if len(rows) == 1 else jnp.concatenate(rows, axis=0)
        width = tokens.shape[1]
        at = pl.ds(pl.multiple_of(feature_ref[block] * width, width), width)
        k = jnp.dot(tokens, key_ref[at, :], preferred_element_type=jnp.float32)
        v = jnp.dot(tokens, value_ref[at, :], preferred_element_type=jnp.float32)
        f = tokens.astype(jnp.float32)
        s = jnp.sum(f * f, axis=1, keepdims=True)
        if key_sum is None:
            key_sum, value_sum, squares = k, v, s
        else:
            key_sum, value_sum, squares = key_sum + k, value_sum + v, squares + s
    inverse = lax.rsqrt(squares / key_ref.shape[0] + EPSILON)
    keys = (key_sum * inverse).astype(jnp.bfloat16)
    values = value_sum * inverse
    for pair, out_ref in enumerate(out_refs):
        rows = slice(pair * 2 * NLEN, (pair + 1) * 2 * NLEN)
        out_ref[: 2 * NLEN, :] = keys[rows]
        out_ref[2 * NLEN :, :] = values[rows].T.astype(jnp.bfloat16)


def project(feature, blocks, key_weight, value_weight):
    pieces, layout = [], []
    for members in blocks:
        layout.append(tuple(range(len(pieces), len(pieces) + len(members))))
        pieces += members
    vmem = pl.BlockSpec(memory_space=pltpu.VMEM)
    return pl.pallas_call(
        functools.partial(project_kernel, tuple(layout)),
        out_shape=[jax.ShapeDtypeStruct((BLOCK, WIDE), jnp.bfloat16)] * PAIRS,
        in_specs=[pl.BlockSpec(memory_space=pltpu.SMEM)] + [vmem] * (len(pieces) + 2),
        out_specs=[vmem] * PAIRS,
        compiler_params=pltpu.CompilerParams(vmem_limit_bytes=VMEM_LIMIT),
        cost_estimate=pl.CostEstimate(
            flops=2 * 512 * 4096 * 512, bytes_accessed=8 << 20, transcendentals=0
        ),
        name="project",
    )(feature, *pieces, key_weight, value_weight)


def attend_kernel(places, place_ref, lane_ref, bias_ref, query_ref, *refs):
    pieces = refs[: len(places)]
    out_ref, table, stats, sems = refs[len(places) :]
    copies = [
        pltpu.make_async_copy(piece, table.at[pl.ds(row, piece.shape[0])], sems.at[i])
        for i, (row, piece) in enumerate(zip(places, pieces))
    ]
    for copy in copies:
        copy.start()
    lane = lax.broadcasted_iota(jnp.int32, (SPAN, WIDE), 1)
    for copy in copies:
        copy.wait()
    group = 4
    for first in range(0, SPANS_DEV, group):
        scores, values = [], []
        for s in range(first, first + group):
            block = [pl.multiple_of(place_ref[2 * s + j], BLOCK) for j in range(2)]
            side = [pl.multiple_of(lane_ref[2 * s + j], NLEN) for j in range(2)]
            keys = [table[pl.ds(block[j] + side[j], NLEN), :] for j in range(2)]
            values.append(
                jnp.concatenate(
                    [
                        table[pl.ds(block[j] + 2 * NLEN, WIDE), pl.ds(side[j], NLEN)]
                        for j in range(2)
                    ],
                    axis=1,
                )
            )
            q = query_ref[s * SPAN : (s + 1) * SPAN, :]
            zero = jnp.zeros_like(q)
            both = jnp.concatenate(
                [jnp.where(lane < HD, q, zero), jnp.where(lane >= HD, q, zero)], axis=0
            )
            products = lax.dot_general(
                jnp.concatenate(keys, axis=0),
                both,
                (((1,), (1,)), ((), ())),
                preferred_element_type=jnp.float32,
            ) * (1.0 / HD**0.5)
            scores.append([products[j * NLEN : (j + 1) * NLEN] + bias_ref[2 * s + j] for j in range(2)])
        shares, levels = [], []
        for one, two in scores:
            top = jnp.max(jnp.maximum(one, two), axis=0, keepdims=True)
            one, two = jnp.exp(one - top), jnp.exp(two - top)
            total = jnp.sum(one + two, axis=0, keepdims=True)
            levels.append(top + jnp.log(total))
            inverse = 1.0 / total
            shares.append(
                jnp.concatenate([one * inverse, two * inverse], axis=0).astype(jnp.bfloat16)
            )
        attended = [
            jnp.dot(v, p, preferred_element_type=jnp.float32).astype(jnp.bfloat16)
            for v, p in zip(values, shares)
        ]
        for i, s in enumerate(range(first, first + group)):
            out_ref[s * WIDE : (s + 1) * WIDE, :] = attended[i]
            stats[s : s + 1, :] = levels[i]
    level = stats[...]
    high = level.astype(jnp.bfloat16).astype(jnp.float32)
    rest = level - high
    mid = rest.astype(jnp.bfloat16).astype(jnp.float32)
    low = rest - mid
    coded = jnp.concatenate([high, mid, low, jnp.zeros_like(low)], axis=0)
    out_ref[OROWS:, :] = coded.astype(jnp.bfloat16)


def attend(place, lane, bias, queries, pieces):
    places = tuple(row for row, _ in pieces)
    smem = pl.BlockSpec(memory_space=pltpu.SMEM)
    vmem = pl.BlockSpec(memory_space=pltpu.VMEM)
    return pl.pallas_call(
        functools.partial(attend_kernel, places),
        out_shape=jax.ShapeDtypeStruct((OROWS + 4 * SPANS_DEV, 2 * SPAN), jnp.bfloat16),
        in_specs=[smem] * 3 + [vmem] + [pl.BlockSpec(memory_space=pltpu.HBM)] * len(pieces),
        out_specs=vmem,
        scratch_shapes=[
            pltpu.VMEM((PAIRS * NZ * BLOCK, WIDE), jnp.bfloat16),
            pltpu.VMEM((SPANS_DEV, 2 * SPAN), jnp.float32),
            pltpu.SemaphoreType.DMA((len(pieces),)),
        ],
        compiler_params=pltpu.CompilerParams(vmem_limit_bytes=VMEM_LIMIT),
        cost_estimate=pl.CostEstimate(
            flops=1 << 29, bytes_accessed=6 << 20, transcendentals=1 << 18
        ),
        name="attend",
    )(place, lane, bias, queries, *[a for _, a in pieces])


def combine_kernel(lambda_ref, *refs):
    *messages, out_ref = refs
    levels = []
    for message in messages:
        coded = message[OROWS:, :].astype(jnp.float32)
        n = SPANS_DEV
        levels.append((coded[:n] + coded[n : 2 * n]) + coded[2 * n : 3 * n])
    top = functools.reduce(jnp.maximum, levels)
    parts = [jnp.exp(level - top) for level in levels]
    total = functools.reduce(jnp.add, parts)
    lane = lax.broadcasted_iota(jnp.int32, (SPANS_DEV, 2 * SPAN), 1)
    sign = jnp.where(lane < SPAN, 1.0, -lambda_ref[0])
    factors = [part * (sign / total) for part in parts]
    first = lax.broadcasted_iota(jnp.int32, (WIDE, 2 * SPAN), 1) < SPAN
    for pair in range(SPANS_DEV // 2):
        both = []
        for s in (2 * pair, 2 * pair + 1):
            maps = functools.reduce(
                jnp.add,
                [
                    message[s * WIDE : (s + 1) * WIDE, :].astype(jnp.float32) * factor[s : s + 1, :]
                    for factor, message in zip(factors, messages)
                ],
            )
            both.append(maps + pltpu.roll(maps, SPAN, 1))
        attended = jnp.where(first, both[0], both[1])
        inverse = lax.rsqrt(jnp.mean(attended * attended, axis=0, keepdims=True) + EPSILON)
        out_ref[2 * pair * SPAN : 2 * (pair + 1) * SPAN, :] = (attended * inverse).T.astype(
            jnp.bfloat16
        )


def combine(lambda_head, messages):
    vmem = pl.BlockSpec(memory_space=pltpu.VMEM)
    return pl.pallas_call(
        combine_kernel,
        out_shape=jax.ShapeDtypeStruct((QROWS, WIDE), jnp.bfloat16),
        in_specs=[pl.BlockSpec(memory_space=pltpu.SMEM)] + [vmem] * NY,
        out_specs=vmem,
        compiler_params=pltpu.CompilerParams(vmem_limit_bytes=VMEM_LIMIT),
        cost_estimate=pl.CostEstimate(
            flops=1 << 23, bytes_accessed=3 << 20, transcendentals=1 << 13
        ),
        name="combine",
    )(lambda_head, *messages)


def on_device(
    queries, nbr_shard, nbr_row, database, key_weight, value_weight, lambda_head, out_weight
):
    y, z = lax.axis_index("y"), lax.axis_index("z")
    x, c = lax.axis_index("x"), lax.axis_index("c")

    entry = (nbr_shard * ENTRIES + nbr_row).astype(jnp.bfloat16).reshape(1, -1)
    entry = jnp.pad(entry, ((0, 15), (0, 2 * HD - entry.shape[1])))
    packed = jnp.concatenate([queries, entry], axis=0)
    asked = [packed] + [shift(packed, "y", k) for k in (1, 2, -1)]

    feature = jnp.concatenate(
        [
            (((x + NX - jnp.arange(NX)) % NX) * NC + side).astype(jnp.int32)
            for side in (c, 1 - c)
        ]
    )
    own = ring_pieces(database.reshape(ENTRIES * NLEN, -1), "x")
    other = [(k, r, shift(a, "c", 1)) for k, r, a in own]
    blocks = [[a for k, _, a in side if k == d] for side in (own, other) for d in range(NX)]
    rows = project(feature, blocks, key_weight, value_weight)
    table = [
        ((pair * NZ + k) * BLOCK + r, a)
        for pair in range(PAIRS)
        for k, r, a in ring_pieces(rows[pair], "z")
    ]

    held_back, _ = lax.optimization_barrier((out_weight, rows[0]))
    weight = lax.all_gather(held_back, ("x", "c"), axis=0, tiled=True)

    wanted = jnp.stack([a[QROWS, : 2 * SPANS_DEV] for a in asked]).astype(jnp.int32)
    shard, row = wanted // ENTRIES, wanted % ENTRIES
    bias = jnp.where(shard // NZ == y, 0.0, FAR).astype(jnp.float32)
    place = (((row // 2) * NZ + (z + NZ - shard % NZ) % NZ) * BLOCK).astype(jnp.int32)
    lane = ((row % 2) * NLEN).astype(jnp.int32)
    messages = [None] * NY
    for k in (2, 1, 3, 0):
        out = attend(place[k], lane[k], bias[k], asked[k], table)
        messages[k] = shift(out, "y", -k) if k else out
    heads_out = combine(lambda_head, messages)

    heads = lax.all_to_all(
        heads_out.reshape(NX * NC, SPAN, WIDE), ("x", "c"), split_axis=0, concat_axis=0, tiled=True
    )
    rows = jnp.swapaxes(heads, 0, 1).reshape(SPAN, NX * NC * WIDE)
    return jnp.dot(rows, weight, preferred_element_type=jnp.float32).astype(jnp.bfloat16)


def solution(mesh):
    fine = Mesh(mesh.devices.reshape(NY, NZ, NX, NC), ("y", "z", "x", "c"))
    db, tp = ("y", "z"), ("x", "c")
    return jax.shard_map(
        on_device,
        mesh=fine,
        in_specs=(
            P(db, tp),
            P(db, None),
            P(db, None),
            P(db, None, tp),
            P(None, tp),
            P(None, tp),
            P(tp),
            P(tp, None),
        ),
        out_specs=P(db + tp, None),
        check_vma=False,
    )
```

profile of v0, /device:TPU:8, one launch (start us, length us, event | category | flops | bytes accessed | tf_op | source)
XLA Modules:
  0.0 154.8 jit_solution(12940437780007190722)
XLA Ops:
  6.5 2.8 %collective-permute-start.5 = (bf16[512,512]{1,0:T(8,128)(2,1)}, bf16[512,512]{1,0:T(8,128)(2,1)S(1)}, u32[]{:S(2)}, u32[]{:S(2)}) collective-permute-start(bf16[512,512]{1,0:T(8,128)(2,1)} %bitcast.32), channel_id=1, source_target_pairs={{0,6},{2,0},{4,2},{6,4},{1,7},{3,1},{5,3},{7,5},{8,14},{10,8},{12,... | collective-permute-start | bytes 1572872 | tf_op jit(solution)/shard_map/ppermute | solution.py:27
  9.3 11.5 %collective-permute-done.5.refs_4_ = bf16[512,512]{1,0:T(8,128)(2,1)S(1)} collective-permute-done((bf16[512,512]{1,0:T(8,128)(2,1)}, bf16[512,512]{1,0:T(8,128)(2,1)S(1)}, u32[]{:S(2)}, u32[]{:S(2)}) %collective-permute-start.5) | collective-permute-done | bytes 524320 | tf_op jit(solution)/shard_map/ppermute | solution.py:27
  20.8 3.7 %collective-permute-start.6 = (bf16[256,512]{1,0:T(8,128)(2,1)S(1)}, bf16[256,512]{1,0:T(8,128)(2,1)S(1)}, u32[]{:S(2)}, u32[]{:S(2)}) collective-permute-start(bf16[256,512]{1,0:T(8,128)(2,1)S(1)} %slice.89), channel_id=1, source_target_pairs={{0,6},{2,0},{4,2},{6,4},{1,7},{3,1},{5,3},{7,5},{8,14},{10,8},{12,... | collective-permute-start | bytes 786440 | tf_op jit(solution)/shard_map/ppermute | solution.py:27
  25.2 4.0 %collective-permute-done.6.refs_3_ = bf16[256,512]{1,0:T(8,128)(2,1)S(1)} collective-permute-done((bf16[256,512]{1,0:T(8,128)(2,1)S(1)}, bf16[256,512]{1,0:T(8,128)(2,1)S(1)}, u32[]{:S(2)}, u32[]{:S(2)}) %collective-permute-start.6) | collective-permute-done | bytes 262176 | tf_op jit(solution)/shard_map/ppermute | solution.py:27
  29.2 3.5 %collective-permute-done.4.refs_2_ = bf16[256,512]{1,0:T(8,128)(2,1)S(1)} collective-permute-done((bf16[256,512]{1,0:T(8,128)(2,1)S(1)}, bf16[256,512]{1,0:T(8,128)(2,1)S(1)}, u32[]{:S(2)}, u32[]{:S(2)}) %collective-permute-start.4) | collective-permute-done | bytes 262176 | tf_op jit(solution)/shard_map/ppermute | solution.py:27
  37.3 4.9 %project.1 = (bf16[512,256]{1,0:T(8,128)(2,1)S(1)}, bf16[512,256]{1,0:T(8,128)(2,1)S(1)}) custom-call(s32[8]{0:T(128)S(1)} %pad_add_fusion.feature_ref, bf16[512,512]{1,0:T(8,128)(2,1)S(1)} %bitcast.35, bf16[512,512]{1,0:T(8,128)(2,1)S(1)} %collective-permute-done.3.refs_1_, bf16[256,512]{1,0:T(8,128)(2,1)S(1)} %copy-done.2, ...), custom_call_target="tpu_custom_call" | custom-call | flops 2147483648 | bytes 8388608 | tf_op jit(solution)/shard_map/project/pallas_call | solution.py:74
  48.6 3.9 %collective-permute-start.13 = (bf16[512,256]{1,0:T(8,128)(2,1)S(1)}, bf16[512,256]{1,0:T(8,128)(2,1)S(1)}, u32[]{:S(2)}, u32[]{:S(2)}) collective-permute-start(bf16[512,256]{1,0:T(8,128)(2,1)S(1)} %get-tuple-element.8.refs_0_), channel_id=1, source_target_pairs={{0,56},{8,0},{16,8},{24,16},{32,24},{40,32},{48,40},{56,48},{1,57}... | collective-permute-start | bytes 786440 | tf_op jit(solution)/shard_map/ppermute | solution.py:27
  53.5 5.9 %collective-permute-start.21 = (bf16[512,256]{1,0:T(8,128)(2,1)S(1)}, bf16[512,256]{1,0:T(8,128)(2,1)S(1)}, u32[]{:S(2)}, u32[]{:S(2)}) collective-permute-start(bf16[512,256]{1,0:T(8,128)(2,1)S(1)} %get-tuple-element.9.refs_9_), channel_id=1, source_target_pairs={{0,56},{8,0},{16,8},{24,16},{32,24},{40,32},{48,40},{56,48},{1,57}... | collective-permute-start | bytes 786440 | tf_op jit(solution)/shard_map/ppermute | solution.py:27
  63.5 4.0 %collective-permute-start.15 = (bf16[512,256]{1,0:T(8,128)(2,1)S(1)}, bf16[512,256]{1,0:T(8,128)(2,1)S(1)}, u32[]{:S(2)}, u32[]{:S(2)}) collective-permute-start(bf16[512,256]{1,0:T(8,128)(2,1)S(1)} %collective-permute-done.13.refs_2_), channel_id=1, source_target_pairs={{0,56},{8,0},{16,8},{24,16},{32,24},{40,32},{48,40},{56,48},{1,57}... | collective-permute-start | bytes 786440 | tf_op jit(solution)/shard_map/ppermute | solution.py:27
  67.5 3.2 %collective-permute-start.23 = (bf16[512,256]{1,0:T(8,128)(2,1)S(1)}, bf16[512,256]{1,0:T(8,128)(2,1)S(1)}, u32[]{:S(2)}, u32[]{:S(2)}) collective-permute-start(bf16[512,256]{1,0:T(8,128)(2,1)S(1)} %collective-permute-done.21.refs_11_), channel_id=1, source_target_pairs={{0,56},{8,0},{16,8},{24,16},{32,24},{40,32},{48,40},{56,48},{1,57}... | collective-permute-start | bytes 786440 | tf_op jit(solution)/shard_map/ppermute | solution.py:27
  71.5 3.1 %collective-permute-done.14.refs_3_ = bf16[512,256]{1,0:T(8,128)(2,1)S(1)} collective-permute-done((bf16[512,256]{1,0:T(8,128)(2,1)S(1)}, bf16[512,256]{1,0:T(8,128)(2,1)S(1)}, u32[]{:S(2)}, u32[]{:S(2)}) %collective-permute-start.14) | collective-permute-done | bytes 262176 | tf_op jit(solution)/shard_map/ppermute | solution.py:27
  74.7 3.3 %collective-permute-start.17 = (bf16[512,256]{1,0:T(8,128)(2,1)S(1)}, bf16[512,256]{1,0:T(8,128)(2,1)S(1)}, u32[]{:S(2)}, u32[]{:S(2)}) collective-permute-start(bf16[512,256]{1,0:T(8,128)(2,1)S(1)} %collective-permute-done.15.refs_4_), channel_id=1, source_target_pairs={{0,56},{8,0},{16,8},{24,16},{32,24},{40,32},{48,40},{56,48},{1,57}... | collective-permute-start | bytes 786440 | tf_op jit(solution)/shard_map/ppermute | solution.py:27
  80.3 3.3 %collective-permute-start.25 = (bf16[512,256]{1,0:T(8,128)(2,1)S(1)}, bf16[512,256]{1,0:T(8,128)(2,1)S(1)}, u32[]{:S(2)}, u32[]{:S(2)}) collective-permute-start(bf16[512,256]{1,0:T(8,128)(2,1)S(1)} %collective-permute-done.23.refs_13_), channel_id=1, source_target_pairs={{0,56},{8,0},{16,8},{24,16},{32,24},{40,32},{48,40},{56,48},{1,57}... | collective-permute-start | bytes 786440 | tf_op jit(solution)/shard_map/ppermute | solution.py:27
  86.0 3.3 %collective-permute-start.19 = (bf16[256,256]{1,0:T(8,128)(2,1)S(1)}, bf16[256,256]{1,0:T(8,128)(2,1)S(1)}, u32[]{:S(2)}, u32[]{:S(2)}) collective-permute-start(bf16[256,256]{1,0:T(8,128)(2,1)S(1)} %slice.91), channel_id=1, source_target_pairs={{0,56},{8,0},{16,8},{24,16},{32,24},{40,32},{48,40},{56,48},{1,57}... | collective-permute-start | bytes 393224 | tf_op jit(solution)/shard_map/ppermute | solution.py:27
  91.6 3.3 %collective-permute-start.27 = (bf16[256,256]{1,0:T(8,128)(2,1)S(1)}, bf16[256,256]{1,0:T(8,128)(2,1)S(1)}, u32[]{:S(2)}, u32[]{:S(2)}) collective-permute-start(bf16[256,256]{1,0:T(8,128)(2,1)S(1)} %slice.93), channel_id=1, source_target_pairs={{0,56},{8,0},{16,8},{24,16},{32,24},{40,32},{48,40},{56,48},{1,57}... | collective-permute-start | bytes 393224 | tf_op jit(solution)/shard_map/ppermute | solution.py:27
  94.9 2.8 %collective-permute-done.26.refs_16_ = bf16[256,256]{1,0:T(8,128)(2,1)S(1)} collective-permute-done((bf16[256,256]{1,0:T(8,128)(2,1)S(1)}, bf16[256,256]{1,0:T(8,128)(2,1)S(1)}, u32[]{:S(2)}, u32[]{:S(2)}) %collective-permute-start.26) | collective-permute-done | bytes 131104 | tf_op jit(solution)/shard_map/ppermute | solution.py:27
  97.7 3.2 %attend.7 = bf16[2080,128]{1,0:T(8,128)(2,1)S(1)} custom-call(s32[16]{0:T(128)S(1)} %get-tuple-element.28.place_ref, s32[16]{0:T(128)S(1)} %get-tuple-element.15.lane_ref, f32[16]{0:T(128)S(1)} %get-tuple-element.11.bias_ref, bf16[528,256]{1,0:T(8,128)(2,1)} %collective-permute-done.2.query_ref, bf16[512,256]{1,0:T(8,128)(2,1)S(1)} %get-tuple-element.8.refs_0_, ...), custom_call_target="tpu_custom_call" | custom-call | flops 536870912 | bytes 6291456 | tf_op jit(solution)/shard_map/attend/pallas_call | solution.py:157
  100.9 2.8 %collective-permute-start.30 = (bf16[2080,128]{1,0:T(8,128)(2,1)S(1)}, bf16[2080,128]{1,0:T(8,128)(2,1)S(1)}, u32[]{:S(2)}, u32[]{:S(2)}) collective-permute-start(bf16[2080,128]{1,0:T(8,128)(2,1)S(1)} %attend.7), channel_id=1, source_target_pairs={{0,64},{64,128},{128,192},{192,0},{1,65},{65,129},{129,193},{193,1... | collective-permute-start | bytes 1597448 | tf_op jit(solution)/shard_map/ppermute | solution.py:27
  106.5 2.7 %attend.5 = bf16[2080,128]{1,0:T(8,128)(2,1)S(1)} custom-call(s32[16]{0:T(128)S(1)} %get-tuple-element.26.place_ref, s32[16]{0:T(128)S(1)} %get-tuple-element.17.lane_ref, f32[16]{0:T(128)S(1)} %get-tuple-element.13.bias_ref, bf16[528,256]{1,0:T(8,128)(2,1)S(1)} %collective-permute-done.query_ref, bf16[512,256]{1,0:T(8,128)(2,1)S(1)} %get-tuple-element.8.refs_0_, ...), custom_call_target="tpu_custom_call" | custom-call | flops 536870912 | bytes 6291456 | tf_op jit(solution)/shard_map/attend/pallas_call | solution.py:157
  112.0 2.7 %attend.4.refs_0_ = bf16[2080,128]{1,0:T(8,128)(2,1)S(1)} custom-call(s32[16]{0:T(128)S(1)} %get-tuple-element.25.place_ref, s32[16]{0:T(128)S(1)} %get-tuple-element.18.lane_ref, f32[16]{0:T(128)S(1)} %get-tuple-element.14.bias_ref, bf16[528,256]{1,0:T(8,128)(2,1)S(1)} %fusion.1.query_ref, bf16[512,256]{1,0:T(8,128)(2,1)S(1)} %get-tuple-element.8.refs_0_, ...), custom_call_target="tpu_custom_call" | custom-call | flops 536870912 | bytes 6291456 | tf_op jit(solution)/shard_map/attend/pallas_call | solution.py:157
  116.2 5.9 %collective-permute-done.29.refs_2_ = bf16[2080,128]{1,0:T(8,128)(2,1)S(1)} collective-permute-done((bf16[2080,128]{1,0:T(8,128)(2,1)S(1)}, bf16[2080,128]{1,0:T(8,128)(2,1)S(1)}, u32[]{:S(2)}, u32[]{:S(2)}) %collective-permute-start.29) | collective-permute-done | bytes 532512 | tf_op jit(solution)/shard_map/ppermute | solution.py:27
  122.1 5.6 %collective-permute-done.28.refs_1_ = bf16[2080,128]{1,0:T(8,128)(2,1)S(1)} collective-permute-done((bf16[2080,128]{1,0:T(8,128)(2,1)S(1)}, bf16[2080,128]{1,0:T(8,128)(2,1)S(1)}, u32[]{:S(2)}, u32[]{:S(2)}) %collective-permute-start.28) | collective-permute-done | bytes 532512 | tf_op jit(solution)/shard_map/ppermute | solution.py:27
  128.4 9.9 %all_to_all.5 = bf16[8,64,256]{2,1,0:T(8,128)(2,1)S(1)} all-to-all(bf16[8,64,256]{2,1,0:T(8,128)(2,1)S(1)} %bitcast.31), channel_id=1, replica_groups=mesh['y'=4,'z'=8,'x'=4,'c'=2] {'x','c'}, dimensions={0} | all-to-all | bytes 524288 | tf_op jit(solution)/shard_map/all_to_all | solution.py:263
  138.4 9.6 %convolution_convert_fusion = bf16[64,4096]{1,0:T(8,128)(2,1)} fusion(bf16[64,2048]{1,0:T(8,128)(2,1)S(1)} %bitcast.36, bf16[2048,4096]{1,0:T(8,128)(2,1)} %all-gather.2.cloned.1.call-done), kind=kOutput, calls=%fused_computation | convolution fusion | flops 1074003968 | bytes 17563648 | tf_op jit(solution)/shard_map/dot_general | solution.py:267
  (79 shorter events, 31.7 us)
Async XLA Ops:
  6.5 131.9 %all-gather.2.cloned.1.call-start = ((), (), s32[]{:S(2)}) async-start(), calls=%async_computation.1 | async-start | bytes 18874368 | tf_op jit(solution)/shard_map/all_gather | solution.py:250
  6.5 14.3 %collective-permute-start.5 = (bf16[512,512]{1,0:T(8,128)(2,1)}, bf16[512,512]{1,0:T(8,128)(2,1)S(1)}, u32[]{:S(2)}, u32[]{:S(2)}) collective-permute-start(bf16[512,512]{1,0:T(8,128)(2,1)} %bitcast.32), channel_id=1, source_target_pairs={{0,6},{2,0},{4,2},{6,4},{1,7},{3,1},{5,3},{7,5},{8,14},{10,8},{12,... | collective-permute-start | bytes 1572872 | tf_op jit(solution)/shard_map/ppermute | solution.py:27
  9.3 15.2 %collective-permute-start.3 = (bf16[512,512]{1,0:T(8,128)(2,1)}, bf16[512,512]{1,0:T(8,128)(2,1)S(1)}, u32[]{:S(2)}, u32[]{:S(2)}) collective-permute-start(bf16[512,512]{1,0:T(8,128)(2,1)} %bitcast.33), channel_id=1, source_target_pairs={{0,2},{2,4},{4,6},{6,0},{1,3},{3,5},{5,7},{7,1},{8,10},{10,12},{12... | collective-permute-start | bytes 1572872 | tf_op jit(solution)/shard_map/ppermute | solution.py:27
  9.3 24.2 %collective-permute-start.7 = (bf16[512,512]{1,0:T(8,128)(2,1)}, bf16[512,512]{1,0:T(8,128)(2,1)S(1)}, u32[]{:S(2)}, u32[]{:S(2)}) collective-permute-start(bf16[512,512]{1,0:T(8,128)(2,1)} %bitcast.34), channel_id=1, source_target_pairs={{0,1},{1,0},{2,3},{3,2},{4,5},{5,4},{6,7},{7,6},{8,9},{9,8},{10,11... | collective-permute-start | bytes 1572872 | tf_op jit(solution)/shard_map/ppermute | solution.py:27
  24.6 9.8 %collective-permute-start.11 = (bf16[512,512]{1,0:T(8,128)(2,1)S(1)}, bf16[512,512]{1,0:T(8,128)(2,1)S(1)}, u32[]{:S(2)}, u32[]{:S(2)}) collective-permute-start(bf16[512,512]{1,0:T(8,128)(2,1)S(1)} %collective-permute-done.5.refs_4_), channel_id=1, source_target_pairs={{0,1},{1,0},{2,3},{3,2},{4,5},{5,4},{6,7},{7,6},{8,9},{9,8},{10,11... | collective-permute-start | bytes 1572872 | tf_op jit(solution)/shard_map/ppermute | solution.py:27
  24.7 9.7 %collective-permute-start.8 = (bf16[512,512]{1,0:T(8,128)(2,1)S(1)}, bf16[512,512]{1,0:T(8,128)(2,1)S(1)}, u32[]{:S(2)}, u32[]{:S(2)}) collective-permute-start(bf16[512,512]{1,0:T(8,128)(2,1)S(1)} %collective-permute-done.3.refs_1_), channel_id=1, source_target_pairs={{0,1},{1,0},{2,3},{3,2},{4,5},{5,4},{6,7},{7,6},{8,9},{9,8},{10,11... | collective-permute-start | bytes 1572872 | tf_op jit(solution)/shard_map/ppermute | solution.py:27
  44.1 9.4 %collective-permute-start = (bf16[528,256]{1,0:T(8,128)(2,1)S(1)}, bf16[528,256]{1,0:T(8,128)(2,1)S(1)}, u32[]{:S(2)}, u32[]{:S(2)}) collective-permute-start(bf16[528,256]{1,0:T(8,128)(2,1)S(1)} %fusion.1.query_ref), channel_id=1, source_target_pairs={{0,64},{64,128},{128,192},{192,0},{1,65},{65,129},{129,193},{193,1... | collective-permute-start | bytes 811016 | tf_op jit(solution)/shard_map/ppermute | solution.py:27
  45.7 13.6 %collective-permute-start.1 = (bf16[528,256]{1,0:T(8,128)(2,1)S(1)}, bf16[528,256]{1,0:T(8,128)(2,1)S(1)}, u32[]{:S(2)}, u32[]{:S(2)}) collective-permute-start(bf16[528,256]{1,0:T(8,128)(2,1)S(1)} %fusion.1.query_ref), channel_id=1, source_target_pairs={{0,128},{64,192},{128,0},{192,64},{1,129},{65,193},{129,1},{193,65... | collective-permute-start | bytes 811016 | tf_op jit(solution)/shard_map/ppermute | solution.py:27
  46.7 14.9 %collective-permute-start.12 = (bf16[512,256]{1,0:T(8,128)(2,1)S(1)}, bf16[512,256]{1,0:T(8,128)(2,1)S(1)}, u32[]{:S(2)}, u32[]{:S(2)}) collective-permute-start(bf16[512,256]{1,0:T(8,128)(2,1)S(1)} %get-tuple-element.8.refs_0_), channel_id=1, source_target_pairs={{0,8},{8,16},{16,24},{24,32},{32,40},{40,48},{48,56},{56,0},{1,9},... | collective-permute-start | bytes 786440 | tf_op jit(solution)/shard_map/ppermute | solution.py:27
  48.6 14.9 %collective-permute-start.13 = (bf16[512,256]{1,0:T(8,128)(2,1)S(1)}, bf16[512,256]{1,0:T(8,128)(2,1)S(1)}, u32[]{:S(2)}, u32[]{:S(2)}) collective-permute-start(bf16[512,256]{1,0:T(8,128)(2,1)S(1)} %get-tuple-element.8.refs_0_), channel_id=1, source_target_pairs={{0,56},{8,0},{16,8},{24,16},{32,24},{40,32},{48,40},{56,48},{1,57}... | collective-permute-start | bytes 786440 | tf_op jit(solution)/shard_map/ppermute | solution.py:27
  52.5 15.0 %collective-permute-start.20 = (bf16[512,256]{1,0:T(8,128)(2,1)S(1)}, bf16[512,256]{1,0:T(8,128)(2,1)S(1)}, u32[]{:S(2)}, u32[]{:S(2)}) collective-permute-start(bf16[512,256]{1,0:T(8,128)(2,1)S(1)} %get-tuple-element.9.refs_9_), channel_id=1, source_target_pairs={{0,8},{8,16},{16,24},{24,32},{32,40},{40,48},{48,56},{56,0},{1,9},... | collective-permute-start | bytes 786440 | tf_op jit(solution)/shard_map/ppermute | solution.py:27
  53.5 14.1 %collective-permute-start.21 = (bf16[512,256]{1,0:T(8,128)(2,1)S(1)}, bf16[512,256]{1,0:T(8,128)(2,1)S(1)}, u32[]{:S(2)}, u32[]{:S(2)}) collective-permute-start(bf16[512,256]{1,0:T(8,128)(2,1)S(1)} %get-tuple-element.9.refs_9_), channel_id=1, source_target_pairs={{0,56},{8,0},{16,8},{24,16},{32,24},{40,32},{48,40},{56,48},{1,57}... | collective-permute-start | bytes 786440 | tf_op jit(solution)/shard_map/ppermute | solution.py:27
  59.3 11.5 %collective-permute-start.2 = (bf16[528,256]{1,0:T(8,128)(2,1)S(1)}, bf16[528,256]{1,0:T(8,128)(2,1)}, u32[]{:S(2)}, u32[]{:S(2)}) collective-permute-start(bf16[528,256]{1,0:T(8,128)(2,1)S(1)} %fusion.1.query_ref), channel_id=1, source_target_pairs={{0,192},{64,0},{128,64},{192,128},{1,193},{65,1},{129,65},{193,129... | collective-permute-start | bytes 811016 | tf_op jit(solution)/shard_map/ppermute | solution.py:27
  61.6 13.1 %collective-permute-start.14 = (bf16[512,256]{1,0:T(8,128)(2,1)S(1)}, bf16[512,256]{1,0:T(8,128)(2,1)S(1)}, u32[]{:S(2)}, u32[]{:S(2)}) collective-permute-start(bf16[512,256]{1,0:T(8,128)(2,1)S(1)} %collective-permute-done.12.refs_1_), channel_id=1, source_target_pairs={{0,8},{8,16},{16,24},{24,32},{32,40},{40,48},{48,56},{56,0},{1,9},... | collective-permute-start | bytes 786440 | tf_op jit(solution)/shard_map/ppermute | solution.py:27
  63.5 11.1 %collective-permute-start.15 = (bf16[512,256]{1,0:T(8,128)(2,1)S(1)}, bf16[512,256]{1,0:T(8,128)(2,1)S(1)}, u32[]{:S(2)}, u32[]{:S(2)}) collective-permute-start(bf16[512,256]{1,0:T(8,128)(2,1)S(1)} %collective-permute-done.13.refs_2_), channel_id=1, source_target_pairs={{0,56},{8,0},{16,8},{24,16},{32,24},{40,32},{48,40},{56,48},{1,57}... | collective-permute-start | bytes 786440 | tf_op jit(solution)/shard_map/ppermute | solution.py:27
  67.5 12.7 %collective-permute-start.22 = (bf16[512,256]{1,0:T(8,128)(2,1)S(1)}, bf16[512,256]{1,0:T(8,128)(2,1)S(1)}, u32[]{:S(2)}, u32[]{:S(2)}) collective-permute-start(bf16[512,256]{1,0:T(8,128)(2,1)S(1)} %collective-permute-done.20.refs_10_), channel_id=1, source_target_pairs={{0,8},{8,16},{16,24},{24,32},{32,40},{40,48},{48,56},{56,0},{1,9},... | collective-permute-start | bytes 786440 | tf_op jit(solution)/shard_map/ppermute | solution.py:27
  67.5 12.7 %collective-permute-start.23 = (bf16[512,256]{1,0:T(8,128)(2,1)S(1)}, bf16[512,256]{1,0:T(8,128)(2,1)S(1)}, u32[]{:S(2)}, u32[]{:S(2)}) collective-permute-start(bf16[512,256]{1,0:T(8,128)(2,1)S(1)} %collective-permute-done.21.refs_11_), channel_id=1, source_target_pairs={{0,56},{8,0},{16,8},{24,16},{32,24},{40,32},{48,40},{56,48},{1,57}... | collective-permute-start | bytes 786440 | tf_op jit(solution)/shard_map/ppermute | solution.py:27
  74.7 11.2 %collective-permute-start.16 = (bf16[512,256]{1,0:T(8,128)(2,1)S(1)}, bf16[512,256]{1,0:T(8,128)(2,1)S(1)}, u32[]{:S(2)}, u32[]{:S(2)}) collective-permute-start(bf16[512,256]{1,0:T(8,128)(2,1)S(1)} %collective-permute-done.14.refs_3_), channel_id=1, source_target_pairs={{0,8},{8,16},{16,24},{24,32},{32,40},{40,48},{48,56},{56,0},{1,9},... | collective-permute-start | bytes 786440 | tf_op jit(solution)/shard_map/ppermute | solution.py:27
  74.7 11.3 %collective-permute-start.17 = (bf16[512,256]{1,0:T(8,128)(2,1)S(1)}, bf16[512,256]{1,0:T(8,128)(2,1)S(1)}, u32[]{:S(2)}, u32[]{:S(2)}) collective-permute-start(bf16[512,256]{1,0:T(8,128)(2,1)S(1)} %collective-permute-done.15.refs_4_), channel_id=1, source_target_pairs={{0,56},{8,0},{16,8},{24,16},{32,24},{40,32},{48,40},{56,48},{1,57}... | collective-permute-start | bytes 786440 | tf_op jit(solution)/shard_map/ppermute | solution.py:27
  80.3 11.2 %collective-permute-start.24 = (bf16[512,256]{1,0:T(8,128)(2,1)S(1)}, bf16[512,256]{1,0:T(8,128)(2,1)S(1)}, u32[]{:S(2)}, u32[]{:S(2)}) collective-permute-start(bf16[512,256]{1,0:T(8,128)(2,1)S(1)} %collective-permute-done.22.refs_12_), channel_id=1, source_target_pairs={{0,8},{8,16},{16,24},{24,32},{32,40},{40,48},{48,56},{56,0},{1,9},... | collective-permute-start | bytes 786440 | tf_op jit(solution)/shard_map/ppermute | solution.py:27
  80.3 11.3 %collective-permute-start.25 = (bf16[512,256]{1,0:T(8,128)(2,1)S(1)}, bf16[512,256]{1,0:T(8,128)(2,1)S(1)}, u32[]{:S(2)}, u32[]{:S(2)}) collective-permute-start(bf16[512,256]{1,0:T(8,128)(2,1)S(1)} %collective-permute-done.23.refs_13_), channel_id=1, source_target_pairs={{0,56},{8,0},{16,8},{24,16},{32,24},{40,32},{48,40},{56,48},{1,57}... | collective-permute-start | bytes 786440 | tf_op jit(solution)/shard_map/ppermute | solution.py:27
  100.9 15.3 %collective-permute-start.30 = (bf16[2080,128]{1,0:T(8,128)(2,1)S(1)}, bf16[2080,128]{1,0:T(8,128)(2,1)S(1)}, u32[]{:S(2)}, u32[]{:S(2)}) collective-permute-start(bf16[2080,128]{1,0:T(8,128)(2,1)S(1)} %attend.7), channel_id=1, source_target_pairs={{0,64},{64,128},{128,192},{192,0},{1,65},{65,129},{129,193},{193,1... | collective-permute-start | bytes 1597448 | tf_op jit(solution)/shard_map/ppermute | solution.py:27
  106.4 15.7 %collective-permute-start.29 = (bf16[2080,128]{1,0:T(8,128)(2,1)S(1)}, bf16[2080,128]{1,0:T(8,128)(2,1)S(1)}, u32[]{:S(2)}, u32[]{:S(2)}) collective-permute-start(bf16[2080,128]{1,0:T(8,128)(2,1)S(1)} %attend.6), channel_id=1, source_target_pairs={{0,128},{64,192},{128,0},{192,64},{1,129},{65,193},{129,1},{193,65... | collective-permute-start | bytes 1597448 | tf_op jit(solution)/shard_map/ppermute | solution.py:27
  109.2 18.5 %collective-permute-start.28 = (bf16[2080,128]{1,0:T(8,128)(2,1)S(1)}, bf16[2080,128]{1,0:T(8,128)(2,1)S(1)}, u32[]{:S(2)}, u32[]{:S(2)}) collective-permute-start(bf16[2080,128]{1,0:T(8,128)(2,1)S(1)} %attend.5), channel_id=1, source_target_pairs={{0,192},{64,0},{128,64},{192,128},{1,193},{65,1},{129,65},{193,129... | collective-permute-start | bytes 1597448 | tf_op jit(solution)/shard_map/ppermute | solution.py:27
  (13 other events, 57.1 us)
Sparse Core Ops, SparseCore 0:
  42.3 88.4 all-gather.1
where the time goes:
time: 156 us; the launch traced here: 155 us
  starting transfers between devices  51.3 us (33%)
  waiting for transfers between devices  45.7 us (29%)
  Pallas kernels  16.9 us (11%)
  between operations  14.2 us (9%)
  blocking collectives  9.95 us (6%)
  matrix products  9.58 us (6%)
  local copies, waits for them, and re-layouts  5.32 us (3%)
  other arithmetic  1.83 us (1%)
    ppermute x31, starting transfers between devices, shift(): return lax.ppermute(a, axis, [(i, (i + k) % n) for i in range(n)])  51.3 us
    ppermute x31, waiting for transfers between devices, shift(): return lax.ppermute(a, axis, [(i, (i + k) % n) for i in range(n)])  45.7 us
    pallas_call x4, Pallas kernels, attend(): pl.pallas_call(functools.partial(attend_kernel, places), out_shape=jax.Sh...  11.3 us
    all_to_all x1, blocking collectives, on_device(): lax.all_to_all(heads_out.reshape(NX * NC, SPAN, WIDE), ('x', 'c'), split_...  9.95 us
    dot_general x1, matrix products, on_device(): jnp.dot(rows, weight, preferred_element_type=jnp.float32)  9.58 us
    pallas_call x1, Pallas kernels, project(): pl.pallas_call(functools.partial(project_kernel, tuple(layout)), out_shap...  4.87 us
    unnamed x10, local copies, waits for them, and re-layouts  4.34 us
  transfers between devices with their start and end apart: 32, of which 13 were waited for; matrix products, arithmetic and copies ran while one was open for 2% of the time, Pallas kernels for 8%

commit v1 on v0

--- a/solution.py
+++ b/solution.py
@@ -20,6 +20,7 @@
 WIDE = 2 * HD
 OROWS = SPANS_DEV * WIDE
 VMEM_LIMIT = 48 * 1024 * 1024
+PROJECT_LIMIT = 58 * 1024 * 1024
 
 
 def shift(a, axis, k):
@@ -39,49 +40,62 @@
     return out
 
 
-def project_kernel(layout, feature_ref, *refs):
-    pieces, (key_ref, value_ref) = refs[: -2 - PAIRS], refs[-2 - PAIRS : -PAIRS]
-    out_refs = refs[-PAIRS:]
+def project_kernel(rows, feature_ref, *refs):
+    n = len(rows)
+    pieces, (key_ref, value_ref, out_ref, tokens, weights, sems) = refs[:n], refs[n:]
+    width = tokens.shape[2]
+    copies = []
+    for i, (row, piece) in enumerate(zip(rows, pieces)):
+        at = pl.ds(pl.multiple_of(feature_ref[i] * width, width), width)
+        copies.append(
+            [
+                pltpu.make_async_copy(piece.at[pl.ds(row, 2 * NLEN)], tokens.at[i], sems.at[i]),
+                pltpu.make_async_copy(key_ref.at[at], weights.at[i], sems.at[n + i]),
+                pltpu.make_async_copy(value_ref.at[at], weights.at[n + i], sems.at[2 * n + i]),
+            ]
+        )
+    for group in copies:
+        for copy in group:
+            copy.start()
     key_sum = value_sum = squares = None
-    for block, members in enumerate(layout):
-        rows = [pieces[i][...] for i in members]
-        tokens = rows[0] if len(rows) == 1 else jnp.concatenate(rows, axis=0)
-        width = tokens.shape[1]
-        at = pl.ds(pl.multiple_of(feature_ref[block] * width, width), width)
-        k = jnp.dot(tokens, key_ref[at, :], preferred_element_type=jnp.float32)
-        v = jnp.dot(tokens, value_ref[at, :], preferred_element_type=jnp.float32)
-        f = tokens.astype(jnp.float32)
+    for i, group in enumerate(copies):
+        for copy in group:
+            copy.wait()
+        block = tokens[i]
+        k = jnp.dot(block, weights[i], preferred_element_type=jnp.float32)
+        v = jnp.dot(block, weights[n + i], preferred_element_type=jnp.float32)
+        f = block.astype(jnp.float32)
         s = jnp.sum(f * f, axis=1, keepdims=True)
         if key_sum is None:
             key_sum, value_sum, squares = k, v, s
         else:
             key_sum, value_sum, squares = key_sum + k, value_sum + v, squares + s
     inverse = lax.rsqrt(squares / key_ref.shape[0] + EPSILON)
-    keys = (key_sum * inverse).astype(jnp.bfloat16)
-    values = value_sum * inverse
-    for pair, out_ref in enumerate(out_refs):
-        rows = slice(pair * 2 * NLEN, (pair + 1) * 2 * NLEN)
-        out_ref[: 2 * NLEN, :] = keys[rows]
-        out_ref[2 * NLEN :, :] = values[rows].T.astype(jnp.bfloat16)
+    out_ref[: 2 * NLEN, :] = (key_sum * inverse).astype(jnp.bfloat16)
+    out_ref[2 * NLEN :, :] = (value_sum * inverse).T.astype(jnp.bfloat16)
 
 
 def project(feature, blocks, key_weight, value_weight):
-    pieces, layout = [], []
-    for members in blocks:
-        layout.append(tuple(range(len(pieces), len(pieces) + len(members))))
-        pieces += members
+    rows = tuple(row for row, _ in blocks)
+    width = key_weight.shape[0] // len(blocks)
     vmem = pl.BlockSpec(memory_space=pltpu.VMEM)
     return pl.pallas_call(
-        functools.partial(project_kernel, tuple(layout)),
-        out_shape=[jax.ShapeDtypeStruct((BLOCK, WIDE), jnp.bfloat16)] * PAIRS,
-        in_specs=[pl.BlockSpec(memory_space=pltpu.SMEM)] + [vmem] * (len(pieces) + 2),
-        out_specs=[vmem] * PAIRS,
-        compiler_params=pltpu.CompilerParams(vmem_limit_bytes=VMEM_LIMIT),
+        functools.partial(project_kernel, rows),
+        out_shape=jax.ShapeDtypeStruct((BLOCK, WIDE), jnp.bfloat16),
+        in_specs=[pl.BlockSpec(memory_space=pltpu.SMEM)]
+        + [pl.BlockSpec(memory_space=pltpu.HBM)] * (len(blocks) + 2),
+        out_specs=vmem,
+        scratch_shapes=[
+            pltpu.VMEM((len(blocks), 2 * NLEN, width), jnp.bfloat16),
+            pltpu.VMEM((2 * len(blocks), width, WIDE), jnp.bfloat16),
+            pltpu.SemaphoreType.DMA((3 * len(blocks),)),
+        ],
+        compiler_params=pltpu.CompilerParams(vmem_limit_bytes=PROJECT_LIMIT),
         cost_estimate=pl.CostEstimate(
-            flops=2 * 512 * 4096 * 512, bytes_accessed=8 << 20, transcendentals=0
+            flops=256 * 4096 * 1024, bytes_accessed=6 << 20, transcendentals=0
         ),
         name="project",
-    )(feature, *pieces, key_weight, value_weight)
+    )(feature, *[a for _, a in blocks], key_weight, value_weight)
 
 
 def attend_kernel(places, place_ref, lane_ref, bias_ref, query_ref, *refs):
@@ -219,6 +233,32 @@
     )(lambda_head, *messages)
 
 
+def output_kernel(rows_ref, weight_ref, out_ref):
+    out_ref[...] = jnp.dot(
+        rows_ref[...], weight_ref[...], preferred_element_type=jnp.float32
+    ).astype(jnp.bfloat16)
+
+
+def output(rows, weight):
+    depth, width = weight.shape
+    step = 512
+    return pl.pallas_call(
+        output_kernel,
+        grid=(width // step,),
+        out_shape=jax.ShapeDtypeStruct((rows.shape[0], width), jnp.bfloat16),
+        in_specs=[
+            pl.BlockSpec((rows.shape[0], depth), lambda i: (0, 0)),
+            pl.BlockSpec((depth, step), lambda i: (0, i)),
+        ],
+        out_specs=pl.BlockSpec((rows.shape[0], step), lambda i: (0, i)),
+        compiler_params=pltpu.CompilerParams(vmem_limit_bytes=VMEM_LIMIT),
+        cost_estimate=pl.CostEstimate(
+            flops=2 * 64 * 2048 * 4096, bytes_accessed=16 << 20, transcendentals=0
+        ),
+        name="output",
+    )(rows, weight)
+
+
 def on_device(
     queries, nbr_shard, nbr_row, database, key_weight, value_weight, lambda_head, out_weight
 ):
@@ -236,10 +276,27 @@
             for side in (c, 1 - c)
         ]
     )
-    own = ring_pieces(database.reshape(ENTRIES * NLEN, -1), "x")
+    tokens = database.reshape(ENTRIES * NLEN, -1)
+    half = tokens.shape[0] // 2
+    up, down = shift(tokens, "x", 1), shift(tokens, "x", -1)
+    *asked, low, high = lax.optimization_barrier((*asked, up[:half], down[half:]))
+    own = [(0, 0, tokens), (1, 0, up), (3, 0, down)]
+    own += [(2, 0, shift(low, "x", 1)), (2, half, shift(high, "x", -1))]
     other = [(k, r, shift(a, "c", 1)) for k, r, a in own]
-    blocks = [[a for k, _, a in side if k == d] for side in (own, other) for d in range(NX)]
-    rows = project(feature, blocks, key_weight, value_weight)
+    arrived = lax.optimization_barrier([a for _, _, a in own + other])
+    own, other = (
+        [(k, r, a) for (k, r, _), a in zip(own, arrived[at : at + len(own)])]
+        for at in (0, len(own))
+    )
+    rows = []
+    for pair in range(PAIRS):
+        blocks = []
+        for side in (own, other):
+            for d in range(NX):
+                for k, r, a in side:
+                    if k == d and r <= pair * half < r + a.shape[0]:
+                        blocks.append((pair * half - r, a))
+        rows.append(project(feature, blocks, key_weight, value_weight))
     table = [
         ((pair * NZ + k) * BLOCK + r, a)
         for pair in range(PAIRS)
@@ -264,7 +321,7 @@
         heads_out.reshape(NX * NC, SPAN, WIDE), ("x", "c"), split_axis=0, concat_axis=0, tiled=True
     )
     rows = jnp.swapaxes(heads, 0, 1).reshape(SPAN, NX * NC * WIDE)
-    return jnp.dot(rows, weight, preferred_element_type=jnp.float32).astype(jnp.bfloat16)
+    return output(rows, weight)
 
 
 def solution(mesh):

time: 156 us -> 158 us (1.013)
  Pallas kernels: 16.9 us -> 31.3 us
  matrix products: 9.58 us -> 0 us
  local copies, waits for them, and re-layouts: 5.32 us -> 2.04 us
  starting transfers between devices: 51.3 us -> 48.8 us
    pallas_call x1 -> x3, Pallas kernels: 4.87 us -> 19.7 us  [the longest x1 10.1 us: output(): pl.pallas_call(output_kernel, grid=(width // step,), out_shape=jax.ShapeD...]
    dot_general x1 -> x0, matrix products: 9.58 us -> none  [on_device(): jnp.dot(rows, weight, preferred_element_type=jnp.float32)]
    unnamed x10 -> x14, local copies, waits for them, and re-layouts: 4.34 us -> 1.74 us
    ppermute x31, starting transfers between devices: 51.3 us -> 48.8 us  [shift(): return lax.ppermute(a, axis, [(i, (i + k) % n) for i in range(n)])]
  transfers between devices with their start and end apart: 32 -> 32, of which waited for: 13 -> 17; matrix products, arithmetic and copies ran while one was open for 2% -> 2% of each run, Pallas kernels for 8% -> 10%
where the time goes in v1:
time: 158 us; the launch traced here: 157 us
  starting transfers between devices  48.8 us (31%)
  waiting for transfers between devices  47.1 us (30%)
  Pallas kernels  31.3 us (20%)
  between operations  14.3 us (9%)
  blocking collectives  11.2 us (7%)
  other arithmetic  2.35 us (1%)
  local copies, waits for them, and re-layouts  2.04 us (1%)
    ppermute x31, starting transfers between devices, shift(): return lax.ppermute(a, axis, [(i, (i + k) % n) for i in range(n)])  48.8 us
    ppermute x31, waiting for transfers between devices, shift(): return lax.ppermute(a, axis, [(i, (i + k) % n) for i in range(n)])  47.1 us
    all_to_all x1, blocking collectives, on_device(): lax.all_to_all(heads_out.reshape(NX * NC, SPAN, WIDE), ('x', 'c'), split_...  11.2 us
    pallas_call x4, Pallas kernels, attend(): pl.pallas_call(functools.partial(attend_kernel, places), out_shape=jax.Sh...  10.9 us
    pallas_call x1, Pallas kernels, output(): pl.pallas_call(output_kernel, grid=(width // step,), out_shape=jax.ShapeD...  10.1 us
    pallas_call x2, Pallas kernels, project(): pl.pallas_call(functools.partial(project_kernel, rows), out_shape=jax.Sha...  9.61 us
  transfers between devices with their start and end apart: 32, of which 17 were waited for; matrix products, arithmetic and copies ran while one was open for 2% of the time, Pallas kernels for 10%

profile of v1, /device:TPU:8, one launch (start us, length us, event | category | flops | bytes accessed | tf_op | source)
XLA Modules:
  0.0 157.2 jit_solution(17092901171972151084)
XLA Ops:
  16.6 5.0 %collective-permute-done.3.refs_1_ = bf16[512,512]{1,0:T(8,128)(2,1)S(1)} collective-permute-done((bf16[512,512]{1,0:T(8,128)(2,1)}, bf16[512,512]{1,0:T(8,128)(2,1)S(1)}, u32[]{:S(2)}, u32[]{:S(2)}) %collective-permute-start.3) | collective-permute-done | bytes 524320 | tf_op jit(solution)/shard_map/ppermute | solution.py:28
  24.2 3.1 %collective-permute-done.2.query_ref = bf16[528,256]{1,0:T(8,128)(2,1)S(1)} collective-permute-done((bf16[528,256]{1,0:T(8,128)(2,1)S(1)}, bf16[528,256]{1,0:T(8,128)(2,1)S(1)}, u32[]{:S(2)}, u32[]{:S(2)}) %collective-permute-start.2) | collective-permute-done | bytes 270368 | tf_op jit(solution)/shard_map/ppermute | solution.py:28
  27.6 3.0 %collective-permute-start.6 = (bf16[256,512]{1,0:T(8,128)(2,1)S(1)}, bf16[256,512]{1,0:T(8,128)(2,1)S(1)}, u32[]{:S(2)}, u32[]{:S(2)}) collective-permute-start(bf16[256,512]{1,0:T(8,128)(2,1)S(1)} %slice.89), channel_id=1, source_target_pairs={{0,6},{2,0},{4,2},{6,4},{1,7},{3,1},{5,3},{7,5},{8,14},{10,8},{12,... | collective-permute-start | bytes 786440 | tf_op jit(solution)/shard_map/ppermute | solution.py:28
  31.0 5.0 %collective-permute-done.5.refs_2_ = bf16[256,512]{1,0:T(8,128)(2,1)} collective-permute-done((bf16[256,512]{1,0:T(8,128)(2,1)S(1)}, bf16[256,512]{1,0:T(8,128)(2,1)}, u32[]{:S(2)}, u32[]{:S(2)}) %collective-permute-start.5) | collective-permute-done | bytes 262176 | tf_op jit(solution)/shard_map/ppermute | solution.py:28
  38.9 4.7 %project.2.refs_0_ = bf16[512,256]{1,0:T(8,128)(2,1)} custom-call(s32[8]{0:T(128)} %pad_add_fusion.feature_ref, bf16[512,512]{1,0:T(8,128)(2,1)} %bitcast.34, bf16[512,512]{1,0:T(8,128)(2,1)} %copy-done.2, bf16[256,512]{1,0:T(8,128)(2,1)} %collective-permute-done.5.refs_2_, bf16[512,512]{1,0:T(8,128)(2,1)} %copy-done.3, bf16[512,512]{1,0:T(8,128)(2,1)} %copy-done.4, ...), custom_call_target="tpu_custom_call" | custom-call | flops 1073741824 | bytes 6291456 | tf_op jit(solution)/shard_map/project/pallas_call | solution.py:82
  43.7 4.9 %project.3.refs_9_ = bf16[512,256]{1,0:T(8,128)(2,1)} custom-call(s32[8]{0:T(128)} %pad_add_fusion.feature_ref, bf16[512,512]{1,0:T(8,128)(2,1)} %bitcast.35, bf16[512,512]{1,0:T(8,128)(2,1)} %copy-done.2, bf16[256,512]{1,0:T(8,128)(2,1)} %copy-done.6, bf16[512,512]{1,0:T(8,128)(2,1)} %copy-done.3, bf16[512,512]{1,0:T(8,128)(2,1)} %copy-done.4, ...), custom_call_target="tpu_custom_call" | custom-call | flops 1073741824 | bytes 6291456 | tf_op jit(solution)/shard_map/project/pallas_call | solution.py:82
  50.6 4.2 %collective-permute-start.21 = (bf16[512,256]{1,0:T(8,128)(2,1)}, bf16[512,256]{1,0:T(8,128)(2,1)S(1)}, u32[]{:S(2)}, u32[]{:S(2)}) collective-permute-start(bf16[512,256]{1,0:T(8,128)(2,1)} %project.3.refs_9_), channel_id=1, source_target_pairs={{0,56},{8,0},{16,8},{24,16},{32,24},{40,32},{48,40},{56,48},{1,57}... | collective-permute-start | bytes 786440 | tf_op jit(solution)/shard_map/ppermute | solution.py:28
  54.8 3.2 %collective-permute-start.13 = (bf16[512,256]{1,0:T(8,128)(2,1)S(1)}, bf16[512,256]{1,0:T(8,128)(2,1)S(1)}, u32[]{:S(2)}, u32[]{:S(2)}) collective-permute-start(bf16[512,256]{1,0:T(8,128)(2,1)S(1)} %copy-done), channel_id=1, source_target_pairs={{0,56},{8,0},{16,8},{24,16},{32,24},{40,32},{48,40},{56,48},{1,57}... | collective-permute-start | bytes 786440 | tf_op jit(solution)/shard_map/ppermute | solution.py:28
  58.0 3.8 %collective-permute-done.20.refs_10_ = bf16[512,256]{1,0:T(8,128)(2,1)S(1)} collective-permute-done((bf16[512,256]{1,0:T(8,128)(2,1)}, bf16[512,256]{1,0:T(8,128)(2,1)S(1)}, u32[]{:S(2)}, u32[]{:S(2)}) %collective-permute-start.20) | collective-permute-done | bytes 262176 | tf_op jit(solution)/shard_map/ppermute | solution.py:28
  61.8 3.5 %collective-permute-start.23 = (bf16[512,256]{1,0:T(8,128)(2,1)S(1)}, bf16[512,256]{1,0:T(8,128)(2,1)S(1)}, u32[]{:S(2)}, u32[]{:S(2)}) collective-permute-start(bf16[512,256]{1,0:T(8,128)(2,1)S(1)} %collective-permute-done.21.refs_11_), channel_id=1, source_target_pairs={{0,56},{8,0},{16,8},{24,16},{32,24},{40,32},{48,40},{56,48},{1,57}... | collective-permute-start | bytes 786440 | tf_op jit(solution)/shard_map/ppermute | solution.py:28
  67.5 3.5 %collective-permute-start.15 = (bf16[512,256]{1,0:T(8,128)(2,1)S(1)}, bf16[512,256]{1,0:T(8,128)(2,1)S(1)}, u32[]{:S(2)}, u32[]{:S(2)}) collective-permute-start(bf16[512,256]{1,0:T(8,128)(2,1)S(1)} %collective-permute-done.13.refs_2_), channel_id=1, source_target_pairs={{0,56},{8,0},{16,8},{24,16},{32,24},{40,32},{48,40},{56,48},{1,57}... | collective-permute-start | bytes 786440 | tf_op jit(solution)/shard_map/ppermute | solution.py:28
  73.1 3.5 %collective-permute-start.25 = (bf16[512,256]{1,0:T(8,128)(2,1)S(1)}, bf16[512,256]{1,0:T(8,128)(2,1)S(1)}, u32[]{:S(2)}, u32[]{:S(2)}) collective-permute-start(bf16[512,256]{1,0:T(8,128)(2,1)S(1)} %collective-permute-done.23.refs_13_), channel_id=1, source_target_pairs={{0,56},{8,0},{16,8},{24,16},{32,24},{40,32},{48,40},{56,48},{1,57}... | collective-permute-start | bytes 786440 | tf_op jit(solution)/shard_map/ppermute | solution.py:28
  78.7 3.5 %collective-permute-start.17 = (bf16[512,256]{1,0:T(8,128)(2,1)S(1)}, bf16[512,256]{1,0:T(8,128)(2,1)S(1)}, u32[]{:S(2)}, u32[]{:S(2)}) collective-permute-start(bf16[512,256]{1,0:T(8,128)(2,1)S(1)} %collective-permute-done.15.refs_4_), channel_id=1, source_target_pairs={{0,56},{8,0},{16,8},{24,16},{32,24},{40,32},{48,40},{56,48},{1,57}... | collective-permute-start | bytes 786440 | tf_op jit(solution)/shard_map/ppermute | solution.py:28
  84.4 3.5 %collective-permute-start.27 = (bf16[256,256]{1,0:T(8,128)(2,1)S(1)}, bf16[256,256]{1,0:T(8,128)(2,1)S(1)}, u32[]{:S(2)}, u32[]{:S(2)}) collective-permute-start(bf16[256,256]{1,0:T(8,128)(2,1)S(1)} %slice.93), channel_id=1, source_target_pairs={{0,56},{8,0},{16,8},{24,16},{32,24},{40,32},{48,40},{56,48},{1,57}... | collective-permute-start | bytes 393224 | tf_op jit(solution)/shard_map/ppermute | solution.py:28
  90.1 3.7 %collective-permute-start.19 = (bf16[256,256]{1,0:T(8,128)(2,1)S(1)}, bf16[256,256]{1,0:T(8,128)(2,1)S(1)}, u32[]{:S(2)}, u32[]{:S(2)}) collective-permute-start(bf16[256,256]{1,0:T(8,128)(2,1)S(1)} %slice.91), channel_id=1, source_target_pairs={{0,56},{8,0},{16,8},{24,16},{32,24},{40,32},{48,40},{56,48},{1,57}... | collective-permute-start | bytes 393224 | tf_op jit(solution)/shard_map/ppermute | solution.py:28
  97.2 2.7 %attend.7 = bf16[2080,128]{1,0:T(8,128)(2,1)S(1)} custom-call(s32[16]{0:T(128)S(1)} %get-tuple-element.56.place_ref, s32[16]{0:T(128)S(1)} %get-tuple-element.43.lane_ref, f32[16]{0:T(128)S(1)} %get-tuple-element.39.bias_ref, bf16[528,256]{1,0:T(8,128)(2,1)S(1)} %collective-permute-done.2.query_ref, bf16[512,256]{1,0:T(8,128)(2,1)S(1)} %copy-done, ...), custom_call_target="tpu_custom_call" | custom-call | flops 536870912 | bytes 6291456 | tf_op jit(solution)/shard_map/attend/pallas_call | solution.py:171
  100.2 2.7 %attend.6 = bf16[2080,128]{1,0:T(8,128)(2,1)S(1)} custom-call(s32[16]{0:T(128)S(1)} %get-tuple-element.55.place_ref, s32[16]{0:T(128)S(1)} %get-tuple-element.44.lane_ref, f32[16]{0:T(128)S(1)} %get-tuple-element.40.bias_ref, bf16[528,256]{1,0:T(8,128)(2,1)S(1)} %collective-permute-done.1.query_ref, bf16[512,256]{1,0:T(8,128)(2,1)S(1)} %copy-done, ...), custom_call_target="tpu_custom_call" | custom-call | flops 536870912 | bytes 6291456 | tf_op jit(solution)/shard_map/attend/pallas_call | solution.py:171
  105.4 2.7 %attend.5 = bf16[2080,128]{1,0:T(8,128)(2,1)S(1)} custom-call(s32[16]{0:T(128)S(1)} %get-tuple-element.54.place_ref, s32[16]{0:T(128)S(1)} %get-tuple-element.45.lane_ref, f32[16]{0:T(128)S(1)} %get-tuple-element.41.bias_ref, bf16[528,256]{1,0:T(8,128)(2,1)S(1)} %collective-permute-done.query_ref, bf16[512,256]{1,0:T(8,128)(2,1)S(1)} %copy-done, ...), custom_call_target="tpu_custom_call" | custom-call | flops 536870912 | bytes 6291456 | tf_op jit(solution)/shard_map/attend/pallas_call | solution.py:171
  108.1 2.7 %collective-permute-start.28 = (bf16[2080,128]{1,0:T(8,128)(2,1)S(1)}, bf16[2080,128]{1,0:T(8,128)(2,1)S(1)}, u32[]{:S(2)}, u32[]{:S(2)}) collective-permute-start(bf16[2080,128]{1,0:T(8,128)(2,1)S(1)} %attend.5), channel_id=1, source_target_pairs={{0,192},{64,0},{128,64},{192,128},{1,193},{65,1},{129,65},{193,129... | collective-permute-start | bytes 1597448 | tf_op jit(solution)/shard_map/ppermute | solution.py:28
  111.5 2.7 %attend.4.refs_0_ = bf16[2080,128]{1,0:T(8,128)(2,1)S(1)} custom-call(s32[16]{0:T(128)S(1)} %get-tuple-element.53.place_ref, s32[16]{0:T(128)S(1)} %get-tuple-element.46.lane_ref, f32[16]{0:T(128)S(1)} %get-tuple-element.42.bias_ref, bf16[528,256]{1,0:T(8,128)(2,1)S(1)} %fusion.1.query_ref, bf16[512,256]{1,0:T(8,128)(2,1)S(1)} %copy-done, ...), custom_call_target="tpu_custom_call" | custom-call | flops 536870912 | bytes 6291456 | tf_op jit(solution)/shard_map/attend/pallas_call | solution.py:171
  115.1 4.6 %collective-permute-done.29.refs_2_ = bf16[2080,128]{1,0:T(8,128)(2,1)S(1)} collective-permute-done((bf16[2080,128]{1,0:T(8,128)(2,1)S(1)}, bf16[2080,128]{1,0:T(8,128)(2,1)S(1)}, u32[]{:S(2)}, u32[]{:S(2)}) %collective-permute-start.29) | collective-permute-done | bytes 532512 | tf_op jit(solution)/shard_map/ppermute | solution.py:28
  119.6 8.6 %collective-permute-done.28.refs_1_ = bf16[2080,128]{1,0:T(8,128)(2,1)S(1)} collective-permute-done((bf16[2080,128]{1,0:T(8,128)(2,1)S(1)}, bf16[2080,128]{1,0:T(8,128)(2,1)S(1)}, u32[]{:S(2)}, u32[]{:S(2)}) %collective-permute-start.28) | collective-permute-done | bytes 532512 | tf_op jit(solution)/shard_map/ppermute | solution.py:28
  128.9 11.2 %all_to_all.5 = bf16[8,64,256]{2,1,0:T(8,128)(2,1)S(1)} all-to-all(bf16[8,64,256]{2,1,0:T(8,128)(2,1)S(1)} %bitcast.30), channel_id=1, replica_groups=mesh['y'=4,'z'=8,'x'=4,'c'=2] {'x','c'}, dimensions={0} | all-to-all | bytes 524288 | tf_op jit(solution)/shard_map/all_to_all | solution.py:320
  140.2 10.1 %output.1 = bf16[64,4096]{1,0:T(8,128)(2,1)} custom-call(bf16[64,2048]{1,0:T(8,128)(2,1)S(1)} %bitcast.29, bf16[2048,4096]{1,0:T(8,128)(2,1)} %all-gather.2.cloned.1.call-done.weight_ref), custom_call_target="tpu_custom_call" | custom-call | flops 1073741824 | bytes 16777216 | tf_op jit(solution)/shard_map/output/pallas_call | solution.py:245
  (85 shorter events, 36.6 us)
Async XLA Ops:
  6.5 133.7 %all-gather.2.cloned.1.call-start = ((), (), s32[]{:S(2)}) async-start(), calls=%async_computation.1 | async-start | bytes 18874368 | tf_op jit(solution)/shard_map/all_gather | solution.py:307
  6.5 15.1 %collective-permute-start.3 = (bf16[512,512]{1,0:T(8,128)(2,1)}, bf16[512,512]{1,0:T(8,128)(2,1)S(1)}, u32[]{:S(2)}, u32[]{:S(2)}) collective-permute-start(bf16[512,512]{1,0:T(8,128)(2,1)} %bitcast.31), channel_id=1, source_target_pairs={{0,2},{2,4},{4,6},{6,0},{1,3},{3,5},{5,7},{7,1},{8,10},{10,12},{12... | collective-permute-start | bytes 1572872 | tf_op jit(solution)/shard_map/ppermute | solution.py:28
  8.0 13.6 %collective-permute-start.4 = (bf16[512,512]{1,0:T(8,128)(2,1)}, bf16[512,512]{1,0:T(8,128)(2,1)S(1)}, u32[]{:S(2)}, u32[]{:S(2)}) collective-permute-start(bf16[512,512]{1,0:T(8,128)(2,1)} %bitcast.32), channel_id=1, source_target_pairs={{0,6},{2,0},{4,2},{6,4},{1,7},{3,1},{5,3},{7,5},{8,14},{10,8},{12,... | collective-permute-start | bytes 1572872 | tf_op jit(solution)/shard_map/ppermute | solution.py:28
  11.6 10.1 %collective-permute-start = (bf16[528,256]{1,0:T(8,128)(2,1)S(1)}, bf16[528,256]{1,0:T(8,128)(2,1)S(1)}, u32[]{:S(2)}, u32[]{:S(2)}) collective-permute-start(bf16[528,256]{1,0:T(8,128)(2,1)S(1)} %fusion.1.query_ref), channel_id=1, source_target_pairs={{0,64},{64,128},{128,192},{192,0},{1,65},{65,129},{129,193},{193,1... | collective-permute-start | bytes 811016 | tf_op jit(solution)/shard_map/ppermute | solution.py:28
  13.3 10.9 %collective-permute-start.1 = (bf16[528,256]{1,0:T(8,128)(2,1)S(1)}, bf16[528,256]{1,0:T(8,128)(2,1)S(1)}, u32[]{:S(2)}, u32[]{:S(2)}) collective-permute-start(bf16[528,256]{1,0:T(8,128)(2,1)S(1)} %fusion.1.query_ref), channel_id=1, source_target_pairs={{0,128},{64,192},{128,0},{192,64},{1,129},{65,193},{129,1},{193,65... | collective-permute-start | bytes 811016 | tf_op jit(solution)/shard_map/ppermute | solution.py:28
  16.0 11.3 %collective-permute-start.2 = (bf16[528,256]{1,0:T(8,128)(2,1)S(1)}, bf16[528,256]{1,0:T(8,128)(2,1)S(1)}, u32[]{:S(2)}, u32[]{:S(2)}) collective-permute-start(bf16[528,256]{1,0:T(8,128)(2,1)S(1)} %fusion.1.query_ref), channel_id=1, source_target_pairs={{0,192},{64,0},{128,64},{192,128},{1,193},{65,1},{129,65},{193,129... | collective-permute-start | bytes 811016 | tf_op jit(solution)/shard_map/ppermute | solution.py:28
  21.6 15.6 %collective-permute-start.7 = (bf16[512,512]{1,0:T(8,128)(2,1)}, bf16[512,512]{1,0:T(8,128)(2,1)S(1)}, u32[]{:S(2)}, u32[]{:S(2)}) collective-permute-start(bf16[512,512]{1,0:T(8,128)(2,1)} %bitcast.33), channel_id=1, source_target_pairs={{0,1},{1,0},{2,3},{3,2},{4,5},{5,4},{6,7},{7,6},{8,9},{9,8},{10,11... | collective-permute-start | bytes 1572872 | tf_op jit(solution)/shard_map/ppermute | solution.py:28
  48.6 13.2 %collective-permute-start.20 = (bf16[512,256]{1,0:T(8,128)(2,1)}, bf16[512,256]{1,0:T(8,128)(2,1)S(1)}, u32[]{:S(2)}, u32[]{:S(2)}) collective-permute-start(bf16[512,256]{1,0:T(8,128)(2,1)} %project.3.refs_9_), channel_id=1, source_target_pairs={{0,8},{8,16},{16,24},{24,32},{32,40},{40,48},{48,56},{56,0},{1,9},... | collective-permute-start | bytes 786440 | tf_op jit(solution)/shard_map/ppermute | solution.py:28
  50.6 11.2 %collective-permute-start.21 = (bf16[512,256]{1,0:T(8,128)(2,1)}, bf16[512,256]{1,0:T(8,128)(2,1)S(1)}, u32[]{:S(2)}, u32[]{:S(2)}) collective-permute-start(bf16[512,256]{1,0:T(8,128)(2,1)} %project.3.refs_9_), channel_id=1, source_target_pairs={{0,56},{8,0},{16,8},{24,16},{32,24},{40,32},{48,40},{56,48},{1,57}... | collective-permute-start | bytes 786440 | tf_op jit(solution)/shard_map/ppermute | solution.py:28
  54.8 12.6 %collective-permute-start.12 = (bf16[512,256]{1,0:T(8,128)(2,1)S(1)}, bf16[512,256]{1,0:T(8,128)(2,1)S(1)}, u32[]{:S(2)}, u32[]{:S(2)}) collective-permute-start(bf16[512,256]{1,0:T(8,128)(2,1)S(1)} %copy-done), channel_id=1, source_target_pairs={{0,8},{8,16},{16,24},{24,32},{32,40},{40,48},{48,56},{56,0},{1,9},... | collective-permute-start | bytes 786440 | tf_op jit(solution)/shard_map/ppermute | solution.py:28
  54.8 12.6 %collective-permute-start.13 = (bf16[512,256]{1,0:T(8,128)(2,1)S(1)}, bf16[512,256]{1,0:T(8,128)(2,1)S(1)}, u32[]{:S(2)}, u32[]{:S(2)}) collective-permute-start(bf16[512,256]{1,0:T(8,128)(2,1)S(1)} %copy-done), channel_id=1, source_target_pairs={{0,56},{8,0},{16,8},{24,16},{32,24},{40,32},{48,40},{56,48},{1,57}... | collective-permute-start | bytes 786440 | tf_op jit(solution)/shard_map/ppermute | solution.py:28
  61.8 11.2 %collective-permute-start.22 = (bf16[512,256]{1,0:T(8,128)(2,1)S(1)}, bf16[512,256]{1,0:T(8,128)(2,1)S(1)}, u32[]{:S(2)}, u32[]{:S(2)}) collective-permute-start(bf16[512,256]{1,0:T(8,128)(2,1)S(1)} %collective-permute-done.20.refs_10_), channel_id=1, source_target_pairs={{0,8},{8,16},{16,24},{24,32},{32,40},{40,48},{48,56},{56,0},{1,9},... | collective-permute-start | bytes 786440 | tf_op jit(solution)/shard_map/ppermute | solution.py:28
  61.8 11.2 %collective-permute-start.23 = (bf16[512,256]{1,0:T(8,128)(2,1)S(1)}, bf16[512,256]{1,0:T(8,128)(2,1)S(1)}, u32[]{:S(2)}, u32[]{:S(2)}) collective-permute-start(bf16[512,256]{1,0:T(8,128)(2,1)S(1)} %collective-permute-done.21.refs_11_), channel_id=1, source_target_pairs={{0,56},{8,0},{16,8},{24,16},{32,24},{40,32},{48,40},{56,48},{1,57}... | collective-permute-start | bytes 786440 | tf_op jit(solution)/shard_map/ppermute | solution.py:28
  67.5 11.2 %collective-permute-start.14 = (bf16[512,256]{1,0:T(8,128)(2,1)S(1)}, bf16[512,256]{1,0:T(8,128)(2,1)S(1)}, u32[]{:S(2)}, u32[]{:S(2)}) collective-permute-start(bf16[512,256]{1,0:T(8,128)(2,1)S(1)} %collective-permute-done.12.refs_1_), channel_id=1, source_target_pairs={{0,8},{8,16},{16,24},{24,32},{32,40},{40,48},{48,56},{56,0},{1,9},... | collective-permute-start | bytes 786440 | tf_op jit(solution)/shard_map/ppermute | solution.py:28
  67.5 11.2 %collective-permute-start.15 = (bf16[512,256]{1,0:T(8,128)(2,1)S(1)}, bf16[512,256]{1,0:T(8,128)(2,1)S(1)}, u32[]{:S(2)}, u32[]{:S(2)}) collective-permute-start(bf16[512,256]{1,0:T(8,128)(2,1)S(1)} %collective-permute-done.13.refs_2_), channel_id=1, source_target_pairs={{0,56},{8,0},{16,8},{24,16},{32,24},{40,32},{48,40},{56,48},{1,57}... | collective-permute-start | bytes 786440 | tf_op jit(solution)/shard_map/ppermute | solution.py:28
  73.1 11.2 %collective-permute-start.24 = (bf16[512,256]{1,0:T(8,128)(2,1)S(1)}, bf16[512,256]{1,0:T(8,128)(2,1)S(1)}, u32[]{:S(2)}, u32[]{:S(2)}) collective-permute-start(bf16[512,256]{1,0:T(8,128)(2,1)S(1)} %collective-permute-done.22.refs_12_), channel_id=1, source_target_pairs={{0,8},{8,16},{16,24},{24,32},{32,40},{40,48},{48,56},{56,0},{1,9},... | collective-permute-start | bytes 786440 | tf_op jit(solution)/shard_map/ppermute | solution.py:28
  73.1 11.3 %collective-permute-start.25 = (bf16[512,256]{1,0:T(8,128)(2,1)S(1)}, bf16[512,256]{1,0:T(8,128)(2,1)S(1)}, u32[]{:S(2)}, u32[]{:S(2)}) collective-permute-start(bf16[512,256]{1,0:T(8,128)(2,1)S(1)} %collective-permute-done.23.refs_13_), channel_id=1, source_target_pairs={{0,56},{8,0},{16,8},{24,16},{32,24},{40,32},{48,40},{56,48},{1,57}... | collective-permute-start | bytes 786440 | tf_op jit(solution)/shard_map/ppermute | solution.py:28
  78.7 11.2 %collective-permute-start.16 = (bf16[512,256]{1,0:T(8,128)(2,1)S(1)}, bf16[512,256]{1,0:T(8,128)(2,1)S(1)}, u32[]{:S(2)}, u32[]{:S(2)}) collective-permute-start(bf16[512,256]{1,0:T(8,128)(2,1)S(1)} %collective-permute-done.14.refs_3_), channel_id=1, source_target_pairs={{0,8},{8,16},{16,24},{24,32},{32,40},{40,48},{48,56},{56,0},{1,9},... | collective-permute-start | bytes 786440 | tf_op jit(solution)/shard_map/ppermute | solution.py:28
  78.7 11.3 %collective-permute-start.17 = (bf16[512,256]{1,0:T(8,128)(2,1)S(1)}, bf16[512,256]{1,0:T(8,128)(2,1)S(1)}, u32[]{:S(2)}, u32[]{:S(2)}) collective-permute-start(bf16[512,256]{1,0:T(8,128)(2,1)S(1)} %collective-permute-done.15.refs_4_), channel_id=1, source_target_pairs={{0,56},{8,0},{16,8},{24,16},{32,24},{40,32},{48,40},{56,48},{1,57}... | collective-permute-start | bytes 786440 | tf_op jit(solution)/shard_map/ppermute | solution.py:28
  84.3 9.5 %collective-permute-start.26 = (bf16[256,256]{1,0:T(8,128)(2,1)S(1)}, bf16[256,256]{1,0:T(8,128)(2,1)S(1)}, u32[]{:S(2)}, u32[]{:S(2)}) collective-permute-start(bf16[256,256]{1,0:T(8,128)(2,1)S(1)} %slice.92), channel_id=1, source_target_pairs={{0,8},{8,16},{16,24},{24,32},{32,40},{40,48},{48,56},{56,0},{1,9},... | collective-permute-start | bytes 393224 | tf_op jit(solution)/shard_map/ppermute | solution.py:28
  84.4 9.3 %collective-permute-start.27 = (bf16[256,256]{1,0:T(8,128)(2,1)S(1)}, bf16[256,256]{1,0:T(8,128)(2,1)S(1)}, u32[]{:S(2)}, u32[]{:S(2)}) collective-permute-start(bf16[256,256]{1,0:T(8,128)(2,1)S(1)} %slice.93), channel_id=1, source_target_pairs={{0,56},{8,0},{16,8},{24,16},{32,24},{40,32},{48,40},{56,48},{1,57}... | collective-permute-start | bytes 393224 | tf_op jit(solution)/shard_map/ppermute | solution.py:28
  100.0 15.1 %collective-permute-start.30 = (bf16[2080,128]{1,0:T(8,128)(2,1)S(1)}, bf16[2080,128]{1,0:T(8,128)(2,1)S(1)}, u32[]{:S(2)}, u32[]{:S(2)}) collective-permute-start(bf16[2080,128]{1,0:T(8,128)(2,1)S(1)} %attend.7), channel_id=1, source_target_pairs={{0,64},{64,128},{128,192},{192,0},{1,65},{65,129},{129,193},{193,1... | collective-permute-start | bytes 1597448 | tf_op jit(solution)/shard_map/ppermute | solution.py:28
  103.0 16.7 %collective-permute-start.29 = (bf16[2080,128]{1,0:T(8,128)(2,1)S(1)}, bf16[2080,128]{1,0:T(8,128)(2,1)S(1)}, u32[]{:S(2)}, u32[]{:S(2)}) collective-permute-start(bf16[2080,128]{1,0:T(8,128)(2,1)S(1)} %attend.6), channel_id=1, source_target_pairs={{0,128},{64,192},{128,0},{192,64},{1,129},{65,193},{129,1},{193,65... | collective-permute-start | bytes 1597448 | tf_op jit(solution)/shard_map/ppermute | solution.py:28
  108.1 20.1 %collective-permute-start.28 = (bf16[2080,128]{1,0:T(8,128)(2,1)S(1)}, bf16[2080,128]{1,0:T(8,128)(2,1)S(1)}, u32[]{:S(2)}, u32[]{:S(2)}) collective-permute-start(bf16[2080,128]{1,0:T(8,128)(2,1)S(1)} %attend.5), channel_id=1, source_target_pairs={{0,192},{64,0},{128,64},{192,128},{1,193},{65,1},{129,65},{193,129... | collective-permute-start | bytes 1597448 | tf_op jit(solution)/shard_map/ppermute | solution.py:28
  (15 other events, 103.3 us)
Sparse Core Ops, SparseCore 0:
  43.8 89.8 all-gather.1

commit v2 on v0

--- a/solution.py
+++ b/solution.py
@@ -39,49 +39,106 @@
     return out
 
 
-def project_kernel(layout, feature_ref, *refs):
-    pieces, (key_ref, value_ref) = refs[: -2 - PAIRS], refs[-2 - PAIRS : -PAIRS]
-    out_refs = refs[-PAIRS:]
-    key_sum = value_sum = squares = None
-    for block, members in enumerate(layout):
-        rows = [pieces[i][...] for i in members]
-        tokens = rows[0] if len(rows) == 1 else jnp.concatenate(rows, axis=0)
-        width = tokens.shape[1]
-        at = pl.ds(pl.multiple_of(feature_ref[block] * width, width), width)
-        k = jnp.dot(tokens, key_ref[at, :], preferred_element_type=jnp.float32)
-        v = jnp.dot(tokens, value_ref[at, :], preferred_element_type=jnp.float32)
-        f = tokens.astype(jnp.float32)
-        s = jnp.sum(f * f, axis=1, keepdims=True)
-        if key_sum is None:
-            key_sum, value_sum, squares = k, v, s
-        else:
-            key_sum, value_sum, squares = key_sum + k, value_sum + v, squares + s
-    inverse = lax.rsqrt(squares / key_ref.shape[0] + EPSILON)
-    keys = (key_sum * inverse).astype(jnp.bfloat16)
-    values = value_sum * inverse
-    for pair, out_ref in enumerate(out_refs):
+def add_block(sums, tokens, key_rows, value_rows):
+    f = tokens.astype(jnp.float32)
+    terms = (
+        jnp.dot(tokens, key_rows, preferred_element_type=jnp.float32),
+        jnp.dot(tokens, value_rows, preferred_element_type=jnp.float32),
+        jnp.sum(f * f, axis=1, keepdims=True),
+    )
+    return terms if sums is None else tuple(a + b for a, b in zip(sums, terms))
+
+
+def weight_copies(feature_ref, key_ref, value_ref, places, sems):
+    copies = []
+    for i, (key_place, value_place) in enumerate(places):
+        width = key_place.shape[0]
+        at = pl.ds(pl.multiple_of(feature_ref[i] * width, width), width)
+        copies.append(
+            [
+                pltpu.make_async_copy(key_ref.at[at], key_place, sems.at[2 * i]),
+                pltpu.make_async_copy(value_ref.at[at], value_place, sems.at[2 * i + 1]),
+            ]
+        )
+    for group in copies:
+        for copy in group:
+            copy.start()
+    return copies
+
+
+def early_kernel(feature_ref, *refs):
+    pieces, rest = refs[:-7], refs[-7:]
+    key_ref, value_ref, sum_ref, square_ref, late_ref, weights, sems = rest
+    places = [(weights.at[2 * i], weights.at[2 * i + 1]) for i in range(len(pieces))]
+    places += [(late_ref.at[2 * i], late_ref.at[2 * i + 1]) for i in range(late_ref.shape[0] // 2)]
+    copies = weight_copies(feature_ref, key_ref, value_ref, places, sems)
+    sums = None
+    for i, piece in enumerate(pieces):
+        for copy in copies[i]:
+            copy.wait()
+        sums = add_block(sums, piece[...], weights[2 * i], weights[2 * i + 1])
+    sum_ref[:, :WIDE] = sums[0]
+    sum_ref[:, WIDE:] = sums[1]
+    square_ref[...] = jnp.broadcast_to(sums[2], square_ref.shape)
+    for group in copies[len(pieces) :]:
+        for copy in group:
+            copy.wait()
+
+
+def late_kernel(depth, *refs):
+    *pieces, sum_ref, square_ref, weights, out_0, out_1 = refs
+    for pair, out_ref in enumerate((out_0, out_1)):
         rows = slice(pair * 2 * NLEN, (pair + 1) * 2 * NLEN)
-        out_ref[: 2 * NLEN, :] = keys[rows]
-        out_ref[2 * NLEN :, :] = values[rows].T.astype(jnp.bfloat16)
-
-
-def project(feature, blocks, key_weight, value_weight):
-    pieces, layout = [], []
-    for members in blocks:
-        layout.append(tuple(range(len(pieces), len(pieces) + len(members))))
-        pieces += members
+        sums = (sum_ref[rows, :WIDE], sum_ref[rows, WIDE:], square_ref[rows, :1])
+        for i in range(len(pieces) // PAIRS):
+            sums = add_block(
+                sums, pieces[i * PAIRS + pair][...], weights[2 * i], weights[2 * i + 1]
+            )
+        inverse = lax.rsqrt(sums[2] / depth + EPSILON)
+        out_ref[: 2 * NLEN, :] = (sums[0] * inverse).astype(jnp.bfloat16)
+        out_ref[2 * NLEN :, :] = (sums[1] * inverse).T.astype(jnp.bfloat16)
+
+
+def project_early(feature, pieces, key_weight, value_weight):
+    tokens, width = pieces[0].shape
+    blocks, count = feature.shape[0], len(pieces)
     vmem = pl.BlockSpec(memory_space=pltpu.VMEM)
     return pl.pallas_call(
-        functools.partial(project_kernel, tuple(layout)),
+        early_kernel,
+        out_shape=[
+            jax.ShapeDtypeStruct((tokens, 2 * WIDE), jnp.float32),
+            jax.ShapeDtypeStruct((tokens, HD), jnp.float32),
+            jax.ShapeDtypeStruct((2 * (blocks - count), width, WIDE), jnp.bfloat16),
+        ],
+        in_specs=[pl.BlockSpec(memory_space=pltpu.SMEM)]
+        + [vmem] * count
+        + [pl.BlockSpec(memory_space=pltpu.HBM)] * 2,
+        out_specs=[vmem] * 3,
+        scratch_shapes=[
+            pltpu.VMEM((2 * count, width, WIDE), jnp.bfloat16),
+            pltpu.SemaphoreType.DMA((2 * blocks,)),
+        ],
+        compiler_params=pltpu.CompilerParams(vmem_limit_bytes=VMEM_LIMIT),
+        cost_estimate=pl.CostEstimate(
+            flops=count * 512 * 512 * 1024, bytes_accessed=count << 20, transcendentals=0
+        ),
+        name="project_early",
+    )(feature, *pieces, key_weight, value_weight)
+
+
+def project_late(pieces, sums, depth):
+    vmem = pl.BlockSpec(memory_space=pltpu.VMEM)
+    return pl.pallas_call(
+        functools.partial(late_kernel, depth),
         out_shape=[jax.ShapeDtypeStruct((BLOCK, WIDE), jnp.bfloat16)] * PAIRS,
-        in_specs=[pl.BlockSpec(memory_space=pltpu.SMEM)] + [vmem] * (len(pieces) + 2),
+        in_specs=[vmem] * (len(pieces) + len(sums)),
         out_specs=[vmem] * PAIRS,
         compiler_params=pltpu.CompilerParams(vmem_limit_bytes=VMEM_LIMIT),
         cost_estimate=pl.CostEstimate(
-            flops=2 * 512 * 4096 * 512, bytes_accessed=8 << 20, transcendentals=0
-        ),
-        name="project",
-    )(feature, *pieces, key_weight, value_weight)
+            flops=2 * 512 * 512 * 1024, bytes_accessed=2 << 20, transcendentals=0
+        ),
+        name="project_late",
+    )(*pieces, *sums)
 
 
 def attend_kernel(places, place_ref, lane_ref, bias_ref, query_ref, *refs):
@@ -225,26 +282,33 @@
     y, z = lax.axis_index("y"), lax.axis_index("z")
     x, c = lax.axis_index("x"), lax.axis_index("c")
 
-    entry = (nbr_shard * ENTRIES + nbr_row).astype(jnp.bfloat16).reshape(1, -1)
-    entry = jnp.pad(entry, ((0, 15), (0, 2 * HD - entry.shape[1])))
-    packed = jnp.concatenate([queries, entry], axis=0)
-    asked = [packed] + [shift(packed, "y", k) for k in (1, 2, -1)]
-
-    feature = jnp.concatenate(
-        [
-            (((x + NX - jnp.arange(NX)) % NX) * NC + side).astype(jnp.int32)
-            for side in (c, 1 - c)
-        ]
-    )
-    own = ring_pieces(database.reshape(ENTRIES * NLEN, -1), "x")
-    other = [(k, r, shift(a, "c", 1)) for k, r, a in own]
-    blocks = [[a for k, _, a in side if k == d] for side in (own, other) for d in range(NX)]
-    rows = project(feature, blocks, key_weight, value_weight)
+    def feature(*offsets):
+        return jnp.stack(
+            [((x + NX - k) % NX) * NC + side for k in offsets for side in (c, 1 - c)]
+        ).astype(jnp.int32)
+
+    tokens = database.reshape(ENTRIES * NLEN, -1)
+    half = tokens.shape[0] // 2
+    up, down = shift(tokens, "x", 1), shift(tokens, "x", -1)
+    low, high = shift(up[:half], "x", 1), shift(down[half:], "x", -1)
+    early = [p for a in (tokens, up, down) for p in (a, shift(a, "c", 1))]
+    sums = project_early(feature(0, 1, 3, 2), early, key_weight, value_weight)
+    low, high, *sums = lax.optimization_barrier((low, high, *sums))
+    late = [low, high, shift(low, "c", 1), shift(high, "c", 1)]
+    rows = project_late(late, sums, key_weight.shape[0])
     table = [
         ((pair * NZ + k) * BLOCK + r, a)
         for pair in range(PAIRS)
         for k, r, a in ring_pieces(rows[pair], "z")
     ]
+
+    entry = (nbr_shard * ENTRIES + nbr_row).astype(jnp.bfloat16).reshape(1, -1)
+    entry = jnp.pad(entry, ((0, 15), (0, WIDE - entry.shape[1])))
+    packed = jnp.concatenate([queries, entry], axis=0)
+    asked = [packed]
+    for k, place in ((1, 1), (2, 2), (-1, 3)):
+        after, _ = lax.optimization_barrier((packed, table[place][1]))
+        asked.append(shift(after, "y", k))
 
     held_back, _ = lax.optimization_barrier((out_weight, rows[0]))
     weight = lax.all_gather(held_back, ("x", "c"), axis=0, tiled=True)

time: 156 us -> 150 us (0.962)
  waiting for transfers between devices: 45.7 us -> 37.9 us
  starting transfers between devices: 51.3 us -> 47.6 us
  Pallas kernels: 16.9 us -> 20.1 us
  blocking collectives: 9.95 us -> 11.6 us
    ppermute x31, waiting for transfers between devices: 45.7 us -> 37.9 us  [shift(): return lax.ppermute(a, axis, [(i, (i + k) % n) for i in range(n)])]
    ppermute x31, starting transfers between devices: 51.3 us -> 47.6 us  [shift(): return lax.ppermute(a, axis, [(i, (i + k) % n) for i in range(n)])]
    pallas_call x4, Pallas kernels: 11.3 us -> 14.6 us  [attend(): pl.pallas_call(functools.partial(attend_kernel, places), out_shape=jax.Sh...]
    unnamed x10 -> x2, local copies, waits for them, and re-layouts: 4.34 us -> 1.04 us
    all_to_all x1, blocking collectives: 9.95 us -> 11.6 us  [on_device(): lax.all_to_all(heads_out.reshape(NX * NC, SPAN, WIDE), ('x', 'c'), split_...]
    pallas_call x1 -> x2, Pallas kernels: 4.87 us -> 4.75 us  [the longest x1 3.93 us: project_early(): pl.pallas_call(early_kernel, out_shape=[jax.ShapeDtypeStruct((tokens, 2 *...]
  transfers between devices with their start and end apart: 32 -> 32, of which waited for: 13 -> 16; matrix products, arithmetic and copies ran while one was open for 2% -> 4% of each run, Pallas kernels for 8% -> 13%
where the time goes in v2:
time: 150 us; the launch traced here: 148 us
  starting transfers between devices  47.6 us (32%)
  waiting for transfers between devices  37.9 us (25%)
  Pallas kernels  20.1 us (13%)
  between operations  14.2 us (9%)
  blocking collectives  11.6 us (8%)
  matrix products  9.58 us (6%)
  local copies, waits for them, and re-layouts  4.12 us (3%)
  other arithmetic  2.48 us (2%)
    ppermute x31, starting transfers between devices, shift(): return lax.ppermute(a, axis, [(i, (i + k) % n) for i in range(n)])  47.6 us
    ppermute x31, waiting for transfers between devices, shift(): return lax.ppermute(a, axis, [(i, (i + k) % n) for i in range(n)])  37.9 us
    pallas_call x4, Pallas kernels, attend(): pl.pallas_call(functools.partial(attend_kernel, places), out_shape=jax.Sh...  14.6 us
    all_to_all x1, blocking collectives, on_device(): lax.all_to_all(heads_out.reshape(NX * NC, SPAN, WIDE), ('x', 'c'), split_...  11.6 us
    dot_general x1, matrix products, on_device(): jnp.dot(rows, weight, preferred_element_type=jnp.float32)  9.58 us
    pallas_call x1, Pallas kernels, project_early(): pl.pallas_call(early_kernel, out_shape=[jax.ShapeDtypeStruct((tokens, 2 *...  3.93 us
  transfers between devices with their start and end apart: 32, of which 16 were waited for; matrix products, arithmetic and copies ran while one was open for 4% of the time, Pallas kernels for 13%

profile of v2, /device:TPU:8, one launch (start us, length us, event | category | flops | bytes accessed | tf_op | source)
XLA Modules:
  0.0 147.6 jit_solution(13341995287027436130)
XLA Ops:
  9.8 11.8 %collective-permute-done.refs_2_ = bf16[512,512]{1,0:T(8,128)(2,1)S(1)} collective-permute-done((bf16[512,512]{1,0:T(8,128)(2,1)}, bf16[512,512]{1,0:T(8,128)(2,1)S(1)}, u32[]{:S(2)}, u32[]{:S(2)}) %collective-permute-start) | collective-permute-done | bytes 524320 | tf_op jit(solution)/shard_map/ppermute | solution.py:27
  23.9 2.3 %collective-permute-start.3 = (bf16[256,512]{1,0:T(8,128)(2,1)}, bf16[256,512]{1,0:T(8,128)(2,1)S(1)}, u32[]{:S(2)}, u32[]{:S(2)}) collective-permute-start(bf16[256,512]{1,0:T(8,128)(2,1)} %slice.86), channel_id=1, source_target_pairs={{0,6},{2,0},{4,2},{6,4},{1,7},{3,1},{5,3},{7,5},{8,14},{10,8},{12,... | collective-permute-start | bytes 786440 | tf_op jit(solution)/shard_map/ppermute | solution.py:27
  27.3 3.9 %project_early.1 = (f32[512,512]{1,0:T(8,128)S(1)}, f32[512,128]{1,0:T(8,128)S(1)}, bf16[4,512,256]{2,1,0:T(8,128)(2,1)S(1)}) custom-call(s32[8]{0:T(128)S(1)} %stack.38.feature_ref, bf16[512,512]{1,0:T(8,128)(2,1)S(1)} %bitcast.43, bf16[512,512]{1,0:T(8,128)(2,1)S(1)} %collective-permute-done.4.refs_1_, bf16[512,512]{1,0:T(8,128)(2,1)S(1)} %collective-permute-done.refs_2_, ...), custom_call_target="tpu_custom_call" | custom-call | flops 1610612736 | bytes 6291456 | tf_op jit(solution)/shard_map/project_early/pallas_call | solution.py:106
  35.3 2.0 %collective-permute-start.9 = (bf16[512,256]{1,0:T(8,128)(2,1)S(1)}, bf16[512,256]{1,0:T(8,128)(2,1)S(1)}, u32[]{:S(2)}, u32[]{:S(2)}) collective-permute-start(bf16[512,256]{1,0:T(8,128)(2,1)S(1)} %get-tuple-element.27.refs_0_), channel_id=1, source_target_pairs={{0,8},{8,16},{16,24},{24,32},{32,40},{40,48},{48,56},{56,0},{1,9},... | collective-permute-start | bytes 786440 | tf_op jit(solution)/shard_map/ppermute | solution.py:27
  37.3 4.0 %collective-permute-start.11 = (bf16[512,256]{1,0:T(8,128)(2,1)S(1)}, bf16[512,256]{1,0:T(8,128)(2,1)S(1)}, u32[]{:S(2)}, u32[]{:S(2)}) collective-permute-start(bf16[512,256]{1,0:T(8,128)(2,1)S(1)} %get-tuple-element.27.refs_0_), channel_id=1, source_target_pairs={{0,56},{8,0},{16,8},{24,16},{32,24},{40,32},{48,40},{56,48},{1,57}... | collective-permute-start | bytes 786440 | tf_op jit(solution)/shard_map/ppermute | solution.py:27
  41.4 3.2 %collective-permute-start.21 = (bf16[512,256]{1,0:T(8,128)(2,1)S(1)}, bf16[512,256]{1,0:T(8,128)(2,1)S(1)}, u32[]{:S(2)}, u32[]{:S(2)}) collective-permute-start(bf16[512,256]{1,0:T(8,128)(2,1)S(1)} %get-tuple-element.31.refs_9_), channel_id=1, source_target_pairs={{0,56},{8,0},{16,8},{24,16},{32,24},{40,32},{48,40},{56,48},{1,57}... | collective-permute-start | bytes 786440 | tf_op jit(solution)/shard_map/ppermute | solution.py:27
  44.6 3.8 %collective-permute-done.9.refs_1_ = bf16[512,256]{1,0:T(8,128)(2,1)S(1)} collective-permute-done((bf16[512,256]{1,0:T(8,128)(2,1)S(1)}, bf16[512,256]{1,0:T(8,128)(2,1)S(1)}, u32[]{:S(2)}, u32[]{:S(2)}) %collective-permute-start.9) | collective-permute-done | bytes 262176 | tf_op jit(solution)/shard_map/ppermute | solution.py:27
  54.0 2.7 %collective-permute-start.15 = (bf16[512,256]{1,0:T(8,128)(2,1)S(1)}, bf16[512,256]{1,0:T(8,128)(2,1)S(1)}, u32[]{:S(2)}, u32[]{:S(2)}) collective-permute-start(bf16[512,256]{1,0:T(8,128)(2,1)S(1)} %collective-permute-done.11.refs_2_), channel_id=1, source_target_pairs={{0,56},{8,0},{16,8},{24,16},{32,24},{40,32},{48,40},{56,48},{1,57}... | collective-permute-start | bytes 786440 | tf_op jit(solution)/shard_map/ppermute | solution.py:27
  56.7 2.9 %collective-permute-done.13.refs_3_ = bf16[512,256]{1,0:T(8,128)(2,1)S(1)} collective-permute-done((bf16[512,256]{1,0:T(8,128)(2,1)S(1)}, bf16[512,256]{1,0:T(8,128)(2,1)S(1)}, u32[]{:S(2)}, u32[]{:S(2)}) %collective-permute-start.13) | collective-permute-done | bytes 262176 | tf_op jit(solution)/shard_map/ppermute | solution.py:27
  59.6 2.1 %collective-permute-start.23 = (bf16[512,256]{1,0:T(8,128)(2,1)S(1)}, bf16[512,256]{1,0:T(8,128)(2,1)}, u32[]{:S(2)}, u32[]{:S(2)}) collective-permute-start(bf16[512,256]{1,0:T(8,128)(2,1)S(1)} %collective-permute-done.21.refs_11_), channel_id=1, source_target_pairs={{0,56},{8,0},{16,8},{24,16},{32,24},{40,32},{48,40},{56,48},{1,57}... | collective-permute-start | bytes 786440 | tf_op jit(solution)/shard_map/ppermute | solution.py:27
  61.7 3.8 %collective-permute-start.14 = (bf16[528,256]{1,0:T(8,128)(2,1)}, bf16[528,256]{1,0:T(8,128)(2,1)}, u32[]{:S(2)}, u32[]{:S(2)}) collective-permute-start(bf16[528,256]{1,0:T(8,128)(2,1)} %fusion.1.query_ref), channel_id=1, source_target_pairs={{0,192},{64,0},{128,64},{192,128},{1,193},{65,1},{129,65},{193,129... | collective-permute-start | bytes 811016 | tf_op jit(solution)/shard_map/ppermute | solution.py:27
  67.2 3.0 %collective-permute-start.17 = (bf16[512,256]{1,0:T(8,128)(2,1)S(1)}, bf16[512,256]{1,0:T(8,128)(2,1)S(1)}, u32[]{:S(2)}, u32[]{:S(2)}) collective-permute-start(bf16[512,256]{1,0:T(8,128)(2,1)S(1)} %collective-permute-done.15.refs_4_), channel_id=1, source_target_pairs={{0,56},{8,0},{16,8},{24,16},{32,24},{40,32},{48,40},{56,48},{1,57}... | collective-permute-start | bytes 786440 | tf_op jit(solution)/shard_map/ppermute | solution.py:27
  70.2 3.2 %collective-permute-start.25 = (bf16[512,256]{1,0:T(8,128)(2,1)}, bf16[512,256]{1,0:T(8,128)(2,1)S(1)}, u32[]{:S(2)}, u32[]{:S(2)}) collective-permute-start(bf16[512,256]{1,0:T(8,128)(2,1)} %collective-permute-done.23.refs_13_), channel_id=1, source_target_pairs={{0,56},{8,0},{16,8},{24,16},{32,24},{40,32},{48,40},{56,48},{1,57}... | collective-permute-start | bytes 786440 | tf_op jit(solution)/shard_map/ppermute | solution.py:27
  76.9 3.8 %collective-permute-start.19 = (bf16[256,256]{1,0:T(8,128)(2,1)S(1)}, bf16[256,256]{1,0:T(8,128)(2,1)S(1)}, u32[]{:S(2)}, u32[]{:S(2)}) collective-permute-start(bf16[256,256]{1,0:T(8,128)(2,1)S(1)} %slice.91), channel_id=1, source_target_pairs={{0,56},{8,0},{16,8},{24,16},{32,24},{40,32},{48,40},{56,48},{1,57}... | collective-permute-start | bytes 393224 | tf_op jit(solution)/shard_map/ppermute | solution.py:27
  81.2 3.7 %collective-permute-start.27 = (bf16[256,256]{1,0:T(8,128)(2,1)S(1)}, bf16[256,256]{1,0:T(8,128)(2,1)S(1)}, u32[]{:S(2)}, u32[]{:S(2)}) collective-permute-start(bf16[256,256]{1,0:T(8,128)(2,1)S(1)} %slice.93), channel_id=1, source_target_pairs={{0,56},{8,0},{16,8},{24,16},{32,24},{40,32},{48,40},{56,48},{1,57}... | collective-permute-start | bytes 393224 | tf_op jit(solution)/shard_map/ppermute | solution.py:27
  87.4 3.7 %attend.7 = bf16[2080,128]{1,0:T(8,128)(2,1)S(1)} custom-call(s32[16]{0:T(128)S(1)} %get-tuple-element.50.place_ref, s32[16]{0:T(128)S(1)} %get-tuple-element.37.lane_ref, f32[16]{0:T(128)S(1)} %get-tuple-element.33.bias_ref, bf16[528,256]{1,0:T(8,128)(2,1)} %collective-permute-done.14.query_ref, bf16[512,256]{1,0:T(8,128)(2,1)S(1)} %get-tuple-element.27.refs_0_, ...), custom_call_target="tpu_custom_call" | custom-call | flops 536870912 | bytes 6291456 | tf_op jit(solution)/shard_map/attend/pallas_call | solution.py:214
  92.5 3.7 %attend.6 = bf16[2080,128]{1,0:T(8,128)(2,1)S(1)} custom-call(s32[16]{0:T(128)S(1)} %get-tuple-element.49.place_ref, s32[16]{0:T(128)S(1)} %get-tuple-element.38.lane_ref, f32[16]{0:T(128)S(1)} %get-tuple-element.34.bias_ref, bf16[528,256]{1,0:T(8,128)(2,1)} %collective-permute-done.12.query_ref, bf16[512,256]{1,0:T(8,128)(2,1)S(1)} %get-tuple-element.27.refs_0_, ...), custom_call_target="tpu_custom_call" | custom-call | flops 536870912 | bytes 6291456 | tf_op jit(solution)/shard_map/attend/pallas_call | solution.py:214
  96.2 3.5 %collective-permute-start.29 = (bf16[2080,128]{1,0:T(8,128)(2,1)S(1)}, bf16[2080,128]{1,0:T(8,128)(2,1)S(1)}, u32[]{:S(2)}, u32[]{:S(2)}) collective-permute-start(bf16[2080,128]{1,0:T(8,128)(2,1)S(1)} %attend.6), channel_id=1, source_target_pairs={{0,128},{64,192},{128,0},{192,64},{1,129},{65,193},{129,1},{193,65... | collective-permute-start | bytes 1597448 | tf_op jit(solution)/shard_map/ppermute | solution.py:27
  99.6 3.7 %attend.5 = bf16[2080,128]{1,0:T(8,128)(2,1)S(1)} custom-call(s32[16]{0:T(128)S(1)} %get-tuple-element.48.place_ref, s32[16]{0:T(128)S(1)} %get-tuple-element.39.lane_ref, f32[16]{0:T(128)S(1)} %get-tuple-element.35.bias_ref, bf16[528,256]{1,0:T(8,128)(2,1)} %collective-permute-done.10.query_ref, bf16[512,256]{1,0:T(8,128)(2,1)S(1)} %get-tuple-element.27.refs_0_, ...), custom_call_target="tpu_custom_call" | custom-call | flops 536870912 | bytes 6291456 | tf_op jit(solution)/shard_map/attend/pallas_call | solution.py:214
  104.8 3.7 %attend.4.refs_0_ = bf16[2080,128]{1,0:T(8,128)(2,1)S(1)} custom-call(s32[16]{0:T(128)S(1)} %get-tuple-element.47.place_ref, s32[16]{0:T(128)S(1)} %get-tuple-element.40.lane_ref, f32[16]{0:T(128)S(1)} %get-tuple-element.36.bias_ref, bf16[528,256]{1,0:T(8,128)(2,1)} %fusion.1.query_ref, bf16[512,256]{1,0:T(8,128)(2,1)S(1)} %get-tuple-element.27.refs_0_, ...), custom_call_target="tpu_custom_call" | custom-call | flops 536870912 | bytes 6291456 | tf_op jit(solution)/shard_map/attend/pallas_call | solution.py:214
  108.5 4.3 %collective-permute-done.29.refs_2_ = bf16[2080,128]{1,0:T(8,128)(2,1)S(1)} collective-permute-done((bf16[2080,128]{1,0:T(8,128)(2,1)S(1)}, bf16[2080,128]{1,0:T(8,128)(2,1)S(1)}, u32[]{:S(2)}, u32[]{:S(2)}) %collective-permute-start.29) | collective-permute-done | bytes 532512 | tf_op jit(solution)/shard_map/ppermute | solution.py:27
  112.8 6.0 %collective-permute-done.28.refs_1_ = bf16[2080,128]{1,0:T(8,128)(2,1)S(1)} collective-permute-done((bf16[2080,128]{1,0:T(8,128)(2,1)S(1)}, bf16[2080,128]{1,0:T(8,128)(2,1)S(1)}, u32[]{:S(2)}, u32[]{:S(2)}) %collective-permute-start.28) | collective-permute-done | bytes 532512 | tf_op jit(solution)/shard_map/ppermute | solution.py:27
  119.5 11.6 %all_to_all.5 = bf16[8,64,256]{2,1,0:T(8,128)(2,1)S(1)} all-to-all(bf16[8,64,256]{2,1,0:T(8,128)(2,1)S(1)} %bitcast.39), channel_id=1, replica_groups=mesh['y'=4,'z'=8,'x'=4,'c'=2] {'x','c'}, dimensions={0} | all-to-all | bytes 524288 | tf_op jit(solution)/shard_map/all_to_all | solution.py:327
  131.2 9.6 %convolution_convert_fusion = bf16[64,4096]{1,0:T(8,128)(2,1)} fusion(bf16[64,2048]{1,0:T(8,128)(2,1)S(1)} %bitcast.44, bf16[2048,4096]{1,0:T(8,128)(2,1)} %all-gather.2.cloned.1.call-done), kind=kOutput, calls=%fused_computation | convolution fusion | flops 1074003968 | bytes 17563648 | tf_op jit(solution)/shard_map/dot_general | solution.py:331
  (71 shorter events, 27.6 us)
Async XLA Ops:
  6.5 124.6 %all-gather.2.cloned.1.call-start = ((), (), s32[]{:S(2)}) async-start(), calls=%async_computation.1 | async-start | bytes 18874368 | tf_op jit(solution)/shard_map/all_gather | solution.py:314
  6.5 15.1 %collective-permute-start = (bf16[512,512]{1,0:T(8,128)(2,1)}, bf16[512,512]{1,0:T(8,128)(2,1)S(1)}, u32[]{:S(2)}, u32[]{:S(2)}) collective-permute-start(bf16[512,512]{1,0:T(8,128)(2,1)} %bitcast.40), channel_id=1, source_target_pairs={{0,2},{2,4},{4,6},{6,0},{1,3},{3,5},{5,7},{7,1},{8,10},{10,12},{12... | collective-permute-start | bytes 1572872 | tf_op jit(solution)/shard_map/ppermute | solution.py:27
  8.0 13.6 %collective-permute-start.2 = (bf16[512,512]{1,0:T(8,128)(2,1)}, bf16[512,512]{1,0:T(8,128)(2,1)S(1)}, u32[]{:S(2)}, u32[]{:S(2)}) collective-permute-start(bf16[512,512]{1,0:T(8,128)(2,1)} %bitcast.41), channel_id=1, source_target_pairs={{0,6},{2,0},{4,2},{6,4},{1,7},{3,1},{5,3},{7,5},{8,14},{10,8},{12,... | collective-permute-start | bytes 1572872 | tf_op jit(solution)/shard_map/ppermute | solution.py:27
  9.8 16.5 %collective-permute-start.4 = (bf16[512,512]{1,0:T(8,128)(2,1)}, bf16[512,512]{1,0:T(8,128)(2,1)S(1)}, u32[]{:S(2)}, u32[]{:S(2)}) collective-permute-start(bf16[512,512]{1,0:T(8,128)(2,1)} %bitcast.42), channel_id=1, source_target_pairs={{0,1},{1,0},{2,3},{3,2},{4,5},{5,4},{6,7},{7,6},{8,9},{9,8},{10,11... | collective-permute-start | bytes 1572872 | tf_op jit(solution)/shard_map/ppermute | solution.py:27
  22.2 9.5 %collective-permute-start.1 = (bf16[256,512]{1,0:T(8,128)(2,1)S(1)}, bf16[256,512]{1,0:T(8,128)(2,1)S(1)}, u32[]{:S(2)}, u32[]{:S(2)}) collective-permute-start(bf16[256,512]{1,0:T(8,128)(2,1)S(1)} %slice.85), channel_id=1, source_target_pairs={{0,2},{2,4},{4,6},{6,0},{1,3},{3,5},{5,7},{7,1},{8,10},{10,12},{12... | collective-permute-start | bytes 786440 | tf_op jit(solution)/shard_map/ppermute | solution.py:27
  23.9 8.6 %collective-permute-start.3 = (bf16[256,512]{1,0:T(8,128)(2,1)}, bf16[256,512]{1,0:T(8,128)(2,1)S(1)}, u32[]{:S(2)}, u32[]{:S(2)}) collective-permute-start(bf16[256,512]{1,0:T(8,128)(2,1)} %slice.86), channel_id=1, source_target_pairs={{0,6},{2,0},{4,2},{6,4},{1,7},{3,1},{5,3},{7,5},{8,14},{10,8},{12,... | collective-permute-start | bytes 786440 | tf_op jit(solution)/shard_map/ppermute | solution.py:27
  35.3 13.0 %collective-permute-start.9 = (bf16[512,256]{1,0:T(8,128)(2,1)S(1)}, bf16[512,256]{1,0:T(8,128)(2,1)S(1)}, u32[]{:S(2)}, u32[]{:S(2)}) collective-permute-start(bf16[512,256]{1,0:T(8,128)(2,1)S(1)} %get-tuple-element.27.refs_0_), channel_id=1, source_target_pairs={{0,8},{8,16},{16,24},{24,32},{32,40},{40,48},{48,56},{56,0},{1,9},... | collective-permute-start | bytes 786440 | tf_op jit(solution)/shard_map/ppermute | solution.py:27
  37.3 15.2 %collective-permute-start.11 = (bf16[512,256]{1,0:T(8,128)(2,1)S(1)}, bf16[512,256]{1,0:T(8,128)(2,1)S(1)}, u32[]{:S(2)}, u32[]{:S(2)}) collective-permute-start(bf16[512,256]{1,0:T(8,128)(2,1)S(1)} %get-tuple-element.27.refs_0_), channel_id=1, source_target_pairs={{0,56},{8,0},{16,8},{24,16},{32,24},{40,32},{48,40},{56,48},{1,57}... | collective-permute-start | bytes 786440 | tf_op jit(solution)/shard_map/ppermute | solution.py:27
  41.4 12.6 %collective-permute-start.20 = (bf16[512,256]{1,0:T(8,128)(2,1)S(1)}, bf16[512,256]{1,0:T(8,128)(2,1)S(1)}, u32[]{:S(2)}, u32[]{:S(2)}) collective-permute-start(bf16[512,256]{1,0:T(8,128)(2,1)S(1)} %get-tuple-element.31.refs_9_), channel_id=1, source_target_pairs={{0,8},{8,16},{16,24},{24,32},{32,40},{40,48},{48,56},{56,0},{1,9},... | collective-permute-start | bytes 786440 | tf_op jit(solution)/shard_map/ppermute | solution.py:27
  41.4 15.4 %collective-permute-start.21 = (bf16[512,256]{1,0:T(8,128)(2,1)S(1)}, bf16[512,256]{1,0:T(8,128)(2,1)S(1)}, u32[]{:S(2)}, u32[]{:S(2)}) collective-permute-start(bf16[512,256]{1,0:T(8,128)(2,1)S(1)} %get-tuple-element.31.refs_9_), channel_id=1, source_target_pairs={{0,56},{8,0},{16,8},{24,16},{32,24},{40,32},{48,40},{56,48},{1,57}... | collective-permute-start | bytes 786440 | tf_op jit(solution)/shard_map/ppermute | solution.py:27
  48.4 11.2 %collective-permute-start.13 = (bf16[512,256]{1,0:T(8,128)(2,1)S(1)}, bf16[512,256]{1,0:T(8,128)(2,1)S(1)}, u32[]{:S(2)}, u32[]{:S(2)}) collective-permute-start(bf16[512,256]{1,0:T(8,128)(2,1)S(1)} %collective-permute-done.9.refs_1_), channel_id=1, source_target_pairs={{0,8},{8,16},{16,24},{24,32},{32,40},{40,48},{48,56},{56,0},{1,9},... | collective-permute-start | bytes 786440 | tf_op jit(solution)/shard_map/ppermute | solution.py:27
  51.0 19.2 %collective-permute-start.10 = (bf16[528,256]{1,0:T(8,128)(2,1)}, bf16[528,256]{1,0:T(8,128)(2,1)}, u32[]{:S(2)}, u32[]{:S(2)}) collective-permute-start(bf16[528,256]{1,0:T(8,128)(2,1)} %fusion.1.query_ref), channel_id=1, source_target_pairs={{0,64},{64,128},{128,192},{192,0},{1,65},{65,129},{129,193},{193,1... | collective-permute-start | bytes 811016 | tf_op jit(solution)/shard_map/ppermute | solution.py:27
  52.6 17.7 %collective-permute-start.12 = (bf16[528,256]{1,0:T(8,128)(2,1)}, bf16[528,256]{1,0:T(8,128)(2,1)}, u32[]{:S(2)}, u32[]{:S(2)}) collective-permute-start(bf16[528,256]{1,0:T(8,128)(2,1)} %fusion.1.query_ref), channel_id=1, source_target_pairs={{0,128},{64,192},{128,0},{192,64},{1,129},{65,193},{129,1},{193,65... | collective-permute-start | bytes 811016 | tf_op jit(solution)/shard_map/ppermute | solution.py:27
  56.7 8.7 %collective-permute-start.22 = (bf16[512,256]{1,0:T(8,128)(2,1)S(1)}, bf16[512,256]{1,0:T(8,128)(2,1)S(1)}, u32[]{:S(2)}, u32[]{:S(2)}) collective-permute-start(bf16[512,256]{1,0:T(8,128)(2,1)S(1)} %collective-permute-done.20.refs_10_), channel_id=1, source_target_pairs={{0,8},{8,16},{16,24},{24,32},{32,40},{40,48},{48,56},{56,0},{1,9},... | collective-permute-start | bytes 786440 | tf_op jit(solution)/shard_map/ppermute | solution.py:27
  61.7 23.3 %collective-permute-start.14 = (bf16[528,256]{1,0:T(8,128)(2,1)}, bf16[528,256]{1,0:T(8,128)(2,1)}, u32[]{:S(2)}, u32[]{:S(2)}) collective-permute-start(bf16[528,256]{1,0:T(8,128)(2,1)} %fusion.1.query_ref), channel_id=1, source_target_pairs={{0,192},{64,0},{128,64},{192,128},{1,193},{65,1},{129,65},{193,129... | collective-permute-start | bytes 811016 | tf_op jit(solution)/shard_map/ppermute | solution.py:27
  65.5 9.7 %collective-permute-start.16 = (bf16[512,256]{1,0:T(8,128)(2,1)S(1)}, bf16[512,256]{1,0:T(8,128)(2,1)S(1)}, u32[]{:S(2)}, u32[]{:S(2)}) collective-permute-start(bf16[512,256]{1,0:T(8,128)(2,1)S(1)} %collective-permute-done.13.refs_3_), channel_id=1, source_target_pairs={{0,8},{8,16},{16,24},{24,32},{32,40},{40,48},{48,56},{56,0},{1,9},... | collective-permute-start | bytes 786440 | tf_op jit(solution)/shard_map/ppermute | solution.py:27
  67.2 9.7 %collective-permute-start.17 = (bf16[512,256]{1,0:T(8,128)(2,1)S(1)}, bf16[512,256]{1,0:T(8,128)(2,1)S(1)}, u32[]{:S(2)}, u32[]{:S(2)}) collective-permute-start(bf16[512,256]{1,0:T(8,128)(2,1)S(1)} %collective-permute-done.15.refs_4_), channel_id=1, source_target_pairs={{0,56},{8,0},{16,8},{24,16},{32,24},{40,32},{48,40},{56,48},{1,57}... | collective-permute-start | bytes 786440 | tf_op jit(solution)/shard_map/ppermute | solution.py:27
  70.2 10.5 %collective-permute-start.24 = (bf16[512,256]{1,0:T(8,128)(2,1)S(1)}, bf16[512,256]{1,0:T(8,128)(2,1)S(1)}, u32[]{:S(2)}, u32[]{:S(2)}) collective-permute-start(bf16[512,256]{1,0:T(8,128)(2,1)S(1)} %collective-permute-done.22.refs_12_), channel_id=1, source_target_pairs={{0,8},{8,16},{16,24},{24,32},{32,40},{40,48},{48,56},{56,0},{1,9},... | collective-permute-start | bytes 786440 | tf_op jit(solution)/shard_map/ppermute | solution.py:27
  70.2 11.0 %collective-permute-start.25 = (bf16[512,256]{1,0:T(8,128)(2,1)}, bf16[512,256]{1,0:T(8,128)(2,1)S(1)}, u32[]{:S(2)}, u32[]{:S(2)}) collective-permute-start(bf16[512,256]{1,0:T(8,128)(2,1)} %collective-permute-done.23.refs_13_), channel_id=1, source_target_pairs={{0,56},{8,0},{16,8},{24,16},{32,24},{40,32},{48,40},{56,48},{1,57}... | collective-permute-start | bytes 786440 | tf_op jit(solution)/shard_map/ppermute | solution.py:27
  75.2 10.5 %collective-permute-start.18 = (bf16[256,256]{1,0:T(8,128)(2,1)S(1)}, bf16[256,256]{1,0:T(8,128)(2,1)S(1)}, u32[]{:S(2)}, u32[]{:S(2)}) collective-permute-start(bf16[256,256]{1,0:T(8,128)(2,1)S(1)} %slice.90), channel_id=1, source_target_pairs={{0,8},{8,16},{16,24},{24,32},{32,40},{40,48},{48,56},{56,0},{1,9},... | collective-permute-start | bytes 393224 | tf_op jit(solution)/shard_map/ppermute | solution.py:27
  76.9 8.8 %collective-permute-start.19 = (bf16[256,256]{1,0:T(8,128)(2,1)S(1)}, bf16[256,256]{1,0:T(8,128)(2,1)S(1)}, u32[]{:S(2)}, u32[]{:S(2)}) collective-permute-start(bf16[256,256]{1,0:T(8,128)(2,1)S(1)} %slice.91), channel_id=1, source_target_pairs={{0,56},{8,0},{16,8},{24,16},{32,24},{40,32},{48,40},{56,48},{1,57}... | collective-permute-start | bytes 393224 | tf_op jit(solution)/shard_map/ppermute | solution.py:27
  91.1 17.4 %collective-permute-start.30 = (bf16[2080,128]{1,0:T(8,128)(2,1)S(1)}, bf16[2080,128]{1,0:T(8,128)(2,1)S(1)}, u32[]{:S(2)}, u32[]{:S(2)}) collective-permute-start(bf16[2080,128]{1,0:T(8,128)(2,1)S(1)} %attend.7), channel_id=1, source_target_pairs={{0,64},{64,128},{128,192},{192,0},{1,65},{65,129},{129,193},{193,1... | collective-permute-start | bytes 1597448 | tf_op jit(solution)/shard_map/ppermute | solution.py:27
  96.2 16.6 %collective-permute-start.29 = (bf16[2080,128]{1,0:T(8,128)(2,1)S(1)}, bf16[2080,128]{1,0:T(8,128)(2,1)S(1)}, u32[]{:S(2)}, u32[]{:S(2)}) collective-permute-start(bf16[2080,128]{1,0:T(8,128)(2,1)S(1)} %attend.6), channel_id=1, source_target_pairs={{0,128},{64,192},{128,0},{192,64},{1,129},{65,193},{129,1},{193,65... | collective-permute-start | bytes 1597448 | tf_op jit(solution)/shard_map/ppermute | solution.py:27
  103.3 15.5 %collective-permute-start.28 = (bf16[2080,128]{1,0:T(8,128)(2,1)S(1)}, bf16[2080,128]{1,0:T(8,128)(2,1)S(1)}, u32[]{:S(2)}, u32[]{:S(2)}) collective-permute-start(bf16[2080,128]{1,0:T(8,128)(2,1)S(1)} %attend.5), channel_id=1, source_target_pairs={{0,192},{64,0},{128,64},{192,128},{1,193},{65,1},{129,65},{193,129... | collective-permute-start | bytes 1597448 | tf_op jit(solution)/shard_map/ppermute | solution.py:27
  (9 other events, 41.5 us)
Sparse Core Ops, SparseCore 0:
  35.5 90.2 all-gather.1

commit v3 on v2

--- a/solution.py
+++ b/solution.py
@@ -287,9 +287,15 @@
             [((x + NX - k) % NX) * NC + side for k in offsets for side in (c, 1 - c)]
         ).astype(jnp.int32)
 
+    entry = (nbr_shard * ENTRIES + nbr_row).astype(jnp.bfloat16).reshape(1, -1)
+    entry = jnp.pad(entry, ((0, 15), (0, WIDE - entry.shape[1])))
+    packed = jnp.concatenate([queries, entry], axis=0)
+
     tokens = database.reshape(ENTRIES * NLEN, -1)
     half = tokens.shape[0] // 2
     up, down = shift(tokens, "x", 1), shift(tokens, "x", -1)
+    above, below = shift(packed, "y", 1), shift(packed, "y", -1)
+    above, below, packed, up, down = lax.optimization_barrier((above, below, packed, up, down))
     low, high = shift(up[:half], "x", 1), shift(down[half:], "x", -1)
     early = [p for a in (tokens, up, down) for p in (a, shift(a, "c", 1))]
     sums = project_early(feature(0, 1, 3, 2), early, key_weight, value_weight)
@@ -302,13 +308,8 @@
         for k, r, a in ring_pieces(rows[pair], "z")
     ]
 
-    entry = (nbr_shard * ENTRIES + nbr_row).astype(jnp.bfloat16).reshape(1, -1)
-    entry = jnp.pad(entry, ((0, 15), (0, WIDE - entry.shape[1])))
-    packed = jnp.concatenate([queries, entry], axis=0)
-    asked = [packed]
-    for k, place in ((1, 1), (2, 2), (-1, 3)):
-        after, _ = lax.optimization_barrier((packed, table[place][1]))
-        asked.append(shift(after, "y", k))
+    after, _ = lax.optimization_barrier((packed, table[3][1]))
+    asked = [packed, above, shift(after, "y", 2), below]
 
     held_back, _ = lax.optimization_barrier((out_weight, rows[0]))
     weight = lax.all_gather(held_back, ("x", "c"), axis=0, tiled=True)

time: 150 us -> 147 us (0.980); the launches traced: 148 us -> 147 us
  local copies, waits for them, and re-layouts: 4.12 us -> 7.3 us
  starting transfers between devices: 47.6 us -> 45.6 us
    unnamed x2 -> x10, local copies, waits for them, and re-layouts: 1.04 us -> 3.52 us
    ppermute x31, starting transfers between devices: 47.6 us -> 45.6 us  [shift(): return lax.ppermute(a, axis, [(i, (i + k) % n) for i in range(n)])]
  transfers between devices with their start and end apart: 32 -> 32, of which waited for: 16 -> 14; matrix products, arithmetic and copies ran while one was open for 4% -> 4% of each run, Pallas kernels for 13% -> 13%
where the time goes in v3:
time: 147 us
  starting transfers between devices  45.6 us (31%)
  waiting for transfers between devices  36.6 us (25%)
  Pallas kernels  19.5 us (13%)
  between operations  14.3 us (10%)
  blocking collectives  11.4 us (8%)
  matrix products  9.59 us (7%)
  local copies, waits for them, and re-layouts  7.3 us (5%)
  other arithmetic  2.45 us (2%)
    ppermute x31, starting transfers between devices, shift(): return lax.ppermute(a, axis, [(i, (i + k) % n) for i in range(n)])  45.6 us
    ppermute x31, waiting for transfers between devices, shift(): return lax.ppermute(a, axis, [(i, (i + k) % n) for i in range(n)])  36.6 us
    pallas_call x4, Pallas kernels, attend(): pl.pallas_call(functools.partial(attend_kernel, places), out_shape=jax.Sh...  14 us
    all_to_all x1, blocking collectives, on_device(): lax.all_to_all(heads_out.reshape(NX * NC, SPAN, WIDE), ('x', 'c'), split_...  11.4 us
    dot_general x1, matrix products, on_device(): jnp.dot(rows, weight, preferred_element_type=jnp.float32)  9.59 us
    pallas_call x1, Pallas kernels, project_early(): pl.pallas_call(early_kernel, out_shape=[jax.ShapeDtypeStruct((tokens, 2 *...  3.94 us
    unnamed x10, local copies, waits for them, and re-layouts  3.52 us
  transfers between devices with their start and end apart: 32, of which 14 were waited for; matrix products, arithmetic and copies ran while one was open for 4% of the time, Pallas kernels for 13%

profile of v3, /device:TPU:8, one launch (start us, length us, event | category | flops | bytes accessed | tf_op | source)
XLA Modules:
  0.0 146.6 jit_solution(16854844855847916769)
XLA Ops:
  14.5 5.7 %collective-permute-done.query_ref = bf16[528,256]{1,0:T(8,128)(2,1)S(1)} collective-permute-done((bf16[528,256]{1,0:T(8,128)(2,1)}, bf16[528,256]{1,0:T(8,128)(2,1)S(1)}, u32[]{:S(2)}, u32[]{:S(2)}) %collective-permute-start) | collective-permute-done | bytes 270368 | tf_op jit(solution)/shard_map/ppermute | solution.py:27
  27.4 3.9 %project_early.1 = (f32[512,512]{1,0:T(8,128)S(1)}, f32[512,128]{1,0:T(8,128)S(1)}, bf16[4,512,256]{2,1,0:T(8,128)(2,1)S(1)}) custom-call(s32[8]{0:T(128)S(1)} %stack.38.feature_ref, bf16[512,512]{1,0:T(8,128)(2,1)S(1)} %bitcast.43, bf16[512,512]{1,0:T(8,128)(2,1)S(1)} %collective-permute-done.6.refs_1_, ...), custom_call_target="tpu_custom_call" | custom-call | flops 1610612736 | bytes 6291456 | tf_op jit(solution)/shard_map/project_early/pallas_call | solution.py:106
  38.0 4.0 %collective-permute-start.14 = (bf16[512,256]{1,0:T(8,128)(2,1)S(1)}, bf16[512,256]{1,0:T(8,128)(2,1)S(1)}, u32[]{:S(2)}, u32[]{:S(2)}) collective-permute-start(bf16[512,256]{1,0:T(8,128)(2,1)S(1)} %get-tuple-element.34.refs_0_), channel_id=1, source_target_pairs={{0,56},{8,0},{16,8},{24,16},{32,24},{40,32},{48,40},{56,48},{1,57}... | collective-permute-start | bytes 786440 | tf_op jit(solution)/shard_map/ppermute | solution.py:27
  42.0 3.2 %collective-permute-start.21 = (bf16[512,256]{1,0:T(8,128)(2,1)S(1)}, bf16[512,256]{1,0:T(8,128)(2,1)S(1)}, u32[]{:S(2)}, u32[]{:S(2)}) collective-permute-start(bf16[512,256]{1,0:T(8,128)(2,1)S(1)} %get-tuple-element.37.refs_9_), channel_id=1, source_target_pairs={{0,56},{8,0},{16,8},{24,16},{32,24},{40,32},{48,40},{56,48},{1,57}... | collective-permute-start | bytes 786440 | tf_op jit(solution)/shard_map/ppermute | solution.py:27
  45.2 3.8 %collective-permute-done.11.refs_1_ = bf16[512,256]{1,0:T(8,128)(2,1)S(1)} collective-permute-done((bf16[512,256]{1,0:T(8,128)(2,1)S(1)}, bf16[512,256]{1,0:T(8,128)(2,1)S(1)}, u32[]{:S(2)}, u32[]{:S(2)}) %collective-permute-start.11) | collective-permute-done | bytes 262176 | tf_op jit(solution)/shard_map/ppermute | solution.py:27
  49.0 3.4 %collective-permute-start.15 = (bf16[512,256]{1,0:T(8,128)(2,1)S(1)}, bf16[512,256]{1,0:T(8,128)(2,1)S(1)}, u32[]{:S(2)}, u32[]{:S(2)}) collective-permute-start(bf16[512,256]{1,0:T(8,128)(2,1)S(1)} %collective-permute-done.14.refs_2_), channel_id=1, source_target_pairs={{0,56},{8,0},{16,8},{24,16},{32,24},{40,32},{48,40},{56,48},{1,57}... | collective-permute-start | bytes 786440 | tf_op jit(solution)/shard_map/ppermute | solution.py:27
  52.3 2.3 %collective-permute-done.20.refs_10_ = bf16[512,256]{1,0:T(8,128)(2,1)S(1)} collective-permute-done((bf16[512,256]{1,0:T(8,128)(2,1)S(1)}, bf16[512,256]{1,0:T(8,128)(2,1)S(1)}, u32[]{:S(2)}, u32[]{:S(2)}) %collective-permute-start.20) | collective-permute-done | bytes 262176 | tf_op jit(solution)/shard_map/ppermute | solution.py:27
  54.6 3.4 %collective-permute-start.23 = (bf16[512,256]{1,0:T(8,128)(2,1)S(1)}, bf16[512,256]{1,0:T(8,128)(2,1)}, u32[]{:S(2)}, u32[]{:S(2)}) collective-permute-start(bf16[512,256]{1,0:T(8,128)(2,1)S(1)} %collective-permute-done.21.refs_11_), channel_id=1, source_target_pairs={{0,56},{8,0},{16,8},{24,16},{32,24},{40,32},{48,40},{56,48},{1,57}... | collective-permute-start | bytes 786440 | tf_op jit(solution)/shard_map/ppermute | solution.py:27
  58.0 2.3 %collective-permute-done.12.refs_3_ = bf16[512,256]{1,0:T(8,128)(2,1)S(1)} collective-permute-done((bf16[512,256]{1,0:T(8,128)(2,1)S(1)}, bf16[512,256]{1,0:T(8,128)(2,1)S(1)}, u32[]{:S(2)}, u32[]{:S(2)}) %collective-permute-start.12) | collective-permute-done | bytes 262176 | tf_op jit(solution)/shard_map/ppermute | solution.py:27
  60.2 2.2 %collective-permute-start.13 = (bf16[528,256]{1,0:T(8,128)(2,1)}, bf16[528,256]{1,0:T(8,128)(2,1)}, u32[]{:S(2)}, u32[]{:S(2)}) collective-permute-start(bf16[528,256]{1,0:T(8,128)(2,1)} %fusion.1.query_ref), channel_id=1, source_target_pairs={{0,128},{64,192},{128,0},{192,64},{1,129},{65,193},{129,1},{193,65... | collective-permute-start | bytes 811016 | tf_op jit(solution)/shard_map/ppermute | solution.py:27
  62.4 3.2 %collective-permute-start.17 = (bf16[512,256]{1,0:T(8,128)(2,1)S(1)}, bf16[512,256]{1,0:T(8,128)(2,1)S(1)}, u32[]{:S(2)}, u32[]{:S(2)}) collective-permute-start(bf16[512,256]{1,0:T(8,128)(2,1)S(1)} %collective-permute-done.15.refs_4_), channel_id=1, source_target_pairs={{0,56},{8,0},{16,8},{24,16},{32,24},{40,32},{48,40},{56,48},{1,57}... | collective-permute-start | bytes 786440 | tf_op jit(solution)/shard_map/ppermute | solution.py:27
  65.7 3.2 %collective-permute-start.25 = (bf16[512,256]{1,0:T(8,128)(2,1)}, bf16[512,256]{1,0:T(8,128)(2,1)S(1)}, u32[]{:S(2)}, u32[]{:S(2)}) collective-permute-start(bf16[512,256]{1,0:T(8,128)(2,1)} %collective-permute-done.23.refs_13_), channel_id=1, source_target_pairs={{0,56},{8,0},{16,8},{24,16},{32,24},{40,32},{48,40},{56,48},{1,57}... | collective-permute-start | bytes 786440 | tf_op jit(solution)/shard_map/ppermute | solution.py:27
  73.0 3.3 %collective-permute-start.19 = (bf16[256,256]{1,0:T(8,128)(2,1)S(1)}, bf16[256,256]{1,0:T(8,128)(2,1)S(1)}, u32[]{:S(2)}, u32[]{:S(2)}) collective-permute-start(bf16[256,256]{1,0:T(8,128)(2,1)S(1)} %slice.90), channel_id=1, source_target_pairs={{0,56},{8,0},{16,8},{24,16},{32,24},{40,32},{48,40},{56,48},{1,57}... | collective-permute-start | bytes 393224 | tf_op jit(solution)/shard_map/ppermute | solution.py:27
  78.1 3.3 %collective-permute-start.27 = (bf16[256,256]{1,0:T(8,128)(2,1)S(1)}, bf16[256,256]{1,0:T(8,128)(2,1)S(1)}, u32[]{:S(2)}, u32[]{:S(2)}) collective-permute-start(bf16[256,256]{1,0:T(8,128)(2,1)S(1)} %slice.92), channel_id=1, source_target_pairs={{0,56},{8,0},{16,8},{24,16},{32,24},{40,32},{48,40},{56,48},{1,57}... | collective-permute-start | bytes 393224 | tf_op jit(solution)/shard_map/ppermute | solution.py:27
  82.2 2.1 %collective-permute-done.26.refs_16_ = bf16[256,256]{1,0:T(8,128)(2,1)S(1)} collective-permute-done((bf16[256,256]{1,0:T(8,128)(2,1)S(1)}, bf16[256,256]{1,0:T(8,128)(2,1)S(1)}, u32[]{:S(2)}, u32[]{:S(2)}) %collective-permute-start.26) | collective-permute-done | bytes 131104 | tf_op jit(solution)/shard_map/ppermute | solution.py:27
  85.2 3.3 %attend.7 = bf16[2080,128]{1,0:T(8,128)(2,1)S(1)} custom-call(s32[16]{0:T(128)S(1)} %get-tuple-element.56.place_ref, s32[16]{0:T(128)S(1)} %get-tuple-element.43.lane_ref, f32[16]{0:T(128)S(1)} %get-tuple-element.39.bias_ref, bf16[528,256]{1,0:T(8,128)(2,1)S(1)} %copy-done.4, bf16[512,256]{1,0:T(8,128)(2,1)S(1)} %get-tuple-element.34.refs_0_, ...), custom_call_target="tpu_custom_call" | custom-call | flops 536870912 | bytes 6291456 | tf_op jit(solution)/shard_map/attend/pallas_call | solution.py:214
  89.2 3.7 %attend.6 = bf16[2080,128]{1,0:T(8,128)(2,1)S(1)} custom-call(s32[16]{0:T(128)S(1)} %get-tuple-element.55.place_ref, s32[16]{0:T(128)S(1)} %get-tuple-element.44.lane_ref, f32[16]{0:T(128)S(1)} %get-tuple-element.40.bias_ref, bf16[528,256]{1,0:T(8,128)(2,1)} %collective-permute-done.13.query_ref, bf16[512,256]{1,0:T(8,128)(2,1)S(1)} %get-tuple-element.34.refs_0_, ...), custom_call_target="tpu_custom_call" | custom-call | flops 536870912 | bytes 6291456 | tf_op jit(solution)/shard_map/attend/pallas_call | solution.py:214
  93.0 2.6 %collective-permute-start.29 = (bf16[2080,128]{1,0:T(8,128)(2,1)S(1)}, bf16[2080,128]{1,0:T(8,128)(2,1)S(1)}, u32[]{:S(2)}, u32[]{:S(2)}) collective-permute-start(bf16[2080,128]{1,0:T(8,128)(2,1)S(1)} %attend.6), channel_id=1, source_target_pairs={{0,128},{64,192},{128,0},{192,64},{1,129},{65,193},{129,1},{193,65... | collective-permute-start | bytes 1597448 | tf_op jit(solution)/shard_map/ppermute | solution.py:27
  96.5 3.2 %attend.5 = bf16[2080,128]{1,0:T(8,128)(2,1)S(1)} custom-call(s32[16]{0:T(128)S(1)} %get-tuple-element.54.place_ref, s32[16]{0:T(128)S(1)} %get-tuple-element.45.lane_ref, f32[16]{0:T(128)S(1)} %get-tuple-element.41.bias_ref, bf16[528,256]{1,0:T(8,128)(2,1)S(1)} %copy-done.2, bf16[512,256]{1,0:T(8,128)(2,1)S(1)} %get-tuple-element.34.refs_0_, ...), custom_call_target="tpu_custom_call" | custom-call | flops 536870912 | bytes 6291456 | tf_op jit(solution)/shard_map/attend/pallas_call | solution.py:214
  102.0 3.8 %attend.4.refs_0_ = bf16[2080,128]{1,0:T(8,128)(2,1)S(1)} custom-call(s32[16]{0:T(128)S(1)} %get-tuple-element.53.place_ref, s32[16]{0:T(128)S(1)} %get-tuple-element.46.lane_ref, f32[16]{0:T(128)S(1)} %get-tuple-element.42.bias_ref, bf16[528,256]{1,0:T(8,128)(2,1)} %fusion.1.query_ref, bf16[512,256]{1,0:T(8,128)(2,1)S(1)} %get-tuple-element.34.refs_0_, ...), custom_call_target="tpu_custom_call" | custom-call | flops 536870912 | bytes 6291456 | tf_op jit(solution)/shard_map/attend/pallas_call | solution.py:214
  105.8 4.8 %collective-permute-done.30.refs_3_ = bf16[2080,128]{1,0:T(8,128)(2,1)S(1)} collective-permute-done((bf16[2080,128]{1,0:T(8,128)(2,1)S(1)}, bf16[2080,128]{1,0:T(8,128)(2,1)S(1)}, u32[]{:S(2)}, u32[]{:S(2)}) %collective-permute-start.30) | collective-permute-done | bytes 532512 | tf_op jit(solution)/shard_map/ppermute | solution.py:27
  110.6 7.4 %collective-permute-done.28.refs_1_ = bf16[2080,128]{1,0:T(8,128)(2,1)S(1)} collective-permute-done((bf16[2080,128]{1,0:T(8,128)(2,1)S(1)}, bf16[2080,128]{1,0:T(8,128)(2,1)S(1)}, u32[]{:S(2)}, u32[]{:S(2)}) %collective-permute-start.28) | collective-permute-done | bytes 532512 | tf_op jit(solution)/shard_map/ppermute | solution.py:27
  118.8 11.4 %all_to_all.5 = bf16[8,64,256]{2,1,0:T(8,128)(2,1)S(1)} all-to-all(bf16[8,64,256]{2,1,0:T(8,128)(2,1)S(1)} %bitcast.39), channel_id=1, replica_groups=mesh['y'=4,'z'=8,'x'=4,'c'=2] {'x','c'}, dimensions={0} | all-to-all | bytes 524288 | tf_op jit(solution)/shard_map/all_to_all | solution.py:328
  130.2 9.6 %convolution_convert_fusion = bf16[64,4096]{1,0:T(8,128)(2,1)} fusion(bf16[64,2048]{1,0:T(8,128)(2,1)S(1)} %bitcast.44, bf16[2048,4096]{1,0:T(8,128)(2,1)} %all-gather.2.cloned.1.call-done), kind=kOutput, calls=%fused_computation | convolution fusion | flops 1074003968 | bytes 17563648 | tf_op jit(solution)/shard_map/dot_general | solution.py:332
  (80 shorter events, 33.3 us)
Async XLA Ops:
  6.5 123.6 %all-gather.2.cloned.1.call-start = ((), (), s32[]{:S(2)}) async-start(), calls=%async_computation.1 | async-start | bytes 18874368 | tf_op jit(solution)/shard_map/all_gather | solution.py:315
  6.5 15.1 %collective-permute-start.2 = (bf16[512,512]{1,0:T(8,128)(2,1)}, bf16[512,512]{1,0:T(8,128)(2,1)S(1)}, u32[]{:S(2)}, u32[]{:S(2)}) collective-permute-start(bf16[512,512]{1,0:T(8,128)(2,1)} %bitcast.40), channel_id=1, source_target_pairs={{0,2},{2,4},{4,6},{6,0},{1,3},{3,5},{5,7},{7,1},{8,10},{10,12},{12... | collective-permute-start | bytes 1572872 | tf_op jit(solution)/shard_map/ppermute | solution.py:27
  8.0 13.6 %collective-permute-start.3 = (bf16[512,512]{1,0:T(8,128)(2,1)}, bf16[512,512]{1,0:T(8,128)(2,1)S(1)}, u32[]{:S(2)}, u32[]{:S(2)}) collective-permute-start(bf16[512,512]{1,0:T(8,128)(2,1)} %bitcast.41), channel_id=1, source_target_pairs={{0,6},{2,0},{4,2},{6,4},{1,7},{3,1},{5,3},{7,5},{8,14},{10,8},{12,... | collective-permute-start | bytes 1572872 | tf_op jit(solution)/shard_map/ppermute | solution.py:27
  14.5 11.9 %collective-permute-start.6 = (bf16[512,512]{1,0:T(8,128)(2,1)}, bf16[512,512]{1,0:T(8,128)(2,1)S(1)}, u32[]{:S(2)}, u32[]{:S(2)}) collective-permute-start(bf16[512,512]{1,0:T(8,128)(2,1)} %bitcast.42), channel_id=1, source_target_pairs={{0,1},{1,0},{2,3},{3,2},{4,5},{5,4},{6,7},{7,6},{8,9},{9,8},{10,11... | collective-permute-start | bytes 1572872 | tf_op jit(solution)/shard_map/ppermute | solution.py:27
  23.0 10.2 %collective-permute-start.4 = (bf16[256,512]{1,0:T(8,128)(2,1)}, bf16[256,512]{1,0:T(8,128)(2,1)S(1)}, u32[]{:S(2)}, u32[]{:S(2)}) collective-permute-start(bf16[256,512]{1,0:T(8,128)(2,1)} %slice.68), channel_id=1, source_target_pairs={{0,2},{2,4},{4,6},{6,0},{1,3},{3,5},{5,7},{7,1},{8,10},{10,12},{12... | collective-permute-start | bytes 786440 | tf_op jit(solution)/shard_map/ppermute | solution.py:27
  24.5 8.7 %collective-permute-start.5 = (bf16[256,512]{1,0:T(8,128)(2,1)S(1)}, bf16[256,512]{1,0:T(8,128)(2,1)S(1)}, u32[]{:S(2)}, u32[]{:S(2)}) collective-permute-start(bf16[256,512]{1,0:T(8,128)(2,1)S(1)} %slice.69), channel_id=1, source_target_pairs={{0,6},{2,0},{4,2},{6,4},{1,7},{3,1},{5,3},{7,5},{8,14},{10,8},{12,... | collective-permute-start | bytes 786440 | tf_op jit(solution)/shard_map/ppermute | solution.py:27
  36.0 13.0 %collective-permute-start.11 = (bf16[512,256]{1,0:T(8,128)(2,1)S(1)}, bf16[512,256]{1,0:T(8,128)(2,1)S(1)}, u32[]{:S(2)}, u32[]{:S(2)}) collective-permute-start(bf16[512,256]{1,0:T(8,128)(2,1)S(1)} %get-tuple-element.34.refs_0_), channel_id=1, source_target_pairs={{0,8},{8,16},{16,24},{24,32},{32,40},{40,48},{48,56},{56,0},{1,9},... | collective-permute-start | bytes 786440 | tf_op jit(solution)/shard_map/ppermute | solution.py:27
  38.0 11.0 %collective-permute-start.14 = (bf16[512,256]{1,0:T(8,128)(2,1)S(1)}, bf16[512,256]{1,0:T(8,128)(2,1)S(1)}, u32[]{:S(2)}, u32[]{:S(2)}) collective-permute-start(bf16[512,256]{1,0:T(8,128)(2,1)S(1)} %get-tuple-element.34.refs_0_), channel_id=1, source_target_pairs={{0,56},{8,0},{16,8},{24,16},{32,24},{40,32},{48,40},{56,48},{1,57}... | collective-permute-start | bytes 786440 | tf_op jit(solution)/shard_map/ppermute | solution.py:27
  42.0 12.6 %collective-permute-start.20 = (bf16[512,256]{1,0:T(8,128)(2,1)S(1)}, bf16[512,256]{1,0:T(8,128)(2,1)S(1)}, u32[]{:S(2)}, u32[]{:S(2)}) collective-permute-start(bf16[512,256]{1,0:T(8,128)(2,1)S(1)} %get-tuple-element.37.refs_9_), channel_id=1, source_target_pairs={{0,8},{8,16},{16,24},{24,32},{32,40},{40,48},{48,56},{56,0},{1,9},... | collective-permute-start | bytes 786440 | tf_op jit(solution)/shard_map/ppermute | solution.py:27
  42.0 12.6 %collective-permute-start.21 = (bf16[512,256]{1,0:T(8,128)(2,1)S(1)}, bf16[512,256]{1,0:T(8,128)(2,1)S(1)}, u32[]{:S(2)}, u32[]{:S(2)}) collective-permute-start(bf16[512,256]{1,0:T(8,128)(2,1)S(1)} %get-tuple-element.37.refs_9_), channel_id=1, source_target_pairs={{0,56},{8,0},{16,8},{24,16},{32,24},{40,32},{48,40},{56,48},{1,57}... | collective-permute-start | bytes 786440 | tf_op jit(solution)/shard_map/ppermute | solution.py:27
  49.0 11.2 %collective-permute-start.12 = (bf16[512,256]{1,0:T(8,128)(2,1)S(1)}, bf16[512,256]{1,0:T(8,128)(2,1)S(1)}, u32[]{:S(2)}, u32[]{:S(2)}) collective-permute-start(bf16[512,256]{1,0:T(8,128)(2,1)S(1)} %collective-permute-done.11.refs_1_), channel_id=1, source_target_pairs={{0,8},{8,16},{16,24},{24,32},{32,40},{40,48},{48,56},{56,0},{1,9},... | collective-permute-start | bytes 786440 | tf_op jit(solution)/shard_map/ppermute | solution.py:27
  49.0 13.4 %collective-permute-start.15 = (bf16[512,256]{1,0:T(8,128)(2,1)S(1)}, bf16[512,256]{1,0:T(8,128)(2,1)S(1)}, u32[]{:S(2)}, u32[]{:S(2)}) collective-permute-start(bf16[512,256]{1,0:T(8,128)(2,1)S(1)} %collective-permute-done.14.refs_2_), channel_id=1, source_target_pairs={{0,56},{8,0},{16,8},{24,16},{32,24},{40,32},{48,40},{56,48},{1,57}... | collective-permute-start | bytes 786440 | tf_op jit(solution)/shard_map/ppermute | solution.py:27
  54.6 11.1 %collective-permute-start.22 = (bf16[512,256]{1,0:T(8,128)(2,1)S(1)}, bf16[512,256]{1,0:T(8,128)(2,1)S(1)}, u32[]{:S(2)}, u32[]{:S(2)}) collective-permute-start(bf16[512,256]{1,0:T(8,128)(2,1)S(1)} %collective-permute-done.20.refs_10_), channel_id=1, source_target_pairs={{0,8},{8,16},{16,24},{24,32},{32,40},{40,48},{48,56},{56,0},{1,9},... | collective-permute-start | bytes 786440 | tf_op jit(solution)/shard_map/ppermute | solution.py:27
  54.6 11.1 %collective-permute-start.23 = (bf16[512,256]{1,0:T(8,128)(2,1)S(1)}, bf16[512,256]{1,0:T(8,128)(2,1)}, u32[]{:S(2)}, u32[]{:S(2)}) collective-permute-start(bf16[512,256]{1,0:T(8,128)(2,1)S(1)} %collective-permute-done.21.refs_11_), channel_id=1, source_target_pairs={{0,56},{8,0},{16,8},{24,16},{32,24},{40,32},{48,40},{56,48},{1,57}... | collective-permute-start | bytes 786440 | tf_op jit(solution)/shard_map/ppermute | solution.py:27
  60.2 21.2 %collective-permute-start.13 = (bf16[528,256]{1,0:T(8,128)(2,1)}, bf16[528,256]{1,0:T(8,128)(2,1)}, u32[]{:S(2)}, u32[]{:S(2)}) collective-permute-start(bf16[528,256]{1,0:T(8,128)(2,1)} %fusion.1.query_ref), channel_id=1, source_target_pairs={{0,128},{64,192},{128,0},{192,64},{1,129},{65,193},{129,1},{193,65... | collective-permute-start | bytes 811016 | tf_op jit(solution)/shard_map/ppermute | solution.py:27
  62.4 10.5 %collective-permute-start.16 = (bf16[512,256]{1,0:T(8,128)(2,1)S(1)}, bf16[512,256]{1,0:T(8,128)(2,1)S(1)}, u32[]{:S(2)}, u32[]{:S(2)}) collective-permute-start(bf16[512,256]{1,0:T(8,128)(2,1)S(1)} %collective-permute-done.12.refs_3_), channel_id=1, source_target_pairs={{0,8},{8,16},{16,24},{24,32},{32,40},{40,48},{48,56},{56,0},{1,9},... | collective-permute-start | bytes 786440 | tf_op jit(solution)/shard_map/ppermute | solution.py:27
  62.4 10.6 %collective-permute-start.17 = (bf16[512,256]{1,0:T(8,128)(2,1)S(1)}, bf16[512,256]{1,0:T(8,128)(2,1)S(1)}, u32[]{:S(2)}, u32[]{:S(2)}) collective-permute-start(bf16[512,256]{1,0:T(8,128)(2,1)S(1)} %collective-permute-done.15.refs_4_), channel_id=1, source_target_pairs={{0,56},{8,0},{16,8},{24,16},{32,24},{40,32},{48,40},{56,48},{1,57}... | collective-permute-start | bytes 786440 | tf_op jit(solution)/shard_map/ppermute | solution.py:27
  65.7 12.3 %collective-permute-start.24 = (bf16[512,256]{1,0:T(8,128)(2,1)S(1)}, bf16[512,256]{1,0:T(8,128)(2,1)S(1)}, u32[]{:S(2)}, u32[]{:S(2)}) collective-permute-start(bf16[512,256]{1,0:T(8,128)(2,1)S(1)} %collective-permute-done.22.refs_12_), channel_id=1, source_target_pairs={{0,8},{8,16},{16,24},{24,32},{32,40},{40,48},{48,56},{56,0},{1,9},... | collective-permute-start | bytes 786440 | tf_op jit(solution)/shard_map/ppermute | solution.py:27
  65.7 12.4 %collective-permute-start.25 = (bf16[512,256]{1,0:T(8,128)(2,1)}, bf16[512,256]{1,0:T(8,128)(2,1)S(1)}, u32[]{:S(2)}, u32[]{:S(2)}) collective-permute-start(bf16[512,256]{1,0:T(8,128)(2,1)} %collective-permute-done.23.refs_13_), channel_id=1, source_target_pairs={{0,56},{8,0},{16,8},{24,16},{32,24},{40,32},{48,40},{56,48},{1,57}... | collective-permute-start | bytes 786440 | tf_op jit(solution)/shard_map/ppermute | solution.py:27
  72.9 9.3 %collective-permute-start.18 = (bf16[256,256]{1,0:T(8,128)(2,1)S(1)}, bf16[256,256]{1,0:T(8,128)(2,1)S(1)}, u32[]{:S(2)}, u32[]{:S(2)}) collective-permute-start(bf16[256,256]{1,0:T(8,128)(2,1)S(1)} %slice.89), channel_id=1, source_target_pairs={{0,8},{8,16},{16,24},{24,32},{32,40},{40,48},{48,56},{56,0},{1,9},... | collective-permute-start | bytes 393224 | tf_op jit(solution)/shard_map/ppermute | solution.py:27
  73.0 9.2 %collective-permute-start.19 = (bf16[256,256]{1,0:T(8,128)(2,1)S(1)}, bf16[256,256]{1,0:T(8,128)(2,1)S(1)}, u32[]{:S(2)}, u32[]{:S(2)}) collective-permute-start(bf16[256,256]{1,0:T(8,128)(2,1)S(1)} %slice.90), channel_id=1, source_target_pairs={{0,56},{8,0},{16,8},{24,16},{32,24},{40,32},{48,40},{56,48},{1,57}... | collective-permute-start | bytes 393224 | tf_op jit(solution)/shard_map/ppermute | solution.py:27
  88.5 22.1 %collective-permute-start.30 = (bf16[2080,128]{1,0:T(8,128)(2,1)S(1)}, bf16[2080,128]{1,0:T(8,128)(2,1)S(1)}, u32[]{:S(2)}, u32[]{:S(2)}) collective-permute-start(bf16[2080,128]{1,0:T(8,128)(2,1)S(1)} %attend.7), channel_id=1, source_target_pairs={{0,64},{64,128},{128,192},{192,0},{1,65},{65,129},{129,193},{193,1... | collective-permute-start | bytes 1597448 | tf_op jit(solution)/shard_map/ppermute | solution.py:27
  93.0 17.7 %collective-permute-start.29 = (bf16[2080,128]{1,0:T(8,128)(2,1)S(1)}, bf16[2080,128]{1,0:T(8,128)(2,1)S(1)}, u32[]{:S(2)}, u32[]{:S(2)}) collective-permute-start(bf16[2080,128]{1,0:T(8,128)(2,1)S(1)} %attend.6), channel_id=1, source_target_pairs={{0,128},{64,192},{128,0},{192,64},{1,129},{65,193},{129,1},{193,65... | collective-permute-start | bytes 1597448 | tf_op jit(solution)/shard_map/ppermute | solution.py:27
  99.8 18.2 %collective-permute-start.28 = (bf16[2080,128]{1,0:T(8,128)(2,1)S(1)}, bf16[2080,128]{1,0:T(8,128)(2,1)S(1)}, u32[]{:S(2)}, u32[]{:S(2)}) collective-permute-start(bf16[2080,128]{1,0:T(8,128)(2,1)S(1)} %attend.5), channel_id=1, source_target_pairs={{0,192},{64,0},{128,64},{192,128},{1,193},{65,1},{129,65},{193,129... | collective-permute-start | bytes 1597448 | tf_op jit(solution)/shard_map/ppermute | solution.py:27
  (13 other events, 45.3 us)
Sparse Core Ops, SparseCore 0:
  36.1 89.8 all-gather.1

commit v4 on v3

--- a/solution.py
+++ b/solution.py
@@ -19,7 +19,8 @@
 QROWS = SPANS_DEV * SPAN
 WIDE = 2 * HD
 OROWS = SPANS_DEV * WIDE
-VMEM_LIMIT = 48 * 1024 * 1024
+VMEM_LIMIT = 32 * 1024 * 1024
+PROJECT_LIMIT = 48 * 1024 * 1024
 
 
 def shift(a, axis, k):
@@ -118,7 +119,7 @@
             pltpu.VMEM((2 * count, width, WIDE), jnp.bfloat16),
             pltpu.SemaphoreType.DMA((2 * blocks,)),
         ],
-        compiler_params=pltpu.CompilerParams(vmem_limit_bytes=VMEM_LIMIT),
+        compiler_params=pltpu.CompilerParams(vmem_limit_bytes=PROJECT_LIMIT),
         cost_estimate=pl.CostEstimate(
             flops=count * 512 * 512 * 1024, bytes_accessed=count << 20, transcendentals=0
         ),
@@ -133,7 +134,7 @@
         out_shape=[jax.ShapeDtypeStruct((BLOCK, WIDE), jnp.bfloat16)] * PAIRS,
         in_specs=[vmem] * (len(pieces) + len(sums)),
         out_specs=[vmem] * PAIRS,
-        compiler_params=pltpu.CompilerParams(vmem_limit_bytes=VMEM_LIMIT),
+        compiler_params=pltpu.CompilerParams(vmem_limit_bytes=PROJECT_LIMIT),
         cost_estimate=pl.CostEstimate(
             flops=2 * 512 * 512 * 1024, bytes_accessed=2 << 20, transcendentals=0
         ),
@@ -141,18 +142,25 @@
     )(*pieces, *sums)
 
 
-def attend_kernel(places, place_ref, lane_ref, bias_ref, query_ref, *refs):
-    pieces = refs[: len(places)]
-    out_ref, table, stats, sems = refs[len(places) :]
+def gather_table(places, pieces, table, sems):
     copies = [
         pltpu.make_async_copy(piece, table.at[pl.ds(row, piece.shape[0])], sems.at[i])
         for i, (row, piece) in enumerate(zip(places, pieces))
     ]
     for copy in copies:
         copy.start()
-    lane = lax.broadcasted_iota(jnp.int32, (SPAN, WIDE), 1)
     for copy in copies:
         copy.wait()
+
+
+def first_kernel(places, place_ref, lane_ref, bias_ref, query_ref, *refs):
+    pieces, (out_ref, table, stats, sems) = refs[: len(places)], refs[len(places) :]
+    gather_table(places, pieces, table, sems)
+    attend_kernel(place_ref, lane_ref, bias_ref, query_ref, table, out_ref, stats)
+
+
+def attend_kernel(place_ref, lane_ref, bias_ref, query_ref, table, out_ref, stats):
+    lane = lax.broadcasted_iota(jnp.int32, (SPAN, WIDE), 1)
     group = 4
     for first in range(0, SPANS_DEV, group):
         scores, values = [], []
@@ -207,26 +215,37 @@
     out_ref[OROWS:, :] = coded.astype(jnp.bfloat16)
 
 
-def attend(place, lane, bias, queries, pieces):
+def attend(place, lane, bias, queries, pieces, table=None):
     places = tuple(row for row, _ in pieces)
     smem = pl.BlockSpec(memory_space=pltpu.SMEM)
     vmem = pl.BlockSpec(memory_space=pltpu.VMEM)
-    return pl.pallas_call(
-        functools.partial(attend_kernel, places),
-        out_shape=jax.ShapeDtypeStruct((OROWS + 4 * SPANS_DEV, 2 * SPAN), jnp.bfloat16),
-        in_specs=[smem] * 3 + [vmem] + [pl.BlockSpec(memory_space=pltpu.HBM)] * len(pieces),
+    message = jax.ShapeDtypeStruct((OROWS + 4 * SPANS_DEV, 2 * SPAN), jnp.bfloat16)
+    whole = jax.ShapeDtypeStruct((PAIRS * NZ * BLOCK, WIDE), jnp.bfloat16)
+    stats = pltpu.VMEM((SPANS_DEV, 2 * SPAN), jnp.float32)
+    cost = pl.CostEstimate(flops=1 << 29, bytes_accessed=6 << 20, transcendentals=1 << 18)
+    params = pltpu.CompilerParams(vmem_limit_bytes=VMEM_LIMIT)
+    if table is None:
+        return pl.pallas_call(
+            functools.partial(first_kernel, places),
+            out_shape=[message, whole],
+            in_specs=[smem] * 3 + [vmem] + [pl.BlockSpec(memory_space=pltpu.HBM)] * len(pieces),
+            out_specs=[vmem, vmem],
+            scratch_shapes=[stats, pltpu.SemaphoreType.DMA((len(pieces),))],
+            compiler_params=params,
+            cost_estimate=cost,
+            name="attend_first",
+        )(place, lane, bias, queries, *[a for _, a in pieces])
+    out = pl.pallas_call(
+        attend_kernel,
+        out_shape=message,
+        in_specs=[smem] * 3 + [vmem] * 2,
         out_specs=vmem,
-        scratch_shapes=[
-            pltpu.VMEM((PAIRS * NZ * BLOCK, WIDE), jnp.bfloat16),
-            pltpu.VMEM((SPANS_DEV, 2 * SPAN), jnp.float32),
-            pltpu.SemaphoreType.DMA((len(pieces),)),
-        ],
-        compiler_params=pltpu.CompilerParams(vmem_limit_bytes=VMEM_LIMIT),
-        cost_estimate=pl.CostEstimate(
-            flops=1 << 29, bytes_accessed=6 << 20, transcendentals=1 << 18
-        ),
+        scratch_shapes=[stats],
+        compiler_params=params,
+        cost_estimate=cost,
         name="attend",
-    )(place, lane, bias, queries, *[a for _, a in pieces])
+    )(place, lane, bias, queries, table)
+    return out, table
 
 
 def combine_kernel(lambda_ref, *refs):
@@ -319,9 +338,9 @@
     bias = jnp.where(shard // NZ == y, 0.0, FAR).astype(jnp.float32)
     place = (((row // 2) * NZ + (z + NZ - shard % NZ) % NZ) * BLOCK).astype(jnp.int32)
     lane = ((row % 2) * NLEN).astype(jnp.int32)
-    messages = [None] * NY
+    messages, whole = [None] * NY, None
     for k in (2, 1, 3, 0):
-        out = attend(place[k], lane[k], bias[k], asked[k], table)
+        out, whole = attend(place[k], lane[k], bias[k], asked[k], table, whole)
         messages[k] = shift(out, "y", -k) if k else out
     heads_out = combine(lambda_head, messages)
 

time: 147 us -> 148 us (level)
  waiting for transfers between devices: 36.6 us -> 43.7 us
  Pallas kernels: 19.5 us -> 14.6 us
    ppermute x31, waiting for transfers between devices: 36.6 us -> 43.7 us  [shift(): return lax.ppermute(a, axis, [(i, (i + k) % n) for i in range(n)])]
    pallas_call x4, Pallas kernels: 14 us -> 8.08 us  [the longest x3 4.76 us: attend(): pl.pallas_call(attend_kernel, out_shape=message, in_specs=[smem] * 3 + [v...]
    slice x4, local copies, waits for them, and re-layouts: 2.69 us -> 0.01 us  [on_device(): a[QROWS, :2 * SPANS_DEV]]
  transfers between devices with their start and end apart: 32 -> 32, of which waited for: 14 -> 14; matrix products, arithmetic and copies ran while one was open for 4% -> 2% of each run, Pallas kernels for 13% -> 9%
where the time goes in v4:
time: 148 us; the launch traced here: 147 us
  starting transfers between devices  45.6 us (31%)
  waiting for transfers between devices  43.7 us (30%)
  Pallas kernels  14.6 us (10%)
  between operations  14.3 us (10%)
  blocking collectives  11.5 us (8%)
  matrix products  9.59 us (6%)
  local copies, waits for them, and re-layouts  6.15 us (4%)
  other arithmetic  1.74 us (1%)
    ppermute x31, starting transfers between devices, shift(): return lax.ppermute(a, axis, [(i, (i + k) % n) for i in range(n)])  45.6 us
    ppermute x31, waiting for transfers between devices, shift(): return lax.ppermute(a, axis, [(i, (i + k) % n) for i in range(n)])  43.7 us
    all_to_all x1, blocking collectives, on_device(): lax.all_to_all(heads_out.reshape(NX * NC, SPAN, WIDE), ('x', 'c'), split_...  11.5 us
    dot_general x1, matrix products, on_device(): jnp.dot(rows, weight, preferred_element_type=jnp.float32)  9.59 us
    pallas_call x3, Pallas kernels, attend(): pl.pallas_call(attend_kernel, out_shape=message, in_specs=[smem] * 3 + [v...  4.76 us
    unnamed x10, local copies, waits for them, and re-layouts  4.36 us
    pallas_call x1, Pallas kernels, project_early(): pl.pallas_call(early_kernel, out_shape=[jax.ShapeDtypeStruct((tokens, 2 *...  3.97 us
    pallas_call x1, Pallas kernels, attend(): pl.pallas_call(functools.partial(first_kernel, places), out_shape=[messag...  3.32 us
  transfers between devices with their start and end apart: 32, of which 14 were waited for; matrix products, arithmetic and copies ran while one was open for 2% of the time, Pallas kernels for 9%

profile of v4, /device:TPU:8, one launch (start us, length us, event | category | flops | bytes accessed | tf_op | source)
XLA Modules:
  0.0 147.3 jit_solution(12673187089150879416)
XLA Ops:
  14.0 5.4 %collective-permute-done.query_ref = bf16[528,256]{1,0:T(8,128)(2,1)S(1)} collective-permute-done((bf16[528,256]{1,0:T(8,128)(2,1)S(1)}, bf16[528,256]{1,0:T(8,128)(2,1)S(1)}, u32[]{:S(2)}, u32[]{:S(2)}) %collective-permute-start) | collective-permute-done | bytes 270368 | tf_op jit(solution)/shard_map/ppermute | solution.py:28
  25.1 1.7 %collective-permute-start.5 = (bf16[256,512]{1,0:T(8,128)(2,1)}, bf16[256,512]{1,0:T(8,128)(2,1)}, u32[]{:S(2)}, u32[]{:S(2)}) collective-permute-start(bf16[256,512]{1,0:T(8,128)(2,1)} %slice.69), channel_id=1, source_target_pairs={{0,6},{2,0},{4,2},{6,4},{1,7},{3,1},{5,3},{7,5},{8,14},{10,8},{12,... | collective-permute-start | bytes 786440 | tf_op jit(solution)/shard_map/ppermute | solution.py:28
  28.0 4.0 %project_early.1 = (f32[512,512]{1,0:T(8,128)S(1)}, f32[512,128]{1,0:T(8,128)S(1)}, bf16[4,512,256]{2,1,0:T(8,128)(2,1)S(1)}) custom-call(s32[8]{0:T(128)S(1)} %stack.38.feature_ref, bf16[512,512]{1,0:T(8,128)(2,1)S(1)} %bitcast.43, bf16[512,512]{1,0:T(8,128)(2,1)S(1)} %collective-permute-done.6.refs_1_, ...), custom_call_target="tpu_custom_call" | custom-call | flops 1610612736 | bytes 6291456 | tf_op jit(solution)/shard_map/project_early/pallas_call | solution.py:107
  35.5 1.9 %project_late.1 = (bf16[512,256]{1,0:T(8,128)(2,1)S(1)}, bf16[512,256]{1,0:T(8,128)(2,1)S(1)}) custom-call(bf16[256,512]{1,0:T(8,128)(2,1)} %collective-permute-done.4.refs_0_, bf16[256,512]{1,0:T(8,128)(2,1)} %collective-permute-done.5.refs_1_, bf16[256,512]{1,0:T(8,128)(2,1)S(1)} %collective-permute-done.9.refs_2_, ...), custom_call_target="tpu_custom_call" | custom-call | flops 536870912 | bytes 2097152 | tf_op jit(solution)/shard_map/project_late/pallas_call | solution.py:132
  37.4 2.0 %collective-permute-start.11 = (bf16[512,256]{1,0:T(8,128)(2,1)S(1)}, bf16[512,256]{1,0:T(8,128)(2,1)S(1)}, u32[]{:S(2)}, u32[]{:S(2)}) collective-permute-start(bf16[512,256]{1,0:T(8,128)(2,1)S(1)} %get-tuple-element.36.refs_0_), channel_id=1, source_target_pairs={{0,8},{8,16},{16,24},{24,32},{32,40},{40,48},{48,56},{56,0},{1,9},... | collective-permute-start | bytes 786440 | tf_op jit(solution)/shard_map/ppermute | solution.py:28
  39.3 4.0 %collective-permute-start.14 = (bf16[512,256]{1,0:T(8,128)(2,1)S(1)}, bf16[512,256]{1,0:T(8,128)(2,1)S(1)}, u32[]{:S(2)}, u32[]{:S(2)}) collective-permute-start(bf16[512,256]{1,0:T(8,128)(2,1)S(1)} %get-tuple-element.36.refs_0_), channel_id=1, source_target_pairs={{0,56},{8,0},{16,8},{24,16},{32,24},{40,32},{48,40},{56,48},{1,57}... | collective-permute-start | bytes 786440 | tf_op jit(solution)/shard_map/ppermute | solution.py:28
  43.4 3.2 %collective-permute-start.21 = (bf16[512,256]{1,0:T(8,128)(2,1)S(1)}, bf16[512,256]{1,0:T(8,128)(2,1)S(1)}, u32[]{:S(2)}, u32[]{:S(2)}) collective-permute-start(bf16[512,256]{1,0:T(8,128)(2,1)S(1)} %get-tuple-element.39.refs_9_), channel_id=1, source_target_pairs={{0,56},{8,0},{16,8},{24,16},{32,24},{40,32},{48,40},{56,48},{1,57}... | collective-permute-start | bytes 786440 | tf_op jit(solution)/shard_map/ppermute | solution.py:28
  46.6 3.8 %collective-permute-done.11.refs_1_ = bf16[512,256]{1,0:T(8,128)(2,1)S(1)} collective-permute-done((bf16[512,256]{1,0:T(8,128)(2,1)S(1)}, bf16[512,256]{1,0:T(8,128)(2,1)S(1)}, u32[]{:S(2)}, u32[]{:S(2)}) %collective-permute-start.11) | collective-permute-done | bytes 262176 | tf_op jit(solution)/shard_map/ppermute | solution.py:28
  50.4 3.4 %collective-permute-start.15 = (bf16[512,256]{1,0:T(8,128)(2,1)S(1)}, bf16[512,256]{1,0:T(8,128)(2,1)}, u32[]{:S(2)}, u32[]{:S(2)}) collective-permute-start(bf16[512,256]{1,0:T(8,128)(2,1)S(1)} %collective-permute-done.14.refs_2_), channel_id=1, source_target_pairs={{0,56},{8,0},{16,8},{24,16},{32,24},{40,32},{48,40},{56,48},{1,57}... | collective-permute-start | bytes 786440 | tf_op jit(solution)/shard_map/ppermute | solution.py:28
  53.8 2.3 %collective-permute-done.20.refs_10_ = bf16[512,256]{1,0:T(8,128)(2,1)S(1)} collective-permute-done((bf16[512,256]{1,0:T(8,128)(2,1)S(1)}, bf16[512,256]{1,0:T(8,128)(2,1)S(1)}, u32[]{:S(2)}, u32[]{:S(2)}) %collective-permute-start.20) | collective-permute-done | bytes 262176 | tf_op jit(solution)/shard_map/ppermute | solution.py:28
  56.7 3.2 %collective-permute-start.23 = (bf16[512,256]{1,0:T(8,128)(2,1)S(1)}, bf16[512,256]{1,0:T(8,128)(2,1)}, u32[]{:S(2)}, u32[]{:S(2)}) collective-permute-start(bf16[512,256]{1,0:T(8,128)(2,1)S(1)} %collective-permute-done.21.refs_11_), channel_id=1, source_target_pairs={{0,56},{8,0},{16,8},{24,16},{32,24},{40,32},{48,40},{56,48},{1,57}... | collective-permute-start | bytes 786440 | tf_op jit(solution)/shard_map/ppermute | solution.py:28
  61.7 2.3 %collective-permute-start.13 = (bf16[528,256]{1,0:T(8,128)(2,1)S(1)}, bf16[528,256]{1,0:T(8,128)(2,1)S(1)}, u32[]{:S(2)}, u32[]{:S(2)}) collective-permute-start(bf16[528,256]{1,0:T(8,128)(2,1)S(1)} %fusion.1.query_ref), channel_id=1, source_target_pairs={{0,128},{64,192},{128,0},{192,64},{1,129},{65,193},{129,1},{193,65... | collective-permute-start | bytes 811016 | tf_op jit(solution)/shard_map/ppermute | solution.py:28
  64.0 3.2 %collective-permute-start.17 = (bf16[512,256]{1,0:T(8,128)(2,1)}, bf16[512,256]{1,0:T(8,128)(2,1)S(1)}, u32[]{:S(2)}, u32[]{:S(2)}) collective-permute-start(bf16[512,256]{1,0:T(8,128)(2,1)} %collective-permute-done.15.refs_4_), channel_id=1, source_target_pairs={{0,56},{8,0},{16,8},{24,16},{32,24},{40,32},{48,40},{56,48},{1,57}... | collective-permute-start | bytes 786440 | tf_op jit(solution)/shard_map/ppermute | solution.py:28
  67.3 3.2 %collective-permute-start.25 = (bf16[512,256]{1,0:T(8,128)(2,1)}, bf16[512,256]{1,0:T(8,128)(2,1)S(1)}, u32[]{:S(2)}, u32[]{:S(2)}) collective-permute-start(bf16[512,256]{1,0:T(8,128)(2,1)} %collective-permute-done.23.refs_13_), channel_id=1, source_target_pairs={{0,56},{8,0},{16,8},{24,16},{32,24},{40,32},{48,40},{56,48},{1,57}... | collective-permute-start | bytes 786440 | tf_op jit(solution)/shard_map/ppermute | solution.py:28
  70.5 3.9 %collective-permute-done.16.refs_5_ = bf16[512,256]{1,0:T(8,128)(2,1)S(1)} collective-permute-done((bf16[512,256]{1,0:T(8,128)(2,1)}, bf16[512,256]{1,0:T(8,128)(2,1)S(1)}, u32[]{:S(2)}, u32[]{:S(2)}) %collective-permute-start.16) | collective-permute-done | bytes 262176 | tf_op jit(solution)/shard_map/ppermute | solution.py:28
  74.6 3.3 %collective-permute-start.19 = (bf16[256,256]{1,0:T(8,128)(2,1)S(1)}, bf16[256,256]{1,0:T(8,128)(2,1)S(1)}, u32[]{:S(2)}, u32[]{:S(2)}) collective-permute-start(bf16[256,256]{1,0:T(8,128)(2,1)S(1)} %slice.90), channel_id=1, source_target_pairs={{0,56},{8,0},{16,8},{24,16},{32,24},{40,32},{48,40},{56,48},{1,57}... | collective-permute-start | bytes 393224 | tf_op jit(solution)/shard_map/ppermute | solution.py:28
  79.7 3.5 %collective-permute-start.27 = (bf16[256,256]{1,0:T(8,128)(2,1)S(1)}, bf16[256,256]{1,0:T(8,128)(2,1)S(1)}, u32[]{:S(2)}, u32[]{:S(2)}) collective-permute-start(bf16[256,256]{1,0:T(8,128)(2,1)S(1)} %slice.92), channel_id=1, source_target_pairs={{0,56},{8,0},{16,8},{24,16},{32,24},{40,32},{48,40},{56,48},{1,57}... | collective-permute-start | bytes 393224 | tf_op jit(solution)/shard_map/ppermute | solution.py:28
  83.3 2.5 %collective-permute-done.26.refs_16_ = bf16[256,256]{1,0:T(8,128)(2,1)S(1)} collective-permute-done((bf16[256,256]{1,0:T(8,128)(2,1)S(1)}, bf16[256,256]{1,0:T(8,128)(2,1)S(1)}, u32[]{:S(2)}, u32[]{:S(2)}) %collective-permute-start.26) | collective-permute-done | bytes 131104 | tf_op jit(solution)/shard_map/ppermute | solution.py:28
  87.7 3.3 %attend_first.1 = (bf16[2080,128]{1,0:T(8,128)(2,1)S(1)}, bf16[8192,256]{1,0:T(8,128)(2,1)S(1)}) custom-call(s32[16]{0:T(128)S(1)} %get-tuple-element.58.place_ref, s32[16]{0:T(128)S(1)} %get-tuple-element.49.lane_ref, f32[16]{0:T(128)S(1)} %get-tuple-element.45.bias_ref, bf16[528,256]{1,0:T(8,128)(2,1)S(1)} %collective-permute-done.13.query_ref, ...), custom_call_target="tpu_custom_call" | custom-call | flops 536870912 | bytes 6291456 | tf_op jit(solution)/shard_map/attend_first/pallas_call | solution.py:228
  96.4 2.0 %collective-permute-start.29 = (bf16[2080,128]{1,0:T(8,128)(2,1)S(1)}, bf16[2080,128]{1,0:T(8,128)(2,1)S(1)}, u32[]{:S(2)}, u32[]{:S(2)}) collective-permute-start(bf16[2080,128]{1,0:T(8,128)(2,1)S(1)} %get-tuple-element.41), channel_id=1, source_target_pairs={{0,128},{64,192},{128,0},{192,64},{1,129},{65,193},{129,1},{193,65... | collective-permute-start | bytes 1597448 | tf_op jit(solution)/shard_map/ppermute | solution.py:28
  100.7 14.0 %collective-permute-done.30.refs_3_ = bf16[2080,128]{1,0:T(8,128)(2,1)S(1)} collective-permute-done((bf16[2080,128]{1,0:T(8,128)(2,1)S(1)}, bf16[2080,128]{1,0:T(8,128)(2,1)S(1)}, u32[]{:S(2)}, u32[]{:S(2)}) %collective-permute-start.30) | collective-permute-done | bytes 532512 | tf_op jit(solution)/shard_map/ppermute | solution.py:28
  114.6 3.9 %collective-permute-done.29.refs_2_ = bf16[2080,128]{1,0:T(8,128)(2,1)S(1)} collective-permute-done((bf16[2080,128]{1,0:T(8,128)(2,1)S(1)}, bf16[2080,128]{1,0:T(8,128)(2,1)S(1)}, u32[]{:S(2)}, u32[]{:S(2)}) %collective-permute-start.29) | collective-permute-done | bytes 532512 | tf_op jit(solution)/shard_map/ppermute | solution.py:28
  119.2 11.5 %all_to_all.5 = bf16[8,64,256]{2,1,0:T(8,128)(2,1)S(1)} all-to-all(bf16[8,64,256]{2,1,0:T(8,128)(2,1)S(1)} %bitcast.39), channel_id=1, replica_groups=mesh['y'=4,'z'=8,'x'=4,'c'=2] {'x','c'}, dimensions={0} | all-to-all | bytes 524288 | tf_op jit(solution)/shard_map/all_to_all | solution.py:347
  130.8 9.6 %convolution_convert_fusion = bf16[64,4096]{1,0:T(8,128)(2,1)} fusion(bf16[64,2048]{1,0:T(8,128)(2,1)S(1)} %bitcast.44, bf16[2048,4096]{1,0:T(8,128)(2,1)} %all-gather.2.cloned.1.call-done), kind=kOutput, calls=%fused_computation | convolution fusion | flops 1074003968 | bytes 17563648 | tf_op jit(solution)/shard_map/dot_general | solution.py:351
  (80 shorter events, 31.9 us)
Async XLA Ops:
  6.5 124.3 %all-gather.2.cloned.1.call-start = ((), (), s32[]{:S(2)}) async-start(), calls=%async_computation.1 | async-start | bytes 18874368 | tf_op jit(solution)/shard_map/all_gather | solution.py:334
  6.5 15.1 %collective-permute-start.2 = (bf16[512,512]{1,0:T(8,128)(2,1)}, bf16[512,512]{1,0:T(8,128)(2,1)S(1)}, u32[]{:S(2)}, u32[]{:S(2)}) collective-permute-start(bf16[512,512]{1,0:T(8,128)(2,1)} %bitcast.40), channel_id=1, source_target_pairs={{0,2},{2,4},{4,6},{6,0},{1,3},{3,5},{5,7},{7,1},{8,10},{10,12},{12... | collective-permute-start | bytes 1572872 | tf_op jit(solution)/shard_map/ppermute | solution.py:28
  8.0 13.6 %collective-permute-start.3 = (bf16[512,512]{1,0:T(8,128)(2,1)}, bf16[512,512]{1,0:T(8,128)(2,1)S(1)}, u32[]{:S(2)}, u32[]{:S(2)}) collective-permute-start(bf16[512,512]{1,0:T(8,128)(2,1)} %bitcast.41), channel_id=1, source_target_pairs={{0,6},{2,0},{4,2},{6,4},{1,7},{3,1},{5,3},{7,5},{8,14},{10,8},{12,... | collective-permute-start | bytes 1572872 | tf_op jit(solution)/shard_map/ppermute | solution.py:28
  14.0 12.9 %collective-permute-start.6 = (bf16[512,512]{1,0:T(8,128)(2,1)}, bf16[512,512]{1,0:T(8,128)(2,1)S(1)}, u32[]{:S(2)}, u32[]{:S(2)}) collective-permute-start(bf16[512,512]{1,0:T(8,128)(2,1)} %bitcast.42), channel_id=1, source_target_pairs={{0,1},{1,0},{2,3},{3,2},{4,5},{5,4},{6,7},{7,6},{8,9},{9,8},{10,11... | collective-permute-start | bytes 1572872 | tf_op jit(solution)/shard_map/ppermute | solution.py:28
  23.6 9.7 %collective-permute-start.4 = (bf16[256,512]{1,0:T(8,128)(2,1)}, bf16[256,512]{1,0:T(8,128)(2,1)}, u32[]{:S(2)}, u32[]{:S(2)}) collective-permute-start(bf16[256,512]{1,0:T(8,128)(2,1)} %slice.68), channel_id=1, source_target_pairs={{0,2},{2,4},{4,6},{6,0},{1,3},{3,5},{5,7},{7,1},{8,10},{10,12},{12... | collective-permute-start | bytes 786440 | tf_op jit(solution)/shard_map/ppermute | solution.py:28
  25.1 8.3 %collective-permute-start.5 = (bf16[256,512]{1,0:T(8,128)(2,1)}, bf16[256,512]{1,0:T(8,128)(2,1)}, u32[]{:S(2)}, u32[]{:S(2)}) collective-permute-start(bf16[256,512]{1,0:T(8,128)(2,1)} %slice.69), channel_id=1, source_target_pairs={{0,6},{2,0},{4,2},{6,4},{1,7},{3,1},{5,3},{7,5},{8,14},{10,8},{12,... | collective-permute-start | bytes 786440 | tf_op jit(solution)/shard_map/ppermute | solution.py:28
  37.4 13.0 %collective-permute-start.11 = (bf16[512,256]{1,0:T(8,128)(2,1)S(1)}, bf16[512,256]{1,0:T(8,128)(2,1)S(1)}, u32[]{:S(2)}, u32[]{:S(2)}) collective-permute-start(bf16[512,256]{1,0:T(8,128)(2,1)S(1)} %get-tuple-element.36.refs_0_), channel_id=1, source_target_pairs={{0,8},{8,16},{16,24},{24,32},{32,40},{40,48},{48,56},{56,0},{1,9},... | collective-permute-start | bytes 786440 | tf_op jit(solution)/shard_map/ppermute | solution.py:28
  39.3 11.1 %collective-permute-start.14 = (bf16[512,256]{1,0:T(8,128)(2,1)S(1)}, bf16[512,256]{1,0:T(8,128)(2,1)S(1)}, u32[]{:S(2)}, u32[]{:S(2)}) collective-permute-start(bf16[512,256]{1,0:T(8,128)(2,1)S(1)} %get-tuple-element.36.refs_0_), channel_id=1, source_target_pairs={{0,56},{8,0},{16,8},{24,16},{32,24},{40,32},{48,40},{56,48},{1,57}... | collective-permute-start | bytes 786440 | tf_op jit(solution)/shard_map/ppermute | solution.py:28
  43.4 12.6 %collective-permute-start.20 = (bf16[512,256]{1,0:T(8,128)(2,1)S(1)}, bf16[512,256]{1,0:T(8,128)(2,1)S(1)}, u32[]{:S(2)}, u32[]{:S(2)}) collective-permute-start(bf16[512,256]{1,0:T(8,128)(2,1)S(1)} %get-tuple-element.39.refs_9_), channel_id=1, source_target_pairs={{0,8},{8,16},{16,24},{24,32},{32,40},{40,48},{48,56},{56,0},{1,9},... | collective-permute-start | bytes 786440 | tf_op jit(solution)/shard_map/ppermute | solution.py:28
  43.4 13.3 %collective-permute-start.21 = (bf16[512,256]{1,0:T(8,128)(2,1)S(1)}, bf16[512,256]{1,0:T(8,128)(2,1)S(1)}, u32[]{:S(2)}, u32[]{:S(2)}) collective-permute-start(bf16[512,256]{1,0:T(8,128)(2,1)S(1)} %get-tuple-element.39.refs_9_), channel_id=1, source_target_pairs={{0,56},{8,0},{16,8},{24,16},{32,24},{40,32},{48,40},{56,48},{1,57}... | collective-permute-start | bytes 786440 | tf_op jit(solution)/shard_map/ppermute | solution.py:28
  50.4 11.3 %collective-permute-start.12 = (bf16[512,256]{1,0:T(8,128)(2,1)S(1)}, bf16[512,256]{1,0:T(8,128)(2,1)}, u32[]{:S(2)}, u32[]{:S(2)}) collective-permute-start(bf16[512,256]{1,0:T(8,128)(2,1)S(1)} %collective-permute-done.11.refs_1_), channel_id=1, source_target_pairs={{0,8},{8,16},{16,24},{24,32},{32,40},{40,48},{48,56},{56,0},{1,9},... | collective-permute-start | bytes 786440 | tf_op jit(solution)/shard_map/ppermute | solution.py:28
  50.4 13.6 %collective-permute-start.15 = (bf16[512,256]{1,0:T(8,128)(2,1)S(1)}, bf16[512,256]{1,0:T(8,128)(2,1)}, u32[]{:S(2)}, u32[]{:S(2)}) collective-permute-start(bf16[512,256]{1,0:T(8,128)(2,1)S(1)} %collective-permute-done.14.refs_2_), channel_id=1, source_target_pairs={{0,56},{8,0},{16,8},{24,16},{32,24},{40,32},{48,40},{56,48},{1,57}... | collective-permute-start | bytes 786440 | tf_op jit(solution)/shard_map/ppermute | solution.py:28
  56.0 11.3 %collective-permute-start.22 = (bf16[512,256]{1,0:T(8,128)(2,1)S(1)}, bf16[512,256]{1,0:T(8,128)(2,1)}, u32[]{:S(2)}, u32[]{:S(2)}) collective-permute-start(bf16[512,256]{1,0:T(8,128)(2,1)S(1)} %collective-permute-done.20.refs_10_), channel_id=1, source_target_pairs={{0,8},{8,16},{16,24},{24,32},{32,40},{40,48},{48,56},{56,0},{1,9},... | collective-permute-start | bytes 786440 | tf_op jit(solution)/shard_map/ppermute | solution.py:28
  56.7 10.6 %collective-permute-start.23 = (bf16[512,256]{1,0:T(8,128)(2,1)S(1)}, bf16[512,256]{1,0:T(8,128)(2,1)}, u32[]{:S(2)}, u32[]{:S(2)}) collective-permute-start(bf16[512,256]{1,0:T(8,128)(2,1)S(1)} %collective-permute-done.21.refs_11_), channel_id=1, source_target_pairs={{0,56},{8,0},{16,8},{24,16},{32,24},{40,32},{48,40},{56,48},{1,57}... | collective-permute-start | bytes 786440 | tf_op jit(solution)/shard_map/ppermute | solution.py:28
  61.7 21.4 %collective-permute-start.13 = (bf16[528,256]{1,0:T(8,128)(2,1)S(1)}, bf16[528,256]{1,0:T(8,128)(2,1)S(1)}, u32[]{:S(2)}, u32[]{:S(2)}) collective-permute-start(bf16[528,256]{1,0:T(8,128)(2,1)S(1)} %fusion.1.query_ref), channel_id=1, source_target_pairs={{0,128},{64,192},{128,0},{192,64},{1,129},{65,193},{129,1},{193,65... | collective-permute-start | bytes 811016 | tf_op jit(solution)/shard_map/ppermute | solution.py:28
  64.0 10.4 %collective-permute-start.16 = (bf16[512,256]{1,0:T(8,128)(2,1)}, bf16[512,256]{1,0:T(8,128)(2,1)S(1)}, u32[]{:S(2)}, u32[]{:S(2)}) collective-permute-start(bf16[512,256]{1,0:T(8,128)(2,1)} %collective-permute-done.12.refs_3_), channel_id=1, source_target_pairs={{0,8},{8,16},{16,24},{24,32},{32,40},{40,48},{48,56},{56,0},{1,9},... | collective-permute-start | bytes 786440 | tf_op jit(solution)/shard_map/ppermute | solution.py:28
  64.0 10.5 %collective-permute-start.17 = (bf16[512,256]{1,0:T(8,128)(2,1)}, bf16[512,256]{1,0:T(8,128)(2,1)S(1)}, u32[]{:S(2)}, u32[]{:S(2)}) collective-permute-start(bf16[512,256]{1,0:T(8,128)(2,1)} %collective-permute-done.15.refs_4_), channel_id=1, source_target_pairs={{0,56},{8,0},{16,8},{24,16},{32,24},{40,32},{48,40},{56,48},{1,57}... | collective-permute-start | bytes 786440 | tf_op jit(solution)/shard_map/ppermute | solution.py:28
  67.3 12.3 %collective-permute-start.24 = (bf16[512,256]{1,0:T(8,128)(2,1)}, bf16[512,256]{1,0:T(8,128)(2,1)S(1)}, u32[]{:S(2)}, u32[]{:S(2)}) collective-permute-start(bf16[512,256]{1,0:T(8,128)(2,1)} %collective-permute-done.22.refs_12_), channel_id=1, source_target_pairs={{0,8},{8,16},{16,24},{24,32},{32,40},{40,48},{48,56},{56,0},{1,9},... | collective-permute-start | bytes 786440 | tf_op jit(solution)/shard_map/ppermute | solution.py:28
  67.3 12.4 %collective-permute-start.25 = (bf16[512,256]{1,0:T(8,128)(2,1)}, bf16[512,256]{1,0:T(8,128)(2,1)S(1)}, u32[]{:S(2)}, u32[]{:S(2)}) collective-permute-start(bf16[512,256]{1,0:T(8,128)(2,1)} %collective-permute-done.23.refs_13_), channel_id=1, source_target_pairs={{0,56},{8,0},{16,8},{24,16},{32,24},{40,32},{48,40},{56,48},{1,57}... | collective-permute-start | bytes 786440 | tf_op jit(solution)/shard_map/ppermute | solution.py:28
  74.5 8.8 %collective-permute-start.18 = (bf16[256,256]{1,0:T(8,128)(2,1)S(1)}, bf16[256,256]{1,0:T(8,128)(2,1)S(1)}, u32[]{:S(2)}, u32[]{:S(2)}) collective-permute-start(bf16[256,256]{1,0:T(8,128)(2,1)S(1)} %slice.89), channel_id=1, source_target_pairs={{0,8},{8,16},{16,24},{24,32},{32,40},{40,48},{48,56},{56,0},{1,9},... | collective-permute-start | bytes 393224 | tf_op jit(solution)/shard_map/ppermute | solution.py:28
  74.6 8.7 %collective-permute-start.19 = (bf16[256,256]{1,0:T(8,128)(2,1)S(1)}, bf16[256,256]{1,0:T(8,128)(2,1)S(1)}, u32[]{:S(2)}, u32[]{:S(2)}) collective-permute-start(bf16[256,256]{1,0:T(8,128)(2,1)S(1)} %slice.90), channel_id=1, source_target_pairs={{0,56},{8,0},{16,8},{24,16},{32,24},{40,32},{48,40},{56,48},{1,57}... | collective-permute-start | bytes 393224 | tf_op jit(solution)/shard_map/ppermute | solution.py:28
  92.6 22.0 %collective-permute-start.30 = (bf16[2080,128]{1,0:T(8,128)(2,1)S(1)}, bf16[2080,128]{1,0:T(8,128)(2,1)S(1)}, u32[]{:S(2)}, u32[]{:S(2)}) collective-permute-start(bf16[2080,128]{1,0:T(8,128)(2,1)S(1)} %attend.5), channel_id=1, source_target_pairs={{0,64},{64,128},{128,192},{192,0},{1,65},{65,129},{129,193},{193,1... | collective-permute-start | bytes 1597448 | tf_op jit(solution)/shard_map/ppermute | solution.py:28
  94.8 19.8 %collective-permute-start.28 = (bf16[2080,128]{1,0:T(8,128)(2,1)S(1)}, bf16[2080,128]{1,0:T(8,128)(2,1)S(1)}, u32[]{:S(2)}, u32[]{:S(2)}) collective-permute-start(bf16[2080,128]{1,0:T(8,128)(2,1)S(1)} %attend.4), channel_id=1, source_target_pairs={{0,192},{64,0},{128,64},{192,128},{1,193},{65,1},{129,65},{193,129... | collective-permute-start | bytes 1597448 | tf_op jit(solution)/shard_map/ppermute | solution.py:28
  96.4 22.1 %collective-permute-start.29 = (bf16[2080,128]{1,0:T(8,128)(2,1)S(1)}, bf16[2080,128]{1,0:T(8,128)(2,1)S(1)}, u32[]{:S(2)}, u32[]{:S(2)}) collective-permute-start(bf16[2080,128]{1,0:T(8,128)(2,1)S(1)} %get-tuple-element.41), channel_id=1, source_target_pairs={{0,128},{64,192},{128,0},{192,64},{1,129},{65,193},{129,1},{193,65... | collective-permute-start | bytes 1597448 | tf_op jit(solution)/shard_map/ppermute | solution.py:28
  (13 other events, 46.3 us)
Sparse Core Ops, SparseCore 0:
  37.5 90.2 all-gather.1

commit v5 on v3

--- a/solution.py
+++ b/solution.py
@@ -276,6 +276,44 @@
     )(lambda_head, *messages)
 
 
+def output_kernel(heads_ref, weight_ref, out_ref, total):
+    step = pl.program_id(0)
+    term = jnp.dot(heads_ref[0], weight_ref[...], preferred_element_type=jnp.float32)
+
+    @pl.when(step == 0)
+    def _():
+        total[...] = term
+
+    @pl.when(step > 0)
+    def _():
+        total[...] += term
+
+    @pl.when(step == pl.num_programs(0) - 1)
+    def _():
+        out_ref[...] = total[...].astype(jnp.bfloat16)
+
+
+def output(heads, weight):
+    count, rows, depth = heads.shape
+    width = weight.shape[1]
+    return pl.pallas_call(
+        output_kernel,
+        grid=(count,),
+        out_shape=jax.ShapeDtypeStruct((rows, width), jnp.bfloat16),
+        in_specs=[
+            pl.BlockSpec((1, rows, depth), lambda i: (i, 0, 0)),
+            pl.BlockSpec((depth, width), lambda i: (i, 0)),
+        ],
+        out_specs=pl.BlockSpec((rows, width), lambda i: (0, 0)),
+        scratch_shapes=[pltpu.VMEM((rows, width), jnp.float32)],
+        compiler_params=pltpu.CompilerParams(vmem_limit_bytes=VMEM_LIMIT),
+        cost_estimate=pl.CostEstimate(
+            flops=2 * 64 * 2048 * 4096, bytes_accessed=16 << 20, transcendentals=0
+        ),
+        name="output",
+    )(heads, weight)
+
+
 def on_device(
     queries, nbr_shard, nbr_row, database, key_weight, value_weight, lambda_head, out_weight
 ):
@@ -328,8 +366,7 @@
     heads = lax.all_to_all(
         heads_out.reshape(NX * NC, SPAN, WIDE), ("x", "c"), split_axis=0, concat_axis=0, tiled=True
     )
-    rows = jnp.swapaxes(heads, 0, 1).reshape(SPAN, NX * NC * WIDE)
-    return jnp.dot(rows, weight, preferred_element_type=jnp.float32).astype(jnp.bfloat16)
+    return output(heads, weight)
 
 
 def solution(mesh):

time: 147 us -> 150 us (1.020)
  Pallas kernels: 19.5 us -> 31 us
  matrix products: 9.59 us -> 0 us
  waiting for transfers between devices: 36.6 us -> 38.8 us
    pallas_call x0 -> x1, Pallas kernels: none -> 10.7 us  [output(): pl.pallas_call(output_kernel, grid=(count,), out_shape=jax.ShapeDtypeStru...]
    dot_general x1 -> x0, matrix products: 9.59 us -> none  [on_device(): jnp.dot(rows, weight, preferred_element_type=jnp.float32)]
    ppermute x31, waiting for transfers between devices: 36.6 us -> 38.8 us  [shift(): return lax.ppermute(a, axis, [(i, (i + k) % n) for i in range(n)])]
    unnamed x10, local copies, waits for them, and re-layouts: 3.52 us -> 1.54 us
  transfers between devices with their start and end apart: 32 -> 32, of which waited for: 14 -> 13; matrix products, arithmetic and copies ran while one was open for 4% -> 5% of each run, Pallas kernels for 13% -> 12%
where the time goes in v5:
time: 150 us
  starting transfers between devices  45.5 us (30%)
  waiting for transfers between devices  38.8 us (26%)
  Pallas kernels  31 us (21%)
  between operations  14.3 us (10%)
  blocking collectives  11.7 us (8%)
  local copies, waits for them, and re-layouts  5.99 us (4%)
  other arithmetic  2.45 us (2%)
    ppermute x31, starting transfers between devices, shift(): return lax.ppermute(a, axis, [(i, (i + k) % n) for i in range(n)])  45.5 us
    ppermute x31, waiting for transfers between devices, shift(): return lax.ppermute(a, axis, [(i, (i + k) % n) for i in range(n)])  38.8 us
    pallas_call x4, Pallas kernels, attend(): pl.pallas_call(functools.partial(attend_kernel, places), out_shape=jax.Sh...  14 us
    all_to_all x1, blocking collectives, on_device(): lax.all_to_all(heads_out.reshape(NX * NC, SPAN, WIDE), ('x', 'c'), split_...  11.7 us
    pallas_call x1, Pallas kernels, output(): pl.pallas_call(output_kernel, grid=(count,), out_shape=jax.ShapeDtypeStru...  10.7 us
    pallas_call x1, Pallas kernels, project_early(): pl.pallas_call(early_kernel, out_shape=[jax.ShapeDtypeStruct((tokens, 2 *...  3.95 us
  transfers between devices with their start and end apart: 32, of which 13 were waited for; matrix products, arithmetic and copies ran while one was open for 5% of the time, Pallas kernels for 12%

profile of v5, /device:TPU:8, one launch (start us, length us, event | category | flops | bytes accessed | tf_op | source)
XLA Modules:
  0.0 149.7 jit_solution(6442171625764778554)
XLA Ops:
  14.5 5.7 %collective-permute-done.query_ref = bf16[528,256]{1,0:T(8,128)(2,1)S(1)} collective-permute-done((bf16[528,256]{1,0:T(8,128)(2,1)}, bf16[528,256]{1,0:T(8,128)(2,1)S(1)}, u32[]{:S(2)}, u32[]{:S(2)}) %collective-permute-start) | collective-permute-done | bytes 270368 | tf_op jit(solution)/shard_map/ppermute | solution.py:27
  27.0 3.9 %project_early.1 = (f32[512,512]{1,0:T(8,128)S(1)}, f32[512,128]{1,0:T(8,128)S(1)}, bf16[4,512,256]{2,1,0:T(8,128)(2,1)S(1)}) custom-call(s32[8]{0:T(128)S(1)} %stack.38.feature_ref, bf16[512,512]{1,0:T(8,128)(2,1)S(1)} %bitcast.38, bf16[512,512]{1,0:T(8,128)(2,1)S(1)} %collective-permute-done.6.refs_1_, ...), custom_call_target="tpu_custom_call" | custom-call | flops 1610612736 | bytes 6291456 | tf_op jit(solution)/shard_map/project_early/pallas_call | solution.py:106
  31.0 2.8 %collective-permute-done.4.refs_0_ = bf16[256,512]{1,0:T(8,128)(2,1)S(1)} collective-permute-done((bf16[256,512]{1,0:T(8,128)(2,1)}, bf16[256,512]{1,0:T(8,128)(2,1)S(1)}, u32[]{:S(2)}, u32[]{:S(2)}) %collective-permute-start.4) | collective-permute-done | bytes 262176 | tf_op jit(solution)/shard_map/ppermute | solution.py:27
  39.7 4.0 %collective-permute-start.14 = (bf16[512,256]{1,0:T(8,128)(2,1)S(1)}, bf16[512,256]{1,0:T(8,128)(2,1)S(1)}, u32[]{:S(2)}, u32[]{:S(2)}) collective-permute-start(bf16[512,256]{1,0:T(8,128)(2,1)S(1)} %get-tuple-element.34.refs_0_), channel_id=1, source_target_pairs={{0,56},{8,0},{16,8},{24,16},{32,24},{40,32},{48,40},{56,48},{1,57}... | collective-permute-start | bytes 786440 | tf_op jit(solution)/shard_map/ppermute | solution.py:27
  43.7 3.2 %collective-permute-start.21 = (bf16[512,256]{1,0:T(8,128)(2,1)S(1)}, bf16[512,256]{1,0:T(8,128)(2,1)S(1)}, u32[]{:S(2)}, u32[]{:S(2)}) collective-permute-start(bf16[512,256]{1,0:T(8,128)(2,1)S(1)} %get-tuple-element.37.refs_9_), channel_id=1, source_target_pairs={{0,56},{8,0},{16,8},{24,16},{32,24},{40,32},{48,40},{56,48},{1,57}... | collective-permute-start | bytes 786440 | tf_op jit(solution)/shard_map/ppermute | solution.py:27
  47.0 3.8 %collective-permute-done.11.refs_1_ = bf16[512,256]{1,0:T(8,128)(2,1)S(1)} collective-permute-done((bf16[512,256]{1,0:T(8,128)(2,1)S(1)}, bf16[512,256]{1,0:T(8,128)(2,1)S(1)}, u32[]{:S(2)}, u32[]{:S(2)}) %collective-permute-start.11) | collective-permute-done | bytes 262176 | tf_op jit(solution)/shard_map/ppermute | solution.py:27
  50.7 3.4 %collective-permute-start.15 = (bf16[512,256]{1,0:T(8,128)(2,1)S(1)}, bf16[512,256]{1,0:T(8,128)(2,1)S(1)}, u32[]{:S(2)}, u32[]{:S(2)}) collective-permute-start(bf16[512,256]{1,0:T(8,128)(2,1)S(1)} %collective-permute-done.14.refs_2_), channel_id=1, source_target_pairs={{0,56},{8,0},{16,8},{24,16},{32,24},{40,32},{48,40},{56,48},{1,57}... | collective-permute-start | bytes 786440 | tf_op jit(solution)/shard_map/ppermute | solution.py:27
  54.1 2.3 %collective-permute-done.20.refs_10_ = bf16[512,256]{1,0:T(8,128)(2,1)S(1)} collective-permute-done((bf16[512,256]{1,0:T(8,128)(2,1)S(1)}, bf16[512,256]{1,0:T(8,128)(2,1)S(1)}, u32[]{:S(2)}, u32[]{:S(2)}) %collective-permute-start.20) | collective-permute-done | bytes 262176 | tf_op jit(solution)/shard_map/ppermute | solution.py:27
  56.4 3.4 %collective-permute-start.23 = (bf16[512,256]{1,0:T(8,128)(2,1)S(1)}, bf16[512,256]{1,0:T(8,128)(2,1)}, u32[]{:S(2)}, u32[]{:S(2)}) collective-permute-start(bf16[512,256]{1,0:T(8,128)(2,1)S(1)} %collective-permute-done.21.refs_11_), channel_id=1, source_target_pairs={{0,56},{8,0},{16,8},{24,16},{32,24},{40,32},{48,40},{56,48},{1,57}... | collective-permute-start | bytes 786440 | tf_op jit(solution)/shard_map/ppermute | solution.py:27
  59.7 2.3 %collective-permute-done.12.refs_3_ = bf16[512,256]{1,0:T(8,128)(2,1)S(1)} collective-permute-done((bf16[512,256]{1,0:T(8,128)(2,1)S(1)}, bf16[512,256]{1,0:T(8,128)(2,1)S(1)}, u32[]{:S(2)}, u32[]{:S(2)}) %collective-permute-start.12) | collective-permute-done | bytes 262176 | tf_op jit(solution)/shard_map/ppermute | solution.py:27
  62.0 2.2 %collective-permute-start.13 = (bf16[528,256]{1,0:T(8,128)(2,1)}, bf16[528,256]{1,0:T(8,128)(2,1)}, u32[]{:S(2)}, u32[]{:S(2)}) collective-permute-start(bf16[528,256]{1,0:T(8,128)(2,1)} %fusion.1.query_ref), channel_id=1, source_target_pairs={{0,128},{64,192},{128,0},{192,64},{1,129},{65,193},{129,1},{193,65... | collective-permute-start | bytes 811016 | tf_op jit(solution)/shard_map/ppermute | solution.py:27
  64.2 3.2 %collective-permute-start.17 = (bf16[512,256]{1,0:T(8,128)(2,1)S(1)}, bf16[512,256]{1,0:T(8,128)(2,1)S(1)}, u32[]{:S(2)}, u32[]{:S(2)}) collective-permute-start(bf16[512,256]{1,0:T(8,128)(2,1)S(1)} %collective-permute-done.15.refs_4_), channel_id=1, source_target_pairs={{0,56},{8,0},{16,8},{24,16},{32,24},{40,32},{48,40},{56,48},{1,57}... | collective-permute-start | bytes 786440 | tf_op jit(solution)/shard_map/ppermute | solution.py:27
  67.4 3.2 %collective-permute-start.25 = (bf16[512,256]{1,0:T(8,128)(2,1)}, bf16[512,256]{1,0:T(8,128)(2,1)S(1)}, u32[]{:S(2)}, u32[]{:S(2)}) collective-permute-start(bf16[512,256]{1,0:T(8,128)(2,1)} %collective-permute-done.23.refs_13_), channel_id=1, source_target_pairs={{0,56},{8,0},{16,8},{24,16},{32,24},{40,32},{48,40},{56,48},{1,57}... | collective-permute-start | bytes 786440 | tf_op jit(solution)/shard_map/ppermute | solution.py:27
  74.8 3.3 %collective-permute-start.19 = (bf16[256,256]{1,0:T(8,128)(2,1)S(1)}, bf16[256,256]{1,0:T(8,128)(2,1)S(1)}, u32[]{:S(2)}, u32[]{:S(2)}) collective-permute-start(bf16[256,256]{1,0:T(8,128)(2,1)S(1)} %slice.90), channel_id=1, source_target_pairs={{0,56},{8,0},{16,8},{24,16},{32,24},{40,32},{48,40},{56,48},{1,57}... | collective-permute-start | bytes 393224 | tf_op jit(solution)/shard_map/ppermute | solution.py:27
  79.9 3.3 %collective-permute-start.27 = (bf16[256,256]{1,0:T(8,128)(2,1)S(1)}, bf16[256,256]{1,0:T(8,128)(2,1)S(1)}, u32[]{:S(2)}, u32[]{:S(2)}) collective-permute-start(bf16[256,256]{1,0:T(8,128)(2,1)S(1)} %slice.92), channel_id=1, source_target_pairs={{0,56},{8,0},{16,8},{24,16},{32,24},{40,32},{48,40},{56,48},{1,57}... | collective-permute-start | bytes 393224 | tf_op jit(solution)/shard_map/ppermute | solution.py:27
  87.0 3.2 %attend.7 = bf16[2080,128]{1,0:T(8,128)(2,1)S(1)} custom-call(s32[16]{0:T(128)S(1)} %get-tuple-element.56.place_ref, s32[16]{0:T(128)S(1)} %get-tuple-element.43.lane_ref, f32[16]{0:T(128)S(1)} %get-tuple-element.39.bias_ref, bf16[528,256]{1,0:T(8,128)(2,1)S(1)} %copy-done.4, bf16[512,256]{1,0:T(8,128)(2,1)S(1)} %get-tuple-element.34.refs_0_, ...), custom_call_target="tpu_custom_call" | custom-call | flops 536870912 | bytes 6291456 | tf_op jit(solution)/shard_map/attend/pallas_call | solution.py:214
  90.9 3.7 %attend.6 = bf16[2080,128]{1,0:T(8,128)(2,1)S(1)} custom-call(s32[16]{0:T(128)S(1)} %get-tuple-element.55.place_ref, s32[16]{0:T(128)S(1)} %get-tuple-element.44.lane_ref, f32[16]{0:T(128)S(1)} %get-tuple-element.40.bias_ref, bf16[528,256]{1,0:T(8,128)(2,1)} %collective-permute-done.13.query_ref, bf16[512,256]{1,0:T(8,128)(2,1)S(1)} %get-tuple-element.34.refs_0_, ...), custom_call_target="tpu_custom_call" | custom-call | flops 536870912 | bytes 6291456 | tf_op jit(solution)/shard_map/attend/pallas_call | solution.py:214
  94.6 2.8 %collective-permute-start.29 = (bf16[2080,128]{1,0:T(8,128)(2,1)S(1)}, bf16[2080,128]{1,0:T(8,128)(2,1)S(1)}, u32[]{:S(2)}, u32[]{:S(2)}) collective-permute-start(bf16[2080,128]{1,0:T(8,128)(2,1)S(1)} %attend.6), channel_id=1, source_target_pairs={{0,128},{64,192},{128,0},{192,64},{1,129},{65,193},{129,1},{193,65... | collective-permute-start | bytes 1597448 | tf_op jit(solution)/shard_map/ppermute | solution.py:27
  97.4 3.3 %attend.5 = bf16[2080,128]{1,0:T(8,128)(2,1)S(1)} custom-call(s32[16]{0:T(128)S(1)} %get-tuple-element.54.place_ref, s32[16]{0:T(128)S(1)} %get-tuple-element.45.lane_ref, f32[16]{0:T(128)S(1)} %get-tuple-element.41.bias_ref, bf16[528,256]{1,0:T(8,128)(2,1)S(1)} %copy-done.2, bf16[512,256]{1,0:T(8,128)(2,1)S(1)} %get-tuple-element.34.refs_0_, ...), custom_call_target="tpu_custom_call" | custom-call | flops 536870912 | bytes 6291456 | tf_op jit(solution)/shard_map/attend/pallas_call | solution.py:214
  102.8 3.7 %attend.4.refs_0_ = bf16[2080,128]{1,0:T(8,128)(2,1)S(1)} custom-call(s32[16]{0:T(128)S(1)} %get-tuple-element.53.place_ref, s32[16]{0:T(128)S(1)} %get-tuple-element.46.lane_ref, f32[16]{0:T(128)S(1)} %get-tuple-element.42.bias_ref, bf16[528,256]{1,0:T(8,128)(2,1)} %fusion.1.query_ref, bf16[512,256]{1,0:T(8,128)(2,1)S(1)} %get-tuple-element.34.refs_0_, ...), custom_call_target="tpu_custom_call" | custom-call | flops 536870912 | bytes 6291456 | tf_op jit(solution)/shard_map/attend/pallas_call | solution.py:214
  106.5 5.8 %collective-permute-done.30.refs_3_ = bf16[2080,128]{1,0:T(8,128)(2,1)S(1)} collective-permute-done((bf16[2080,128]{1,0:T(8,128)(2,1)S(1)}, bf16[2080,128]{1,0:T(8,128)(2,1)S(1)}, u32[]{:S(2)}, u32[]{:S(2)}) %collective-permute-start.30) | collective-permute-done | bytes 532512 | tf_op jit(solution)/shard_map/ppermute | solution.py:27
  112.3 7.5 %collective-permute-done.28.refs_1_ = bf16[2080,128]{1,0:T(8,128)(2,1)S(1)} collective-permute-done((bf16[2080,128]{1,0:T(8,128)(2,1)S(1)}, bf16[2080,128]{1,0:T(8,128)(2,1)S(1)}, u32[]{:S(2)}, u32[]{:S(2)}) %collective-permute-start.28) | collective-permute-done | bytes 532512 | tf_op jit(solution)/shard_map/ppermute | solution.py:27
  120.5 11.7 %all_to_all.5.heads_ref = bf16[8,64,256]{2,1,0:T(8,128)(2,1)S(1)} all-to-all(bf16[8,64,256]{2,1,0:T(8,128)(2,1)S(1)} %bitcast.34), channel_id=1, replica_groups=mesh['y'=4,'z'=8,'x'=4,'c'=2] {'x','c'}, dimensions={0} | all-to-all | bytes 524288 | tf_op jit(solution)/shard_map/all_to_all | solution.py:366
  132.2 10.7 %output.1 = bf16[64,4096]{1,0:T(8,128)(2,1)} custom-call(bf16[8,64,256]{2,1,0:T(8,128)(2,1)S(1)} %all_to_all.5.heads_ref, bf16[2048,4096]{1,0:T(8,128)(2,1)} %all-gather.2.cloned.1.call-done.weight_ref), custom_call_target="tpu_custom_call" | custom-call | flops 1073741824 | bytes 16777216 | tf_op jit(solution)/shard_map/output/pallas_call | solution.py:299
  (79 shorter events, 33.1 us)
Async XLA Ops:
  6.5 125.7 %all-gather.2.cloned.1.call-start = ((), (), s32[]{:S(2)}) async-start(), calls=%async_computation.1 | async-start | bytes 18874368 | tf_op jit(solution)/shard_map/all_gather | solution.py:353
  6.5 15.1 %collective-permute-start.2 = (bf16[512,512]{1,0:T(8,128)(2,1)}, bf16[512,512]{1,0:T(8,128)(2,1)S(1)}, u32[]{:S(2)}, u32[]{:S(2)}) collective-permute-start(bf16[512,512]{1,0:T(8,128)(2,1)} %bitcast.35), channel_id=1, source_target_pairs={{0,2},{2,4},{4,6},{6,0},{1,3},{3,5},{5,7},{7,1},{8,10},{10,12},{12... | collective-permute-start | bytes 1572872 | tf_op jit(solution)/shard_map/ppermute | solution.py:27
  8.0 13.6 %collective-permute-start.3 = (bf16[512,512]{1,0:T(8,128)(2,1)}, bf16[512,512]{1,0:T(8,128)(2,1)S(1)}, u32[]{:S(2)}, u32[]{:S(2)}) collective-permute-start(bf16[512,512]{1,0:T(8,128)(2,1)} %bitcast.36), channel_id=1, source_target_pairs={{0,6},{2,0},{4,2},{6,4},{1,7},{3,1},{5,3},{7,5},{8,14},{10,8},{12,... | collective-permute-start | bytes 1572872 | tf_op jit(solution)/shard_map/ppermute | solution.py:27
  14.5 12.5 %collective-permute-start.6 = (bf16[512,512]{1,0:T(8,128)(2,1)}, bf16[512,512]{1,0:T(8,128)(2,1)S(1)}, u32[]{:S(2)}, u32[]{:S(2)}) collective-permute-start(bf16[512,512]{1,0:T(8,128)(2,1)} %bitcast.37), channel_id=1, source_target_pairs={{0,1},{1,0},{2,3},{3,2},{4,5},{5,4},{6,7},{7,6},{8,9},{9,8},{10,11... | collective-permute-start | bytes 1572872 | tf_op jit(solution)/shard_map/ppermute | solution.py:27
  23.7 10.1 %collective-permute-start.4 = (bf16[256,512]{1,0:T(8,128)(2,1)}, bf16[256,512]{1,0:T(8,128)(2,1)S(1)}, u32[]{:S(2)}, u32[]{:S(2)}) collective-permute-start(bf16[256,512]{1,0:T(8,128)(2,1)} %slice.68), channel_id=1, source_target_pairs={{0,2},{2,4},{4,6},{6,0},{1,3},{3,5},{5,7},{7,1},{8,10},{10,12},{12... | collective-permute-start | bytes 786440 | tf_op jit(solution)/shard_map/ppermute | solution.py:27
  25.1 8.7 %collective-permute-start.5 = (bf16[256,512]{1,0:T(8,128)(2,1)}, bf16[256,512]{1,0:T(8,128)(2,1)}, u32[]{:S(2)}, u32[]{:S(2)}) collective-permute-start(bf16[256,512]{1,0:T(8,128)(2,1)} %slice.69), channel_id=1, source_target_pairs={{0,6},{2,0},{4,2},{6,4},{1,7},{3,1},{5,3},{7,5},{8,14},{10,8},{12,... | collective-permute-start | bytes 786440 | tf_op jit(solution)/shard_map/ppermute | solution.py:27
  37.7 13.0 %collective-permute-start.11 = (bf16[512,256]{1,0:T(8,128)(2,1)S(1)}, bf16[512,256]{1,0:T(8,128)(2,1)S(1)}, u32[]{:S(2)}, u32[]{:S(2)}) collective-permute-start(bf16[512,256]{1,0:T(8,128)(2,1)S(1)} %get-tuple-element.34.refs_0_), channel_id=1, source_target_pairs={{0,8},{8,16},{16,24},{24,32},{32,40},{40,48},{48,56},{56,0},{1,9},... | collective-permute-start | bytes 786440 | tf_op jit(solution)/shard_map/ppermute | solution.py:27
  39.7 11.0 %collective-permute-start.14 = (bf16[512,256]{1,0:T(8,128)(2,1)S(1)}, bf16[512,256]{1,0:T(8,128)(2,1)S(1)}, u32[]{:S(2)}, u32[]{:S(2)}) collective-permute-start(bf16[512,256]{1,0:T(8,128)(2,1)S(1)} %get-tuple-element.34.refs_0_), channel_id=1, source_target_pairs={{0,56},{8,0},{16,8},{24,16},{32,24},{40,32},{48,40},{56,48},{1,57}... | collective-permute-start | bytes 786440 | tf_op jit(solution)/shard_map/ppermute | solution.py:27
  43.7 12.6 %collective-permute-start.20 = (bf16[512,256]{1,0:T(8,128)(2,1)S(1)}, bf16[512,256]{1,0:T(8,128)(2,1)S(1)}, u32[]{:S(2)}, u32[]{:S(2)}) collective-permute-start(bf16[512,256]{1,0:T(8,128)(2,1)S(1)} %get-tuple-element.37.refs_9_), channel_id=1, source_target_pairs={{0,8},{8,16},{16,24},{24,32},{32,40},{40,48},{48,56},{56,0},{1,9},... | collective-permute-start | bytes 786440 | tf_op jit(solution)/shard_map/ppermute | solution.py:27
  43.7 12.6 %collective-permute-start.21 = (bf16[512,256]{1,0:T(8,128)(2,1)S(1)}, bf16[512,256]{1,0:T(8,128)(2,1)S(1)}, u32[]{:S(2)}, u32[]{:S(2)}) collective-permute-start(bf16[512,256]{1,0:T(8,128)(2,1)S(1)} %get-tuple-element.37.refs_9_), channel_id=1, source_target_pairs={{0,56},{8,0},{16,8},{24,16},{32,24},{40,32},{48,40},{56,48},{1,57}... | collective-permute-start | bytes 786440 | tf_op jit(solution)/shard_map/ppermute | solution.py:27
  50.7 11.2 %collective-permute-start.12 = (bf16[512,256]{1,0:T(8,128)(2,1)S(1)}, bf16[512,256]{1,0:T(8,128)(2,1)S(1)}, u32[]{:S(2)}, u32[]{:S(2)}) collective-permute-start(bf16[512,256]{1,0:T(8,128)(2,1)S(1)} %collective-permute-done.11.refs_1_), channel_id=1, source_target_pairs={{0,8},{8,16},{16,24},{24,32},{32,40},{40,48},{48,56},{56,0},{1,9},... | collective-permute-start | bytes 786440 | tf_op jit(solution)/shard_map/ppermute | solution.py:27
  50.7 13.4 %collective-permute-start.15 = (bf16[512,256]{1,0:T(8,128)(2,1)S(1)}, bf16[512,256]{1,0:T(8,128)(2,1)S(1)}, u32[]{:S(2)}, u32[]{:S(2)}) collective-permute-start(bf16[512,256]{1,0:T(8,128)(2,1)S(1)} %collective-permute-done.14.refs_2_), channel_id=1, source_target_pairs={{0,56},{8,0},{16,8},{24,16},{32,24},{40,32},{48,40},{56,48},{1,57}... | collective-permute-start | bytes 786440 | tf_op jit(solution)/shard_map/ppermute | solution.py:27
  56.3 11.1 %collective-permute-start.22 = (bf16[512,256]{1,0:T(8,128)(2,1)S(1)}, bf16[512,256]{1,0:T(8,128)(2,1)S(1)}, u32[]{:S(2)}, u32[]{:S(2)}) collective-permute-start(bf16[512,256]{1,0:T(8,128)(2,1)S(1)} %collective-permute-done.20.refs_10_), channel_id=1, source_target_pairs={{0,8},{8,16},{16,24},{24,32},{32,40},{40,48},{48,56},{56,0},{1,9},... | collective-permute-start | bytes 786440 | tf_op jit(solution)/shard_map/ppermute | solution.py:27
  56.4 11.1 %collective-permute-start.23 = (bf16[512,256]{1,0:T(8,128)(2,1)S(1)}, bf16[512,256]{1,0:T(8,128)(2,1)}, u32[]{:S(2)}, u32[]{:S(2)}) collective-permute-start(bf16[512,256]{1,0:T(8,128)(2,1)S(1)} %collective-permute-done.21.refs_11_), channel_id=1, source_target_pairs={{0,56},{8,0},{16,8},{24,16},{32,24},{40,32},{48,40},{56,48},{1,57}... | collective-permute-start | bytes 786440 | tf_op jit(solution)/shard_map/ppermute | solution.py:27
  62.0 21.2 %collective-permute-start.13 = (bf16[528,256]{1,0:T(8,128)(2,1)}, bf16[528,256]{1,0:T(8,128)(2,1)}, u32[]{:S(2)}, u32[]{:S(2)}) collective-permute-start(bf16[528,256]{1,0:T(8,128)(2,1)} %fusion.1.query_ref), channel_id=1, source_target_pairs={{0,128},{64,192},{128,0},{192,64},{1,129},{65,193},{129,1},{193,65... | collective-permute-start | bytes 811016 | tf_op jit(solution)/shard_map/ppermute | solution.py:27
  64.2 10.5 %collective-permute-start.16 = (bf16[512,256]{1,0:T(8,128)(2,1)S(1)}, bf16[512,256]{1,0:T(8,128)(2,1)S(1)}, u32[]{:S(2)}, u32[]{:S(2)}) collective-permute-start(bf16[512,256]{1,0:T(8,128)(2,1)S(1)} %collective-permute-done.12.refs_3_), channel_id=1, source_target_pairs={{0,8},{8,16},{16,24},{24,32},{32,40},{40,48},{48,56},{56,0},{1,9},... | collective-permute-start | bytes 786440 | tf_op jit(solution)/shard_map/ppermute | solution.py:27
  64.2 10.6 %collective-permute-start.17 = (bf16[512,256]{1,0:T(8,128)(2,1)S(1)}, bf16[512,256]{1,0:T(8,128)(2,1)S(1)}, u32[]{:S(2)}, u32[]{:S(2)}) collective-permute-start(bf16[512,256]{1,0:T(8,128)(2,1)S(1)} %collective-permute-done.15.refs_4_), channel_id=1, source_target_pairs={{0,56},{8,0},{16,8},{24,16},{32,24},{40,32},{48,40},{56,48},{1,57}... | collective-permute-start | bytes 786440 | tf_op jit(solution)/shard_map/ppermute | solution.py:27
  67.4 12.3 %collective-permute-start.24 = (bf16[512,256]{1,0:T(8,128)(2,1)S(1)}, bf16[512,256]{1,0:T(8,128)(2,1)S(1)}, u32[]{:S(2)}, u32[]{:S(2)}) collective-permute-start(bf16[512,256]{1,0:T(8,128)(2,1)S(1)} %collective-permute-done.22.refs_12_), channel_id=1, source_target_pairs={{0,8},{8,16},{16,24},{24,32},{32,40},{40,48},{48,56},{56,0},{1,9},... | collective-permute-start | bytes 786440 | tf_op jit(solution)/shard_map/ppermute | solution.py:27
  67.4 12.4 %collective-permute-start.25 = (bf16[512,256]{1,0:T(8,128)(2,1)}, bf16[512,256]{1,0:T(8,128)(2,1)S(1)}, u32[]{:S(2)}, u32[]{:S(2)}) collective-permute-start(bf16[512,256]{1,0:T(8,128)(2,1)} %collective-permute-done.23.refs_13_), channel_id=1, source_target_pairs={{0,56},{8,0},{16,8},{24,16},{32,24},{40,32},{48,40},{56,48},{1,57}... | collective-permute-start | bytes 786440 | tf_op jit(solution)/shard_map/ppermute | solution.py:27
  74.6 9.3 %collective-permute-start.18 = (bf16[256,256]{1,0:T(8,128)(2,1)S(1)}, bf16[256,256]{1,0:T(8,128)(2,1)S(1)}, u32[]{:S(2)}, u32[]{:S(2)}) collective-permute-start(bf16[256,256]{1,0:T(8,128)(2,1)S(1)} %slice.89), channel_id=1, source_target_pairs={{0,8},{8,16},{16,24},{24,32},{32,40},{40,48},{48,56},{56,0},{1,9},... | collective-permute-start | bytes 393224 | tf_op jit(solution)/shard_map/ppermute | solution.py:27
  74.8 9.2 %collective-permute-start.19 = (bf16[256,256]{1,0:T(8,128)(2,1)S(1)}, bf16[256,256]{1,0:T(8,128)(2,1)S(1)}, u32[]{:S(2)}, u32[]{:S(2)}) collective-permute-start(bf16[256,256]{1,0:T(8,128)(2,1)S(1)} %slice.90), channel_id=1, source_target_pairs={{0,56},{8,0},{16,8},{24,16},{32,24},{40,32},{48,40},{56,48},{1,57}... | collective-permute-start | bytes 393224 | tf_op jit(solution)/shard_map/ppermute | solution.py:27
  90.2 22.1 %collective-permute-start.30 = (bf16[2080,128]{1,0:T(8,128)(2,1)S(1)}, bf16[2080,128]{1,0:T(8,128)(2,1)S(1)}, u32[]{:S(2)}, u32[]{:S(2)}) collective-permute-start(bf16[2080,128]{1,0:T(8,128)(2,1)S(1)} %attend.7), channel_id=1, source_target_pairs={{0,64},{64,128},{128,192},{192,0},{1,65},{65,129},{129,193},{193,1... | collective-permute-start | bytes 1597448 | tf_op jit(solution)/shard_map/ppermute | solution.py:27
  94.6 17.8 %collective-permute-start.29 = (bf16[2080,128]{1,0:T(8,128)(2,1)S(1)}, bf16[2080,128]{1,0:T(8,128)(2,1)S(1)}, u32[]{:S(2)}, u32[]{:S(2)}) collective-permute-start(bf16[2080,128]{1,0:T(8,128)(2,1)S(1)} %attend.6), channel_id=1, source_target_pairs={{0,128},{64,192},{128,0},{192,64},{1,129},{65,193},{129,1},{193,65... | collective-permute-start | bytes 1597448 | tf_op jit(solution)/shard_map/ppermute | solution.py:27
  100.8 19.0 %collective-permute-start.28 = (bf16[2080,128]{1,0:T(8,128)(2,1)S(1)}, bf16[2080,128]{1,0:T(8,128)(2,1)S(1)}, u32[]{:S(2)}, u32[]{:S(2)}) collective-permute-start(bf16[2080,128]{1,0:T(8,128)(2,1)S(1)} %attend.5), channel_id=1, source_target_pairs={{0,192},{64,0},{128,64},{192,128},{1,193},{65,1},{129,65},{193,129... | collective-permute-start | bytes 1597448 | tf_op jit(solution)/shard_map/ppermute | solution.py:27
  (13 other events, 72.3 us)
Sparse Core Ops, SparseCore 0:
  37.8 90.1 all-gather.1
